TPU v7x, 128 devices: a whole 4x4x4 slice. The times are simulated.
128 devices in a mesh: segment: 8 (over y, core), band: 16 (over x, z).
Axes of the slice: x: 4, y: 4, z: 4, core: 2. Of those that a mesh axis runs over, the one named last changes fastest.
Arguments:
- tokens: bfloat16 [8, 128, 128, 1536], P('segment', 'band'), may hold values from -6 to 6
- in_gain: float32 [8, 1536], P('segment'), may hold values from 0.1 to 1.9
- w_xbc: bfloat16 [8, 1536, 1664], P('segment'), may hold values from -0.15625 to 0.15625
- w_gate: bfloat16 [8, 1536, 1536], P('segment'), may hold values from -0.15625 to 0.15625
- w_dt: bfloat16 [8, 1536, 24], P('segment'), may hold values from -0.078125 to 0.078125
- dt_bias: float32 [8, 24], P('segment'), may hold values from -1 to 1
- decay_rate: float32 [8, 24], P('segment'), may hold values from 6.1035156e-06 to 0.1, as said below
- conv_w: float32 [8, 9, 1664], P('segment'), may hold values from -2 to 2
- conv_bias: float32 [8, 1664], P('segment'), may hold values from -0.5 to 0.5
- skip: float32 [8, 24], P('segment'), may hold values from 0.5 to 1.5
- out_gain: float32 [8, 1536], P('segment'), may hold values from 0.1 to 1.9
- w_out: bfloat16 [8, 1536, 1536], P('segment'), may hold values from -0.15625 to 0.15625
Outputs:
- handed: bfloat16 [8, 128, 128, 1536], P('segment', 'band')
Inputs may be any that keep to these rules, and one draw needn't show every extreme that they name: `decay_rate`: positive rates per head, differing between heads and sections.
All inputs are finite; a program needn't handle non-finite values.
Results may differ from a plain program's by a relative error of at most 0.015.
Values may be sent and summed in bfloat16 or wider, within the bound.
No kernel may reach another device: no remote copies, remote signals or barrier semaphores. Data moves between devices by JAX's collectives and lax.ppermute only.
A program may use at most 192 MiB of HBM per device.

v0:
```python
import jax
import jax.numpy as jnp
from jax import lax
from jax.sharding import PartitionSpec as P

BLOCK = 128


EPSILON = 1e-05


def with_halo(cells, sides, width):
    for axis, dim in sides:
        count = lax.axis_size(axis)
        ends = count - 1
        head = lax.slice_in_dim(cells, 0, width, axis=dim)
        tail = lax.slice_in_dim(cells, cells.shape[dim] - width, cells.shape[dim], axis=dim)
        cells = jnp.concatenate(
            [
                lax.ppermute(tail, axis, [(i, (i + 1) % count) for i in range(ends)]),
                cells,
                lax.ppermute(head, axis, [((i + 1) % count, i) for i in range(ends)]),
            ],
            axis=dim,
        )
    return cells


def shifted(shard, axis, by):
    peers = lax.axis_size(axis)
    pairs = [(i, i + by) for i in range(peers) if 0 <= i + by < peers]
    return lax.ppermute(shard, axis, pairs)


def passed_along(shard, axis, by):
    peers = lax.axis_size(axis)
    return lax.ppermute(shard, axis, [(i, (i + by) % peers) for i in range(peers)])


def block_step(carry, pieces):
    state, offset = carry
    x_block, b_block, c_block, log_block, dt_block = pieces
    cumul = jnp.cumsum(log_block, axis=0)
    cumul_t = cumul.T
    positions = jnp.arange(log_block.shape[0])
    causal = positions[:, None] >= positions[None, :]
    spread = cumul_t[:, :, None] - cumul_t[:, None, :]
    decay = jnp.exp(jnp.where(causal[None], spread, -jnp.inf))
    intersection = jnp.dot(c_block, b_block.T, preferred_element_type=jnp.float32)
    mixing = (intersection[None] * decay * dt_block.T[:, None, :]).astype(jnp.bfloat16)
    inner_part = jnp.einsum("hij,jhp->ihp", mixing, x_block, preferred_element_type=jnp.float32)
    carried = jnp.exp(cumul)[:, :, None] * jnp.einsum(
        "in,hpn->ihp", c_block.astype(jnp.float32), state, precision=lax.Precision.HIGHEST
    )
    tail = jnp.exp(cumul[-1][None, :] - cumul) * dt_block
    scaled = tail[:, :, None] * x_block.astype(jnp.float32)
    contrib = jnp.einsum(
        "jhp,jn->hpn", scaled, b_block.astype(jnp.float32), precision=lax.Precision.HIGHEST
    )
    new_state = jnp.exp(cumul[-1])[:, None, None] * state + contrib
    running = offset + cumul
    return ((new_state, running[-1]), (inner_part + carried, running))


def shards(
    tokens,
    in_gain,
    w_xbc,
    w_gate,
    w_dt,
    dt_bias,
    decay_rate,
    conv_w,
    conv_bias,
    skip,
    out_gain,
    w_out,
):
    upcast = tokens[0].astype(jnp.float32)
    row_count, grid_size, width_d = upcast.shape
    length = row_count * grid_size
    normed = (
        upcast * lax.rsqrt(jnp.mean(upcast * upcast, -1, keepdims=True) + EPSILON) * in_gain[0]
    ).astype(jnp.bfloat16)
    flat = normed.reshape(length, width_d)
    conv_input = (
        jnp.dot(flat, w_xbc[0], preferred_element_type=jnp.float32)
        .astype(jnp.bfloat16)
        .reshape(row_count, grid_size, -1)
    )
    widened = with_halo(conv_input, (("band", 0),), 1)
    gate = jnp.dot(flat, w_gate[0], preferred_element_type=jnp.float32).astype(jnp.bfloat16)
    step_size = jax.nn.softplus(
        jnp.dot(flat, w_dt[0], preferred_element_type=jnp.float32) + dt_bias[0]
    )
    padded = jnp.pad(widened, ((0, 0), (1, 1), (0, 0)))
    summed = jnp.zeros((row_count, grid_size, padded.shape[2]), jnp.float32)
    taps = conv_w[0]
    for tap_row in range(3):
        for tap_col in range(3):
            window = padded[tap_row : tap_row + row_count, tap_col : tap_col + grid_size].astype(
                jnp.float32
            )
            summed = summed + window * taps[tap_row * 3 + tap_col]
    conv_output = jax.nn.silu(summed + conv_bias[0]).astype(jnp.bfloat16).reshape(length, -1)
    inner = w_gate.shape[2]
    heads = dt_bias.shape[1]
    headdim = inner // heads
    state_n = (conv_output.shape[1] - inner) // 2
    blocks = length // BLOCK
    x_all = conv_output[:, :inner].reshape(blocks, BLOCK, heads, headdim)
    b_all = conv_output[:, inner : inner + state_n].reshape(blocks, BLOCK, state_n)
    c_flat = conv_output[:, inner + state_n :]
    c_all = c_flat.reshape(blocks, BLOCK, state_n)
    log_all = (-step_size * decay_rate[0]).reshape(blocks, BLOCK, heads)
    dt_all = step_size.reshape(blocks, BLOCK, heads)
    start = (jnp.zeros((heads, headdim, state_n), jnp.float32), jnp.zeros((heads,), jnp.float32))
    (local_state, total_log), (outputs, cumuls) = lax.scan(
        block_step, start, (x_all, b_all, c_all, log_all, dt_all)
    )
    decay_dev = jnp.exp(total_log)

    def relay_step(number, arriving):
        return shifted(decay_dev[:, None, None] * arriving + local_state, "band", 1)

    incoming = lax.fori_loop(0, lax.axis_size("band") - 1, relay_step, jnp.zeros_like(local_state))
    entering = jnp.exp(cumuls.reshape(length, heads))[:, :, None] * jnp.einsum(
        "in,hpn->ihp", c_flat.astype(jnp.float32), incoming, precision=lax.Precision.HIGHEST
    )
    x_flat = x_all.reshape(length, heads, headdim).astype(jnp.float32)
    scanned = outputs.reshape(length, heads, headdim) + entering + skip[0][None, :, None] * x_flat
    gated = scanned.reshape(length, inner) * jax.nn.silu(gate.astype(jnp.float32))
    hidden = (
        gated * lax.rsqrt(jnp.mean(gated * gated, -1, keepdims=True) + EPSILON) * out_gain[0]
    ).astype(jnp.bfloat16)
    result = upcast.reshape(length, width_d) + jnp.dot(
        hidden, w_out[0], preferred_element_type=jnp.float32
    )
    section_out = result.astype(jnp.bfloat16).reshape(row_count, grid_size, width_d)
    columns_here = lax.all_to_all(section_out, "band", split_axis=1, concat_axis=0, tiled=True)
    regrouped = passed_along(columns_here, "segment", 1)
    handed = jnp.swapaxes(regrouped, 0, 1)
    return handed[None]


def solution(mesh):
    in_specs = (
        P("segment", "band", None, None),
        P("segment", None),
        P("segment", None, None),
        P("segment", None, None),
        P("segment", None, None),
        P("segment", None),
        P("segment", None),
        P("segment", None, None),
        P("segment", None),
        P("segment", None),
        P("segment", None),
        P("segment", None, None),
    )
    out_specs = P("segment", "band", None, None)
    return jax.shard_map(shards, mesh=mesh, in_specs=in_specs, out_specs=out_specs, check_vma=False)
```

profile of v0, /device:TPU:0, one launch (start us, length us, event | category | flops | bytes accessed | tf_op | source)
XLA Modules:
  0.0 715.5 jit_solution(10909140300842825965)
XLA Ops:
  0.0 2.6 multiply_reduce_fusion.1
  3.3 2.8 multiply_convert_fusion.4
  6.7 6.0 fusion.57
  14.7 3.9 collective-permute-start.1
  20.2 2.9 negate_multiply_fusion
  23.7 4.3 collective-permute-done.1
  28.0 4.0 collective-permute-done.2
  32.0 4.4 fusion.51
  36.4 9.1 %multiply_convert_fusion.2 = bf16[8,128,1664]{2,1,0:T(8,128)(2,1)S(1)} fusion(bf16[8,128,1664]{2,1,0:T(8,128)(2,1)S(1)} %bitcast.151, bf16[10,130,1664]{2,1,0:T(8,128)(2,1)S(1)} %fusion.51, bf16[1,128,1664]{2,1,0:T(8,128)(2,1)S(1)} %collective-permute-done.2, bf16[1,128,1664]{2,1,0:T(8,128)(2,1)S(1)} %collective-permute-done.1, f32[1664]{0:T(1024)S(1)} %reduce.11, ...), kind=kLoop, calls=%fused_computation.51 | loop fusion | flops 57933824 | bytes 28181504 | tf_op jit(solution)/shard_map/convert_element_type | solution.py:105
  45.5 2.2 slice.130
  48.4 4.7 copy.49
  53.0 2.7 copy.58
  55.8 2.5 copy.36
  59.8 236.0 %while.28 = (s32[]{:T(128)}, f32[24,64,64]{2,1,0:T(8,128)S(1)}, f32[24]{0:T(128)S(1)}, f32[8,128,24,64]{1,0,3,2:T(8,128)}, f32[8,128,24]{2,1,0:T(8,128)}, /*inde...) while((s32[]{:T(128)}, f32[24,64,64]{2,1,0:T(8,128)S(1)}, ...), condition=%wide.region_3.4_spmd.clone, body=%wide.region_1.3_spmd.clone.sunk | while | flops 357980192 | bytes 6493268 | solution.py:118
  66.6 20.8 %dynamic_update_slice.14 = f32[8,128,24,64]{1,0,3,2:T(8,128)} dynamic-update-slice(f32[8,128,24,64]{1,0,3,2:T(8,128)} %get-tuple-element.305, f32[1,128,24,64]{1,0,3,2:T(1,128)S(1)} %bitcast.146, s32[]{:T(128)} %get-tuple-element.302, s32[]{:T(128)} %constant.34.clone.1..sunk, s32[]{:T(128)} %constant.34.clone.1..sunk, s32[]{:T(128)} %constant.34.clone.1..sunk) | dynamic-update-slice | bytes 1572868 | tf_op jit(solution)/shard_map/while/body/jit(dynamic_update_index_in_dim)/dynamic_update_slice | solution.py:118
  96.1 20.8 %dynamic_update_slice.14 = f32[8,128,24,64]{1,0,3,2:T(8,128)} dynamic-update-slice(f32[8,128,24,64]{1,0,3,2:T(8,128)} %get-tuple-element.305, f32[1,128,24,64]{1,0,3,2:T(1,128)S(1)} %bitcast.146, s32[]{:T(128)} %get-tuple-element.302, s32[]{:T(128)} %constant.34.clone.1..sunk, s32[]{:T(128)} %constant.34.clone.1..sunk, s32[]{:T(128)} %constant.34.clone.1..sunk) | dynamic-update-slice | bytes 1572868 | tf_op jit(solution)/shard_map/while/body/jit(dynamic_update_index_in_dim)/dynamic_update_slice | solution.py:118
  125.6 20.8 %dynamic_update_slice.14 = f32[8,128,24,64]{1,0,3,2:T(8,128)} dynamic-update-slice(f32[8,128,24,64]{1,0,3,2:T(8,128)} %get-tuple-element.305, f32[1,128,24,64]{1,0,3,2:T(1,128)S(1)} %bitcast.146, s32[]{:T(128)} %get-tuple-element.302, s32[]{:T(128)} %constant.34.clone.1..sunk, s32[]{:T(128)} %constant.34.clone.1..sunk, s32[]{:T(128)} %constant.34.clone.1..sunk) | dynamic-update-slice | bytes 1572868 | tf_op jit(solution)/shard_map/while/body/jit(dynamic_update_index_in_dim)/dynamic_update_slice | solution.py:118
  155.1 20.8 %dynamic_update_slice.14 = f32[8,128,24,64]{1,0,3,2:T(8,128)} dynamic-update-slice(f32[8,128,24,64]{1,0,3,2:T(8,128)} %get-tuple-element.305, f32[1,128,24,64]{1,0,3,2:T(1,128)S(1)} %bitcast.146, s32[]{:T(128)} %get-tuple-element.302, s32[]{:T(128)} %constant.34.clone.1..sunk, s32[]{:T(128)} %constant.34.clone.1..sunk, s32[]{:T(128)} %constant.34.clone.1..sunk) | dynamic-update-slice | bytes 1572868 | tf_op jit(solution)/shard_map/while/body/jit(dynamic_update_index_in_dim)/dynamic_update_slice | solution.py:118
  184.6 20.8 %dynamic_update_slice.14 = f32[8,128,24,64]{1,0,3,2:T(8,128)} dynamic-update-slice(f32[8,128,24,64]{1,0,3,2:T(8,128)} %get-tuple-element.305, f32[1,128,24,64]{1,0,3,2:T(1,128)S(1)} %bitcast.146, s32[]{:T(128)} %get-tuple-element.302, s32[]{:T(128)} %constant.34.clone.1..sunk, s32[]{:T(128)} %constant.34.clone.1..sunk, s32[]{:T(128)} %constant.34.clone.1..sunk) | dynamic-update-slice | bytes 1572868 | tf_op jit(solution)/shard_map/while/body/jit(dynamic_update_index_in_dim)/dynamic_update_slice | solution.py:118
  205.4 1.9 convolution_add_fusion.3
  214.1 20.8 %dynamic_update_slice.14 = f32[8,128,24,64]{1,0,3,2:T(8,128)} dynamic-update-slice(f32[8,128,24,64]{1,0,3,2:T(8,128)} %get-tuple-element.305, f32[1,128,24,64]{1,0,3,2:T(1,128)S(1)} %bitcast.146, s32[]{:T(128)} %get-tuple-element.302, s32[]{:T(128)} %constant.34.clone.1..sunk, s32[]{:T(128)} %constant.34.clone.1..sunk, s32[]{:T(128)} %constant.34.clone.1..sunk) | dynamic-update-slice | bytes 1572868 | tf_op jit(solution)/shard_map/while/body/jit(dynamic_update_index_in_dim)/dynamic_update_slice | solution.py:118
  234.9 1.9 convolution_add_fusion.3
  243.6 20.8 %dynamic_update_slice.14 = f32[8,128,24,64]{1,0,3,2:T(8,128)} dynamic-update-slice(f32[8,128,24,64]{1,0,3,2:T(8,128)} %get-tuple-element.305, f32[1,128,24,64]{1,0,3,2:T(1,128)S(1)} %bitcast.146, s32[]{:T(128)} %get-tuple-element.302, s32[]{:T(128)} %constant.34.clone.1..sunk, s32[]{:T(128)} %constant.34.clone.1..sunk, s32[]{:T(128)} %constant.34.clone.1..sunk) | dynamic-update-slice | bytes 1572868 | tf_op jit(solution)/shard_map/while/body/jit(dynamic_update_index_in_dim)/dynamic_update_slice | solution.py:118
  264.4 1.9 convolution_add_fusion.3
  273.1 20.8 %dynamic_update_slice.14 = f32[8,128,24,64]{1,0,3,2:T(8,128)} dynamic-update-slice(f32[8,128,24,64]{1,0,3,2:T(8,128)} %get-tuple-element.305, f32[1,128,24,64]{1,0,3,2:T(1,128)S(1)} %bitcast.146, s32[]{:T(128)} %get-tuple-element.302, s32[]{:T(128)} %constant.34.clone.1..sunk, s32[]{:T(128)} %constant.34.clone.1..sunk, s32[]{:T(128)} %constant.34.clone.1..sunk) | dynamic-update-slice | bytes 1572868 | tf_op jit(solution)/shard_map/while/body/jit(dynamic_update_index_in_dim)/dynamic_update_slice | solution.py:118
  296.0 288.3 %while.27 = (s32[]{:T(128)}, f32[24,64,64]{2,1,0:T(8,128)S(1)}, f32[24]{0:T(128)S(1)}, f32[24,64,64]{2,1,0:T(8,128)S(1)}, s32[]{:T(128)}) while((s32[]{:T(128)}, f32[24,64,64]{2,1,0:T(8,128)S(1)}, f32[24]{0:T(128)S(1)}, f32[24,64,64]{2,1,0:T(8,128)S(1)}, s32[]{:T(128)}) %tuple.61), condition=%wide.region_5.6_spmd, body=%wide.region_4.5_spmd.sunk | while | flops 196610 | bytes 2752709 | solution.py:126
  296.1 3.7 collective-permute-start
  299.8 15.5 %collective-permute-done = f32[24,64,64]{2,1,0:T(8,128)S(1)} collective-permute-done((f32[24,64,64]{2,1,0:T(8,128)S(1)}, f32[24,64,64]{2,1,0:T(8,128)S(1)}, u32[]{:S(2)}, u32[]{:S(2)}) %collective-permute-start) | collective-permute-done | bytes 393248 | tf_op jit(solution)/shard_map/while/body/eval_jaxpr/ppermute | solution.py:32
  315.5 4.4 collective-permute-start
  320.0 14.6 %collective-permute-done = f32[24,64,64]{2,1,0:T(8,128)S(1)} collective-permute-done((f32[24,64,64]{2,1,0:T(8,128)S(1)}, f32[24,64,64]{2,1,0:T(8,128)S(1)}, u32[]{:S(2)}, u32[]{:S(2)}) %collective-permute-start) | collective-permute-done | bytes 393248 | tf_op jit(solution)/shard_map/while/body/eval_jaxpr/ppermute | solution.py:32
  334.7 4.4 collective-permute-start
  339.2 13.7 %collective-permute-done = f32[24,64,64]{2,1,0:T(8,128)S(1)} collective-permute-done((f32[24,64,64]{2,1,0:T(8,128)S(1)}, f32[24,64,64]{2,1,0:T(8,128)S(1)}, u32[]{:S(2)}, u32[]{:S(2)}) %collective-permute-start) | collective-permute-done | bytes 393248 | tf_op jit(solution)/shard_map/while/body/eval_jaxpr/ppermute | solution.py:32
  353.0 4.4 collective-permute-start
  357.5 12.8 %collective-permute-done = f32[24,64,64]{2,1,0:T(8,128)S(1)} collective-permute-done((f32[24,64,64]{2,1,0:T(8,128)S(1)}, f32[24,64,64]{2,1,0:T(8,128)S(1)}, u32[]{:S(2)}, u32[]{:S(2)}) %collective-permute-start) | collective-permute-done | bytes 393248 | tf_op jit(solution)/shard_map/while/body/eval_jaxpr/ppermute | solution.py:32
  370.4 5.0 collective-permute-start
  375.4 12.3 %collective-permute-done = f32[24,64,64]{2,1,0:T(8,128)S(1)} collective-permute-done((f32[24,64,64]{2,1,0:T(8,128)S(1)}, f32[24,64,64]{2,1,0:T(8,128)S(1)}, u32[]{:S(2)}, u32[]{:S(2)}) %collective-permute-start) | collective-permute-done | bytes 393248 | tf_op jit(solution)/shard_map/while/body/eval_jaxpr/ppermute | solution.py:32
  387.8 6.5 collective-permute-start
  394.4 11.4 %collective-permute-done = f32[24,64,64]{2,1,0:T(8,128)S(1)} collective-permute-done((f32[24,64,64]{2,1,0:T(8,128)S(1)}, f32[24,64,64]{2,1,0:T(8,128)S(1)}, u32[]{:S(2)}, u32[]{:S(2)}) %collective-permute-start) | collective-permute-done | bytes 393248 | tf_op jit(solution)/shard_map/while/body/eval_jaxpr/ppermute | solution.py:32
  405.9 6.5 collective-permute-start
  412.5 11.0 %collective-permute-done = f32[24,64,64]{2,1,0:T(8,128)S(1)} collective-permute-done((f32[24,64,64]{2,1,0:T(8,128)S(1)}, f32[24,64,64]{2,1,0:T(8,128)S(1)}, u32[]{:S(2)}, u32[]{:S(2)}) %collective-permute-start) | collective-permute-done | bytes 393248 | tf_op jit(solution)/shard_map/while/body/eval_jaxpr/ppermute | solution.py:32
  423.6 6.5 collective-permute-start
  430.2 11.1 %collective-permute-done = f32[24,64,64]{2,1,0:T(8,128)S(1)} collective-permute-done((f32[24,64,64]{2,1,0:T(8,128)S(1)}, f32[24,64,64]{2,1,0:T(8,128)S(1)}, u32[]{:S(2)}, u32[]{:S(2)}) %collective-permute-start) | collective-permute-done | bytes 393248 | tf_op jit(solution)/shard_map/while/body/eval_jaxpr/ppermute | solution.py:32
  441.5 6.5 collective-permute-start
  448.0 11.7 %collective-permute-done = f32[24,64,64]{2,1,0:T(8,128)S(1)} collective-permute-done((f32[24,64,64]{2,1,0:T(8,128)S(1)}, f32[24,64,64]{2,1,0:T(8,128)S(1)}, u32[]{:S(2)}, u32[]{:S(2)}) %collective-permute-start) | collective-permute-done | bytes 393248 | tf_op jit(solution)/shard_map/while/body/eval_jaxpr/ppermute | solution.py:32
  459.9 6.5 collective-permute-start
  466.4 12.5 %collective-permute-done = f32[24,64,64]{2,1,0:T(8,128)S(1)} collective-permute-done((f32[24,64,64]{2,1,0:T(8,128)S(1)}, f32[24,64,64]{2,1,0:T(8,128)S(1)}, u32[]{:S(2)}, u32[]{:S(2)}) %collective-permute-start) | collective-permute-done | bytes 393248 | tf_op jit(solution)/shard_map/while/body/eval_jaxpr/ppermute | solution.py:32
  479.1 6.2 collective-permute-start
  485.3 13.2 %collective-permute-done = f32[24,64,64]{2,1,0:T(8,128)S(1)} collective-permute-done((f32[24,64,64]{2,1,0:T(8,128)S(1)}, f32[24,64,64]{2,1,0:T(8,128)S(1)}, u32[]{:S(2)}, u32[]{:S(2)}) %collective-permute-start) | collective-permute-done | bytes 393248 | tf_op jit(solution)/shard_map/while/body/eval_jaxpr/ppermute | solution.py:32
  498.6 7.4 %collective-permute-start = (f32[24,64,64]{2,1,0:T(8,128)S(1)}, f32[24,64,64]{2,1,0:T(8,128)S(1)}, u32[]{:S(2)}, u32[]{:S(2)}) collective-permute-start(f32[24,64,64]{2,1,0:T(8,128)S(1)} %multiply_add_fusion.2), channel_id=1, source_target_pairs={{0,1},{1,2},{2,3},{3,4},{4,5},{5,6},{6,7},{7,8},{8,9},{9,10},{10,1... | collective-permute-start | bytes 1179656 | tf_op jit(solution)/shard_map/while/body/eval_jaxpr/ppermute | solution.py:32
  506.1 14.3 %collective-permute-done = f32[24,64,64]{2,1,0:T(8,128)S(1)} collective-permute-done((f32[24,64,64]{2,1,0:T(8,128)S(1)}, f32[24,64,64]{2,1,0:T(8,128)S(1)}, u32[]{:S(2)}, u32[]{:S(2)}) %collective-permute-start) | collective-permute-done | bytes 393248 | tf_op jit(solution)/shard_map/while/body/eval_jaxpr/ppermute | solution.py:32
  520.5 7.4 %collective-permute-start = (f32[24,64,64]{2,1,0:T(8,128)S(1)}, f32[24,64,64]{2,1,0:T(8,128)S(1)}, u32[]{:S(2)}, u32[]{:S(2)}) collective-permute-start(f32[24,64,64]{2,1,0:T(8,128)S(1)} %multiply_add_fusion.2), channel_id=1, source_target_pairs={{0,1},{1,2},{2,3},{3,4},{4,5},{5,6},{6,7},{7,8},{8,9},{9,10},{10,1... | collective-permute-start | bytes 1179656 | tf_op jit(solution)/shard_map/while/body/eval_jaxpr/ppermute | solution.py:32
  527.9 15.3 %collective-permute-done = f32[24,64,64]{2,1,0:T(8,128)S(1)} collective-permute-done((f32[24,64,64]{2,1,0:T(8,128)S(1)}, f32[24,64,64]{2,1,0:T(8,128)S(1)}, u32[]{:S(2)}, u32[]{:S(2)}) %collective-permute-start) | collective-permute-done | bytes 393248 | tf_op jit(solution)/shard_map/while/body/eval_jaxpr/ppermute | solution.py:32
  543.4 7.4 %collective-permute-start = (f32[24,64,64]{2,1,0:T(8,128)S(1)}, f32[24,64,64]{2,1,0:T(8,128)S(1)}, u32[]{:S(2)}, u32[]{:S(2)}) collective-permute-start(f32[24,64,64]{2,1,0:T(8,128)S(1)} %multiply_add_fusion.2), channel_id=1, source_target_pairs={{0,1},{1,2},{2,3},{3,4},{4,5},{5,6},{6,7},{7,8},{8,9},{9,10},{10,1... | collective-permute-start | bytes 1179656 | tf_op jit(solution)/shard_map/while/body/eval_jaxpr/ppermute | solution.py:32
  550.8 16.4 %collective-permute-done = f32[24,64,64]{2,1,0:T(8,128)S(1)} collective-permute-done((f32[24,64,64]{2,1,0:T(8,128)S(1)}, f32[24,64,64]{2,1,0:T(8,128)S(1)}, u32[]{:S(2)}, u32[]{:S(2)}) %collective-permute-start) | collective-permute-done | bytes 393248 | tf_op jit(solution)/shard_map/while/body/eval_jaxpr/ppermute | solution.py:32
  567.4 7.5 %collective-permute-start = (f32[24,64,64]{2,1,0:T(8,128)S(1)}, f32[24,64,64]{2,1,0:T(8,128)S(1)}, u32[]{:S(2)}, u32[]{:S(2)}) collective-permute-start(f32[24,64,64]{2,1,0:T(8,128)S(1)} %multiply_add_fusion.2), channel_id=1, source_target_pairs={{0,1},{1,2},{2,3},{3,4},{4,5},{5,6},{6,7},{7,8},{8,9},{9,10},{10,1... | collective-permute-start | bytes 1179656 | tf_op jit(solution)/shard_map/while/body/eval_jaxpr/ppermute | solution.py:32
  574.9 9.4 %collective-permute-done = f32[24,64,64]{2,1,0:T(8,128)S(1)} collective-permute-done((f32[24,64,64]{2,1,0:T(8,128)S(1)}, f32[24,64,64]{2,1,0:T(8,128)S(1)}, u32[]{:S(2)}, u32[]{:S(2)}) %collective-permute-start) | collective-permute-done | bytes 393248 | tf_op jit(solution)/shard_map/while/body/eval_jaxpr/ppermute | solution.py:32
  584.3 5.6 fusion.64
  589.9 7.1 reshape.210
  598.3 10.7 %fusion.39 = f32[1024,24,64]{0,2,1:T(8,128)} fusion(bf16[1024,24,64]{0,2,1:T(8,128)(2,1)} %bitcast.143, f32[1024,24,64]{0,2,1:T(8,128)} %reshape.210, f32[1024,24,64]{0,2,1:T(8,128)} %fusion.64, f32[24]{0:T(128)S(1)} %bitcast.167, f32[1024,24]{0,1:T(8,128)S(1)} %copy.40), kind=kLoop, calls=%fused_computation.57 | loop fusion | flops 7864320 | bytes 22118496 | tf_op jit(solution)/shard_map/add | solution.py:131
  608.9 6.7 copy.41
  615.6 10.5 %multiply_reduce_fusion = (f32[1024]{0:T(1024)S(1)}, f32[1024,1536]{1,0:T(8,128)S(1)}) fusion(f32[1024,1536]{1,0:T(8,128)} %copy.41, bf16[1024,1536]{1,0:T(8,128)(2,1)} %bitcast.149, bf16[1,1536,1536]{2,1,0:T(8,128)(2,1)} %param.19), kind=kOutput, calls=%fused_computation.61 | convolution fusion | flops 4845992960 | bytes 20451328 | tf_op jit(solution)/shard_map/dot_general | solution.py:92
  626.2 5.5 fusion.40
  633.4 42.1 %all_to_all.18 = bf16[8,128,1536]{2,0,1:T(8,128)(2,1)S(1)} all-to-all(bf16[8,128,1536]{2,0,1:T(8,128)(2,1)S(1)} %copy.42), channel_id=1, replica_groups=mesh['segment'=8,'band'=16] {'band'}, dimensions={1} | all-to-all | bytes 6291456 | tf_op jit(solution)/shard_map/all_to_all | solution.py:140
  675.9 37.9 %collective-permute-done.3 = bf16[128,8,1536]{2,0,1:T(8,128)(2,1)S(1)} collective-permute-done((bf16[128,8,1536]{2,0,1:T(8,128)(2,1)S(1)}, bf16[128,8,1536]{2,0,1:T(8,128)(2,1)S(1)}, u32[]{:S(2)}, u32[]{:S(2)}) %collective-permute-start.3) | collective-permute-done | bytes 3145760 | tf_op jit(solution)/shard_map/ppermute | solution.py:37
  (214 shorter events, 78.4 us)
Async XLA Ops:
  0.0 20.2 %copy-start = (bf16[1,1536,24]{1,2,0:T(8,128)(2,1)S(1)}, bf16[1,1536,24]{1,2,0:T(8,128)(2,1)}, u32[]{:S(2)}) copy-start(bf16[1,1536,24]{1,2,0:T(8,128)(2,1)} %param.20) | copy-start | bytes 221188
  3.3 3.4 copy-start.13
  6.2 6.6 copy-start.2
  6.7 13.4 %copy-start.8 = (f32[1,1664]{1,0:T(1,128)S(1)}, f32[1,1664]{1,0:T(1,128)}, u32[]{:S(2)}) copy-start(f32[1,1664]{1,0:T(1,128)} %param.24) | copy-start | bytes 19972
  6.7 13.5 %copy-start.10 = (f32[1,24]{1,0:T(1,128)S(1)}, f32[1,24]{1,0:T(1,128)}, u32[]{:S(2)}) copy-start(f32[1,24]{1,0:T(1,128)} %param.22) | copy-start | bytes 292
  6.7 13.5 %copy-start.11 = (f32[1,24]{1,0:T(1,128)S(1)}, f32[1,24]{1,0:T(1,128)}, u32[]{:S(2)}) copy-start(f32[1,24]{1,0:T(1,128)} %param.21) | copy-start | bytes 292
  12.8 1.9 copy-start.3
  12.8 10.7 %copy-start.9 = (f32[1,1536]{1,0:T(1,128)S(1)}, f32[1,1536]{1,0:T(1,128)}, u32[]{:S(2)}) copy-start(f32[1,1536]{1,0:T(1,128)} %param.26) | copy-start | bytes 18436
  12.8 10.7 %copy-start.7 = (f32[1,9,1664]{2,0,1:T(1,128)S(1)}, f32[1,9,1664]{2,0,1:T(1,128)}, u32[]{:S(2)}) copy-start(f32[1,9,1664]{2,0,1:T(1,128)} %param.23) | copy-start | bytes 179716
  14.7 13.3 %collective-permute-start.1 = (bf16[1,128,1664]{2,1,0:T(8,128)(2,1)}, bf16[1,128,1664]{2,1,0:T(8,128)(2,1)S(1)}, u32[]{:S(2)}, u32[]{:S(2)}) collective-permute-start(bf16[1,128,1664]{2,1,0:T(8,128)(2,1)} %get-tuple-element.185), channel_id=1, source_target_pairs={{0,1},{1,2},{2,3},{3,4},{4,5},{5,6},{6,7},{7,8},{8,9},{9,10},{10,1... | collective-permute-start | bytes 1277960 | tf_op jit(solution)/shard_map/ppermute | solution.py:20
  18.6 13.3 %collective-permute-start.2 = (bf16[1,128,1664]{2,1,0:T(8,128)(2,1)S(1)}, bf16[1,128,1664]{2,1,0:T(8,128)(2,1)S(1)}, u32[]{:S(2)}, u32[]{:S(2)}) collective-permute-start(bf16[1,128,1664]{2,1,0:T(8,128)(2,1)S(1)} %get-tuple-element.186), channel_id=1, source_target_pairs={{1,0},{2,1},{3,2},{4,3},{5,4},{6,5},{7,6},{8,7},{9,8},{10,9},{11,1... | collective-permute-start | bytes 1277960 | tf_op jit(solution)/shard_map/ppermute | solution.py:22
  23.5 12.8 %copy-start.4 = (bf16[1024,1664]{1,0:T(8,128)(2,1)S(1)}, bf16[1024,1664]{1,0:T(8,128)(2,1)}, u32[]{:S(2)}) copy-start(bf16[1024,1664]{1,0:T(8,128)(2,1)} %copy-done.3) | copy-start | bytes 10223620
  45.5 2.8 copy-start.5
  61.2 28.1 %copy-start.14 = (f32[24]{0:T(128)S(1)}, f32[24]{0:T(128)}, u32[]{:S(2)}) copy-start(f32[24]{0:T(128)} %get-tuple-element.317) | copy-start | bytes 292 | tf_op jit(solution)/shard_map/while
  90.7 28.1 %copy-start.14 = (f32[24]{0:T(128)S(1)}, f32[24]{0:T(128)}, u32[]{:S(2)}) copy-start(f32[24]{0:T(128)} %get-tuple-element.317) | copy-start | bytes 292 | tf_op jit(solution)/shard_map/while
  120.2 28.1 %copy-start.14 = (f32[24]{0:T(128)S(1)}, f32[24]{0:T(128)}, u32[]{:S(2)}) copy-start(f32[24]{0:T(128)} %get-tuple-element.317) | copy-start | bytes 292 | tf_op jit(solution)/shard_map/while
  149.7 28.1 %copy-start.14 = (f32[24]{0:T(128)S(1)}, f32[24]{0:T(128)}, u32[]{:S(2)}) copy-start(f32[24]{0:T(128)} %get-tuple-element.317) | copy-start | bytes 292 | tf_op jit(solution)/shard_map/while
  179.2 28.1 %copy-start.14 = (f32[24]{0:T(128)S(1)}, f32[24]{0:T(128)}, u32[]{:S(2)}) copy-start(f32[24]{0:T(128)} %get-tuple-element.317) | copy-start | bytes 292 | tf_op jit(solution)/shard_map/while
  208.7 28.1 %copy-start.14 = (f32[24]{0:T(128)S(1)}, f32[24]{0:T(128)}, u32[]{:S(2)}) copy-start(f32[24]{0:T(128)} %get-tuple-element.317) | copy-start | bytes 292 | tf_op jit(solution)/shard_map/while
  238.3 28.1 %copy-start.14 = (f32[24]{0:T(128)S(1)}, f32[24]{0:T(128)}, u32[]{:S(2)}) copy-start(f32[24]{0:T(128)} %get-tuple-element.317) | copy-start | bytes 292 | tf_op jit(solution)/shard_map/while
  267.8 28.1 %copy-start.14 = (f32[24]{0:T(128)S(1)}, f32[24]{0:T(128)}, u32[]{:S(2)}) copy-start(f32[24]{0:T(128)} %get-tuple-element.317) | copy-start | bytes 292 | tf_op jit(solution)/shard_map/while
  296.1 19.2 %collective-permute-start = (f32[24,64,64]{2,1,0:T(8,128)S(1)}, f32[24,64,64]{2,1,0:T(8,128)S(1)}, u32[]{:S(2)}, u32[]{:S(2)}) collective-permute-start(f32[24,64,64]{2,1,0:T(8,128)S(1)} %multiply_add_fusion.2), channel_id=1, source_target_pairs={{0,1},{1,2},{2,3},{3,4},{4,5},{5,6},{6,7},{7,8},{8,9},{9,10},{10,1... | collective-permute-start | bytes 1179656 | tf_op jit(solution)/shard_map/while/body/eval_jaxpr/ppermute | solution.py:32
  315.5 19.1 %collective-permute-start = (f32[24,64,64]{2,1,0:T(8,128)S(1)}, f32[24,64,64]{2,1,0:T(8,128)S(1)}, u32[]{:S(2)}, u32[]{:S(2)}) collective-permute-start(f32[24,64,64]{2,1,0:T(8,128)S(1)} %multiply_add_fusion.2), channel_id=1, source_target_pairs={{0,1},{1,2},{2,3},{3,4},{4,5},{5,6},{6,7},{7,8},{8,9},{9,10},{10,1... | collective-permute-start | bytes 1179656 | tf_op jit(solution)/shard_map/while/body/eval_jaxpr/ppermute | solution.py:32
  334.7 18.1 %collective-permute-start = (f32[24,64,64]{2,1,0:T(8,128)S(1)}, f32[24,64,64]{2,1,0:T(8,128)S(1)}, u32[]{:S(2)}, u32[]{:S(2)}) collective-permute-start(f32[24,64,64]{2,1,0:T(8,128)S(1)} %multiply_add_fusion.2), channel_id=1, source_target_pairs={{0,1},{1,2},{2,3},{3,4},{4,5},{5,6},{6,7},{7,8},{8,9},{9,10},{10,1... | collective-permute-start | bytes 1179656 | tf_op jit(solution)/shard_map/while/body/eval_jaxpr/ppermute | solution.py:32
  353.0 17.2 %collective-permute-start = (f32[24,64,64]{2,1,0:T(8,128)S(1)}, f32[24,64,64]{2,1,0:T(8,128)S(1)}, u32[]{:S(2)}, u32[]{:S(2)}) collective-permute-start(f32[24,64,64]{2,1,0:T(8,128)S(1)} %multiply_add_fusion.2), channel_id=1, source_target_pairs={{0,1},{1,2},{2,3},{3,4},{4,5},{5,6},{6,7},{7,8},{8,9},{9,10},{10,1... | collective-permute-start | bytes 1179656 | tf_op jit(solution)/shard_map/while/body/eval_jaxpr/ppermute | solution.py:32
  370.4 17.3 %collective-permute-start = (f32[24,64,64]{2,1,0:T(8,128)S(1)}, f32[24,64,64]{2,1,0:T(8,128)S(1)}, u32[]{:S(2)}, u32[]{:S(2)}) collective-permute-start(f32[24,64,64]{2,1,0:T(8,128)S(1)} %multiply_add_fusion.2), channel_id=1, source_target_pairs={{0,1},{1,2},{2,3},{3,4},{4,5},{5,6},{6,7},{7,8},{8,9},{9,10},{10,1... | collective-permute-start | bytes 1179656 | tf_op jit(solution)/shard_map/while/body/eval_jaxpr/ppermute | solution.py:32
  387.8 17.9 %collective-permute-start = (f32[24,64,64]{2,1,0:T(8,128)S(1)}, f32[24,64,64]{2,1,0:T(8,128)S(1)}, u32[]{:S(2)}, u32[]{:S(2)}) collective-permute-start(f32[24,64,64]{2,1,0:T(8,128)S(1)} %multiply_add_fusion.2), channel_id=1, source_target_pairs={{0,1},{1,2},{2,3},{3,4},{4,5},{5,6},{6,7},{7,8},{8,9},{9,10},{10,1... | collective-permute-start | bytes 1179656 | tf_op jit(solution)/shard_map/while/body/eval_jaxpr/ppermute | solution.py:32
  405.9 17.6 %collective-permute-start = (f32[24,64,64]{2,1,0:T(8,128)S(1)}, f32[24,64,64]{2,1,0:T(8,128)S(1)}, u32[]{:S(2)}, u32[]{:S(2)}) collective-permute-start(f32[24,64,64]{2,1,0:T(8,128)S(1)} %multiply_add_fusion.2), channel_id=1, source_target_pairs={{0,1},{1,2},{2,3},{3,4},{4,5},{5,6},{6,7},{7,8},{8,9},{9,10},{10,1... | collective-permute-start | bytes 1179656 | tf_op jit(solution)/shard_map/while/body/eval_jaxpr/ppermute | solution.py:32
  423.6 17.7 %collective-permute-start = (f32[24,64,64]{2,1,0:T(8,128)S(1)}, f32[24,64,64]{2,1,0:T(8,128)S(1)}, u32[]{:S(2)}, u32[]{:S(2)}) collective-permute-start(f32[24,64,64]{2,1,0:T(8,128)S(1)} %multiply_add_fusion.2), channel_id=1, source_target_pairs={{0,1},{1,2},{2,3},{3,4},{4,5},{5,6},{6,7},{7,8},{8,9},{9,10},{10,1... | collective-permute-start | bytes 1179656 | tf_op jit(solution)/shard_map/while/body/eval_jaxpr/ppermute | solution.py:32
  441.5 18.3 %collective-permute-start = (f32[24,64,64]{2,1,0:T(8,128)S(1)}, f32[24,64,64]{2,1,0:T(8,128)S(1)}, u32[]{:S(2)}, u32[]{:S(2)}) collective-permute-start(f32[24,64,64]{2,1,0:T(8,128)S(1)} %multiply_add_fusion.2), channel_id=1, source_target_pairs={{0,1},{1,2},{2,3},{3,4},{4,5},{5,6},{6,7},{7,8},{8,9},{9,10},{10,1... | collective-permute-start | bytes 1179656 | tf_op jit(solution)/shard_map/while/body/eval_jaxpr/ppermute | solution.py:32
  459.9 19.1 %collective-permute-start = (f32[24,64,64]{2,1,0:T(8,128)S(1)}, f32[24,64,64]{2,1,0:T(8,128)S(1)}, u32[]{:S(2)}, u32[]{:S(2)}) collective-permute-start(f32[24,64,64]{2,1,0:T(8,128)S(1)} %multiply_add_fusion.2), channel_id=1, source_target_pairs={{0,1},{1,2},{2,3},{3,4},{4,5},{5,6},{6,7},{7,8},{8,9},{9,10},{10,1... | collective-permute-start | bytes 1179656 | tf_op jit(solution)/shard_map/while/body/eval_jaxpr/ppermute | solution.py:32
  479.1 19.4 %collective-permute-start = (f32[24,64,64]{2,1,0:T(8,128)S(1)}, f32[24,64,64]{2,1,0:T(8,128)S(1)}, u32[]{:S(2)}, u32[]{:S(2)}) collective-permute-start(f32[24,64,64]{2,1,0:T(8,128)S(1)} %multiply_add_fusion.2), channel_id=1, source_target_pairs={{0,1},{1,2},{2,3},{3,4},{4,5},{5,6},{6,7},{7,8},{8,9},{9,10},{10,1... | collective-permute-start | bytes 1179656 | tf_op jit(solution)/shard_map/while/body/eval_jaxpr/ppermute | solution.py:32
  498.6 21.7 %collective-permute-start = (f32[24,64,64]{2,1,0:T(8,128)S(1)}, f32[24,64,64]{2,1,0:T(8,128)S(1)}, u32[]{:S(2)}, u32[]{:S(2)}) collective-permute-start(f32[24,64,64]{2,1,0:T(8,128)S(1)} %multiply_add_fusion.2), channel_id=1, source_target_pairs={{0,1},{1,2},{2,3},{3,4},{4,5},{5,6},{6,7},{7,8},{8,9},{9,10},{10,1... | collective-permute-start | bytes 1179656 | tf_op jit(solution)/shard_map/while/body/eval_jaxpr/ppermute | solution.py:32
  520.5 22.8 %collective-permute-start = (f32[24,64,64]{2,1,0:T(8,128)S(1)}, f32[24,64,64]{2,1,0:T(8,128)S(1)}, u32[]{:S(2)}, u32[]{:S(2)}) collective-permute-start(f32[24,64,64]{2,1,0:T(8,128)S(1)} %multiply_add_fusion.2), channel_id=1, source_target_pairs={{0,1},{1,2},{2,3},{3,4},{4,5},{5,6},{6,7},{7,8},{8,9},{9,10},{10,1... | collective-permute-start | bytes 1179656 | tf_op jit(solution)/shard_map/while/body/eval_jaxpr/ppermute | solution.py:32
  543.4 23.9 %collective-permute-start = (f32[24,64,64]{2,1,0:T(8,128)S(1)}, f32[24,64,64]{2,1,0:T(8,128)S(1)}, u32[]{:S(2)}, u32[]{:S(2)}) collective-permute-start(f32[24,64,64]{2,1,0:T(8,128)S(1)} %multiply_add_fusion.2), channel_id=1, source_target_pairs={{0,1},{1,2},{2,3},{3,4},{4,5},{5,6},{6,7},{7,8},{8,9},{9,10},{10,1... | collective-permute-start | bytes 1179656 | tf_op jit(solution)/shard_map/while/body/eval_jaxpr/ppermute | solution.py:32
  567.4 16.9 %collective-permute-start = (f32[24,64,64]{2,1,0:T(8,128)S(1)}, f32[24,64,64]{2,1,0:T(8,128)S(1)}, u32[]{:S(2)}, u32[]{:S(2)}) collective-permute-start(f32[24,64,64]{2,1,0:T(8,128)S(1)} %multiply_add_fusion.2), channel_id=1, source_target_pairs={{0,1},{1,2},{2,3},{3,4},{4,5},{5,6},{6,7},{7,8},{8,9},{9,10},{10,1... | collective-permute-start | bytes 1179656 | tf_op jit(solution)/shard_map/while/body/eval_jaxpr/ppermute | solution.py:32
  589.9 8.4 %copy-start.12 = (f32[1,24]{1,0:T(1,128)S(1)}, f32[1,24]{1,0:T(1,128)}, u32[]{:S(2)}) copy-start(f32[1,24]{1,0:T(1,128)} %param.25) | copy-start | bytes 292
  608.9 17.2 %slice-start = ((s8[4718592]{0:T(1024)(128)(4,1)}), s8[524288]{0:T(1024)(128)(4,1)S(1)}, s32[]{:S(2)}) async-start(s8[4718592]{0:T(1024)(128)(4,1)} %bitcast.168), calls=%async_computation.1 | async-start | bytes 1048576
  615.6 10.6 %copy-start.6 = (bf16[1,8,128,1536]{3,2,1,0:T(8,128)(2,1)S(1)}, bf16[1,8,128,1536]{3,2,1,0:T(8,128)(2,1)}, u32[]{:S(2)}) copy-start(bf16[1,8,128,1536]{3,2,1,0:T(8,128)(2,1)} %param.16) | copy-start | bytes 9437188
  615.6 10.6 %slice-start.1 = ((s8[4718592]{0:T(1024)(128)(4,1)}), s8[4194304]{0:T(1024)(128)(4,1)S(1)}, s32[]{:S(2)}) async-start(s8[4718592]{0:T(1024)(128)(4,1)} %bitcast.168), calls=%async_computation.2 | async-start | bytes 8388608
  675.6 39.9 %copy-start.1 = (bf16[1,1536,24]{1,2,0:T(8,128)(2,1)S(1)}, bf16[1,1536,24]{1,2,0:T(8,128)(2,1)}, u32[]{:S(2)}) copy-start(bf16[1,1536,24]{1,2,0:T(8,128)(2,1)} %param.20) | copy-start | bytes 221188
  675.9 37.9 %collective-permute-start.3 = (bf16[128,8,1536]{2,0,1:T(8,128)(2,1)S(1)}, bf16[128,8,1536]{2,0,1:T(8,128)(2,1)S(1)}, u32[]{:S(2)}, u32[]{:S(2)}) collective-permute-start(bf16[128,8,1536]{2,0,1:T(8,128)(2,1)S(1)} %bitcast.157), channel_id=1, source_target_pairs={{0,16},{16,32},{32,48},{48,64},{64,80},{80,96},{96,112},{112,0},{1... | collective-permute-start | bytes 9437192 | tf_op jit(solution)/shard_map/ppermute | solution.py:37
where the time goes:
time: 722 us; the launch traced here: 715 us
  waiting for transfers between devices  241 us (33%)
  local copies, waits for them, and re-layouts  214 us (30%)
  starting transfers between devices  96.1 us (13%)
  matrix products  77.2 us (11%)
  other arithmetic  43.3 us (6%)
  blocking collectives  42.1 us (6%)
    ppermute x15, waiting for transfers between devices, shifted(): return lax.ppermute(shard, axis, pairs)  195 us
    dynamic_update_slice x8, local copies, waits for them, and re-layouts, shards(): lax.scan(block_step, start, (x_all, b_all, c_all, log_all, dt_all))  166 us
    ppermute x15, starting transfers between devices, shifted(): return lax.ppermute(shard, axis, pairs)  90.7 us
    all_to_all x1, blocking collectives, shards(): lax.all_to_all(section_out, 'band', split_axis=1, concat_axis=0, tiled=True)  42.1 us
    ppermute x1, waiting for transfers between devices, passed_along(): lax.ppermute(shard, axis, [(i, (i + by) % peers) for i in range(peers)])  37.9 us
    unnamed x40, local copies, waits for them, and re-layouts  15.7 us
    dot_general x8, matrix products, block_step(): jnp.einsum('jhp,jn->hpn', scaled, b_block.astype(jnp.float32), precision=...  15.2 us
  transfers between devices with their start and end apart: 18, of which 18 were waited for; matrix products, arithmetic and copies ran while one was open for 0% of the time, Pallas kernels for 0%

commit v1 on v0

v1 whole, which is shorter than its diff:
```python
import functools

import jax
import jax.numpy as jnp
from jax import lax
from jax.experimental import pallas as pl
from jax.experimental.pallas import tpu as pltpu
from jax.sharding import PartitionSpec as P

EPSILON = 1e-05
ROWS = 8
LINE = 128
LENGTH = ROWS * LINE
HEADS = 24
WIDTH = 64
STATE = 64
INNER = HEADS * WIDTH
D = 1536
HALF = D // 2
GROUP = 384
GROUP_HEADS = GROUP // WIDTH
BANDS = 16
F32 = jnp.float32
BF16 = jnp.bfloat16
VMEM = 56 * 1024 * 1024


def params(limit=VMEM):
    return pltpu.CompilerParams(
        dimension_semantics=("arbitrary",), vmem_limit_bytes=limit
    )


def whole(*shape):
    return pl.BlockSpec(shape, lambda i: (0,) * len(shape))


def dot(a, b):
    return jnp.dot(a, b, preferred_element_type=F32)


def rms(values, gain):
    return values * lax.rsqrt(jnp.mean(values * values, -1, keepdims=True) + EPSILON) * gain


def silu(v):
    return v / (1.0 + jnp.exp(-v))


def head_spread(channels, first):
    head = lax.broadcasted_iota(jnp.int32, (HEADS, channels), 0)
    channel = lax.broadcasted_iota(jnp.int32, (HEADS, channels), 1)
    return jnp.where(head - first == channel // WIDTH, 1.0, 0.0).astype(BF16)


def to_channels(values, spread):
    high = values.astype(BF16)
    low = (values - high.astype(F32)).astype(BF16)
    return dot(high, spread) + dot(low, spread)


def project_kernel(
    tok, gain, w_x, w_bc, w_dt, dt_bias, rate, normed, xc, bc, cum, dt, band_tail, band_decay, total
):
    @pl.when(pl.program_id(0) == 0)
    def _():
        for r in range(ROWS):
            part = pl.ds(r * LINE, LINE)
            normed[part, :] = rms(tok[part, :].astype(F32), gain[...]).astype(BF16)
        bc[...] = dot(normed[...], w_bc[...]).astype(BF16)
        raw = dot(normed[...], w_dt[...]) + dt_bias[...]
        step = jnp.maximum(raw, 0.0) + jnp.log1p(jnp.exp(-jnp.abs(raw)))
        dt[...] = step
        log_decay = -rate[...] * step
        i = lax.broadcasted_iota(jnp.int32, (LINE, LINE), 0)
        j = lax.broadcasted_iota(jnp.int32, (LINE, LINE), 1)
        lower = jnp.where(i >= j, 1.0, 0.0).astype(F32)
        lines = [
            jnp.dot(
                lower,
                log_decay[r * LINE : (r + 1) * LINE],
                precision=lax.Precision.HIGHEST,
                preferred_element_type=F32,
            )
            for r in range(ROWS)
        ]
        ends = [line[LINE - 1 : LINE] for line in lines]
        before = [jnp.zeros_like(ends[0])]
        after = [jnp.zeros_like(ends[0])]
        for r in range(ROWS - 1):
            before.append(before[-1] + ends[r])
            after.append(after[-1] + ends[ROWS - 1 - r])
        for r in range(ROWS):
            part = pl.ds(r * LINE, LINE)
            cum[part, :] = lines[r]
            band_decay[part, :] = jnp.exp(lines[r] + before[r])
            band_tail[part, :] = step[r * LINE : (r + 1) * LINE] * jnp.exp(
                (ends[r] - lines[r]) + after[ROWS - 1 - r]
            )
        total[...] = before[-1] + ends[-1]

    for m in range(4):
        part = pl.ds(m * 256, 256)
        xc[part, :] = dot(normed[part, :], w_x[...]).astype(BF16)


def project(tok, gain, w_xbc, w_dt, dt_bias, rate):
    per_head = jax.ShapeDtypeStruct((LENGTH, HEADS), F32)
    return pl.pallas_call(
        project_kernel,
        grid=(6,),
        in_specs=[
            whole(LENGTH, D),
            whole(1, D),
            pl.BlockSpec((D, 256), lambda i: (0, i)),
            pl.BlockSpec((D, 128), lambda i: (0, INNER // 128)),
            whole(D, HEADS),
            whole(1, HEADS),
            whole(1, HEADS),
        ],
        out_specs=[
            whole(LENGTH, D),
            pl.BlockSpec((LENGTH, 256), lambda i: (0, i)),
            whole(LENGTH, 128),
            whole(LENGTH, HEADS),
            whole(LENGTH, HEADS),
            whole(LENGTH, HEADS),
            whole(LENGTH, HEADS),
            whole(1, HEADS),
        ],
        out_shape=[
            jax.ShapeDtypeStruct((LENGTH, D), BF16),
            jax.ShapeDtypeStruct((LENGTH, INNER), BF16),
            jax.ShapeDtypeStruct((LENGTH, 128), BF16),
            per_head,
            per_head,
            per_head,
            per_head,
            jax.ShapeDtypeStruct((1, HEADS), F32),
        ],
        compiler_params=params(),
        cost_estimate=pl.CostEstimate(
            flops=2 * LENGTH * D * 1688, bytes_accessed=16 << 20, transcendentals=LENGTH * 128
        ),
        name="project",
    )(tok, gain, w_xbc, w_xbc, w_dt, dt_bias, rate)


def gate_kernel(normed, w, out):
    for m in range(4):
        part = pl.ds(m * 256, 256)
        out[part, :] = silu(dot(normed[part, :], w[...])).astype(BF16)


def gate_of(normed, w_gate):
    return pl.pallas_call(
        gate_kernel,
        grid=(6,),
        in_specs=[whole(LENGTH, D), pl.BlockSpec((D, 256), lambda i: (0, i))],
        out_specs=pl.BlockSpec((LENGTH, 256), lambda i: (0, i)),
        out_shape=jax.ShapeDtypeStruct((LENGTH, INNER), BF16),
        compiler_params=params(),
        cost_estimate=pl.CostEstimate(
            flops=2 * LENGTH * D * INNER, bytes_accessed=11 << 20, transcendentals=LENGTH * INNER
        ),
        name="gate",
    )(normed, w_gate)


def convolved(above, own, below, taps, bias, out):
    channels = taps.shape[1]
    column = lax.broadcasted_iota(jnp.int32, (LINE, channels), 0)

    def line(r):
        if r < 0:
            return above.astype(F32)
        if r >= ROWS:
            return below.astype(F32)
        return own[pl.ds(r * LINE, LINE), :].astype(F32)

    for r in range(ROWS):
        lines = [line(r - 1), line(r), line(r + 1)]
        west, here, east = (
            sum(lines[i] * taps[3 * i + j : 3 * i + j + 1] for i in range(3)) for j in range(3)
        )
        west = jnp.where(column == 0, 0.0, pltpu.roll(west, 1, 0))
        east = jnp.where(column == LINE - 1, 0.0, pltpu.roll(east, LINE - 1, 0))
        out[pl.ds(r * LINE, LINE), :] = silu(west + here + east + bias).astype(BF16)


def conv_kernel(
    top,
    bottom,
    gain,
    w_x,
    w_bc,
    xc,
    bc,
    taps_x,
    taps_bc,
    bias_x,
    bias_bc,
    band_tail,
    total,
    x,
    bcs,
    pieces,
    edge,
    b_t,
):
    g = pl.program_id(0)

    @pl.when(g == 0)
    def _():
        edge[pl.ds(0, LINE), :] = rms(top[...].astype(F32), gain[...]).astype(BF16)
        edge[pl.ds(LINE, LINE), :] = rms(bottom[...].astype(F32), gain[...]).astype(BF16)
        side = dot(edge[...], w_bc[...]).astype(BF16)
        convolved(side[:LINE], bc, side[LINE:], taps_bc[...], bias_bc[...], bcs)
        for r in range(ROWS):
            part = pl.ds(r * LINE, LINE)
            b_t[:, part] = bcs[part, :].astype(F32).T.astype(BF16)

    side = dot(edge[...], w_x[...]).astype(BF16)
    convolved(side[:LINE], xc, side[LINE:], taps_x[...], bias_x[...], x)
    spread = head_spread(GROUP, g * GROUP_HEADS)
    state = jnp.zeros((STATE, GROUP), F32)
    for r in range(ROWS):
        part = pl.ds(r * LINE, LINE)
        weighted = x[part, :].astype(F32) * to_channels(band_tail[part, :], spread)
        state = state + dot(b_t[pl.ds(0, STATE), part], weighted.astype(BF16))
    head = lax.broadcasted_iota(jnp.int32, (HEADS, 128), 0)
    lane = lax.broadcasted_iota(jnp.int32, (HEADS, 128), 1)
    pick = jnp.where(head == lane + g * GROUP_HEADS, 1.0, 0.0).astype(BF16)
    first = total[...].astype(BF16)
    rest = total[...] - first.astype(F32)
    second = rest.astype(BF16)
    third = (rest - second.astype(F32)).astype(BF16)
    terms = jnp.concatenate(
        [dot(jnp.broadcast_to(t, (8, HEADS)), pick)[:1] for t in (first, second, third)]
        + [jnp.zeros((13, 128), F32)],
        axis=0,
    ).astype(BF16)
    for a in range(4):
        pieces[a, 0, :, pl.ds(0, GROUP)] = state[16 * a : 16 * a + 16].astype(BF16)
        pieces[a, 0, :, pl.ds(GROUP, 128)] = terms


def convolve(top, bottom, gain, w_xbc, xc, bc, conv_w, conv_bias, band_tail, total):
    return pl.pallas_call(
        conv_kernel,
        grid=(4,),
        in_specs=[
            whole(LINE, D),
            whole(LINE, D),
            whole(1, D),
            pl.BlockSpec((D, GROUP), lambda i: (0, i)),
            pl.BlockSpec((D, 128), lambda i: (0, INNER // 128)),
            pl.BlockSpec((LENGTH, GROUP), lambda i: (0, i)),
            whole(LENGTH, 128),
            pl.BlockSpec((9, GROUP), lambda i: (0, i)),
            pl.BlockSpec((9, 128), lambda i: (0, INNER // 128)),
            pl.BlockSpec((1, GROUP), lambda i: (0, i)),
            pl.BlockSpec((1, 128), lambda i: (0, INNER // 128)),
            whole(LENGTH, HEADS),
            whole(1, HEADS),
        ],
        out_specs=[
            pl.BlockSpec((LENGTH, GROUP), lambda i: (0, i)),
            whole(LENGTH, 128),
            pl.BlockSpec((4, 1, 16, GROUP + 128), lambda i: (0, i, 0, 0)),
        ],
        out_shape=[
            jax.ShapeDtypeStruct((LENGTH, INNER), BF16),
            jax.ShapeDtypeStruct((LENGTH, 128), BF16),
            jax.ShapeDtypeStruct((4, 4, 16, GROUP + 128), BF16),
        ],
        scratch_shapes=[pltpu.VMEM((2 * LINE, D), BF16), pltpu.VMEM((128, LENGTH), BF16)],
        compiler_params=params(),
        cost_estimate=pl.CostEstimate(
            flops=2 * 256 * D * 1664 + 40 * LENGTH * 1664,
            bytes_accessed=14 << 20,
            transcendentals=LENGTH * 1664,
        ),
        name="convolve",
    )(top, bottom, gain, w_xbc, w_xbc, xc, bc, conv_w, conv_w, conv_bias, conv_bias, band_tail, total)


def scan_kernel(x, bcs, cum, dt, gate, skip, out, spread, state):
    @pl.when(pl.program_id(0) == 0)
    def _():
        spread[...] = head_spread(INNER, 0)
        state[...] = jnp.zeros_like(state)

    sums = cum[...]
    sums_t = sums.T
    end = sums[LINE - 1 : LINE]
    both = bcs[...]
    lane = lax.broadcasted_iota(jnp.int32, (LINE, LINE), 1)
    row = lax.broadcasted_iota(jnp.int32, (LINE, LINE), 0)
    both_f = both.astype(F32)
    both_t = both_f.T.astype(BF16)
    c_only = jnp.where(lane < STATE, pltpu.roll(both_f, STATE, 1), 0.0).astype(BF16)
    weights = jnp.where(row >= lane, dot(c_only, both_t), 0.0)
    values = jnp.concatenate(
        [
            jnp.exp(sums),
            dt[...],
            dt[...] * jnp.exp(end - sums),
            jnp.broadcast_to(jnp.exp(end), (8, HEADS)),
            jnp.broadcast_to(skip[...], (8, HEADS)),
        ],
        axis=0,
    )
    high = values.astype(BF16)
    low = (values - high.astype(F32)).astype(BF16)
    for p in range(HEADS // 2):
        part = pl.ds(p * 128, 128)
        wide = dot(high, spread[:, part]) + dot(low, spread[:, part])
        carry, step, tail = wide[:LINE], wide[LINE : 2 * LINE], wide[2 * LINE : 3 * LINE]
        past, direct = wide[3 * LINE : 3 * LINE + 1], wide[3 * LINE + 8 : 3 * LINE + 9]
        values_x = x[:, part].astype(F32)
        stepped = values_x * step
        mixing = [
            (jnp.exp(jnp.minimum(sums[:, h : h + 1] - sums_t[h : h + 1], 0.0)) * weights).astype(BF16)
            for h in (2 * p, 2 * p + 1)
        ]
        columns = jnp.concatenate(
            [jnp.where(lane < WIDTH, stepped, 0.0), jnp.where(lane < WIDTH, 0.0, stepped)], axis=0
        ).astype(BF16)
        inner = dot(jnp.concatenate(mixing, axis=1), columns)
        carried = carry * dot(both, state[:, part].astype(BF16))
        y = inner + carried + direct * values_x
        out[:, part] = (y * gate[:, part].astype(F32)).astype(BF16)
        state[pl.ds(STATE, STATE), part] = past * state[pl.ds(STATE, STATE), part] + dot(
            both_t[:STATE], (values_x * tail).astype(BF16)
        )


def scan(x, bcs, cum, dt, gate, skip):
    line = lambda n: pl.BlockSpec((LINE, n), lambda i: (i, 0))
    return pl.pallas_call(
        scan_kernel,
        grid=(ROWS,),
        in_specs=[line(INNER), line(128), line(HEADS), line(HEADS), line(INNER), whole(1, HEADS)],
        out_specs=line(INNER),
        out_shape=jax.ShapeDtypeStruct((LENGTH, INNER), BF16),
        scratch_shapes=[pltpu.VMEM((HEADS, INNER), BF16), pltpu.VMEM((2 * STATE, INNER), F32)],
        compiler_params=params(),
        cost_estimate=pl.CostEstimate(
            flops=4 << 30, bytes_accessed=10 << 20, transcendentals=LENGTH * LINE * HEADS
        ),
        name="scan",
    )(x, bcs, cum, dt, gate, skip)


def relay_kernel(arrived, out):
    logs = jnp.concatenate(
        [
            jnp.sum(arrived[j, :, pl.ds(GROUP, 128)].astype(F32), axis=0, keepdims=True)
            for j in range(BANDS)
        ],
        axis=0,
    )
    decay = jnp.exp(logs)
    lane = lax.broadcasted_iota(jnp.int32, (128, GROUP), 0)
    channel = lax.broadcasted_iota(jnp.int32, (128, GROUP), 1)
    wide = to_channels(decay, jnp.where(lane == channel // WIDTH, 1.0, 0.0).astype(BF16))
    state = jnp.zeros((16, GROUP), F32)
    for j in range(BANDS):
        out[j] = state.astype(BF16)
        state = wide[j : j + 1] * state + arrived[j, :, pl.ds(0, GROUP)].astype(F32)


def relay(arrived):
    return pl.pallas_call(
        relay_kernel,
        out_shape=jax.ShapeDtypeStruct((BANDS, 16, GROUP), BF16),
        compiler_params=pltpu.CompilerParams(vmem_limit_bytes=16 << 20),
        name="relay",
    )(arrived)


def columns_out(values, tokens, turned, out):
    values = values + tokens
    for k in range(HALF // 128):
        part = slice(k * 128, (k + 1) * 128)
        for r in range(ROWS):
            turned[k, pl.ds(r, 32, stride=ROWS), :] = values[r * 32 : (r + 1) * 32, part]
        out[:, part] = turned[k].astype(BF16)


def finish_kernel(local, gate, bcs, band_decay, entering, gain, tok, w, hidden, out, spread, state, turned):
    @pl.when(pl.program_id(0) == 0)
    def _():
        spread[...] = head_spread(INNER, 0)
        state[pl.ds(0, STATE), :] = jnp.zeros((STATE, INNER), BF16)
        for a in range(4):
            for g in range(4):
                state[pl.ds(STATE + 16 * a, 16), pl.ds(g * GROUP, GROUP)] = entering[4 * a + g]

    both = bcs[...].reshape(256, 128)
    decay = band_decay[...].reshape(256, HEADS)
    carried = dot(both, state[...]) * to_channels(decay, spread[...])
    gated = local[...].reshape(256, INNER).astype(F32) + carried * gate[...].reshape(256, INNER).astype(F32)
    normed = rms(gated, gain[...]).astype(BF16)
    hidden[...] = normed.reshape(ROWS, 32, INNER)
    columns_out(dot(normed, w[...]), tok[...].reshape(256, HALF).astype(F32), turned, out)


def finish(local, gate, bcs, band_decay, entering, gain, tok, w_out):
    cells = lambda n: pl.BlockSpec((ROWS, 32, n), lambda i: (0, i, 0))
    return pl.pallas_call(
        finish_kernel,
        grid=(LINE // 32,),
        in_specs=[
            cells(INNER),
            cells(INNER),
            cells(128),
            cells(HEADS),
            whole(BANDS, 16, GROUP),
            whole(1, INNER),
            cells(HALF),
            whole(INNER, HALF),
        ],
        out_specs=[cells(INNER), pl.BlockSpec((256, HALF), lambda i: (i, 0))],
        out_shape=[
            jax.ShapeDtypeStruct((ROWS, LINE, INNER), BF16),
            jax.ShapeDtypeStruct((LENGTH, HALF), BF16),
        ],
        scratch_shapes=[
            pltpu.VMEM((HEADS, INNER), BF16),
            pltpu.VMEM((2 * STATE, INNER), BF16),
            pltpu.VMEM((HALF // 128, 256, 128), F32),
        ],
        compiler_params=params(),
        cost_estimate=pl.CostEstimate(
            flops=2 * LENGTH * D * HALF, bytes_accessed=16 << 20, transcendentals=LENGTH
        ),
        name="finish",
    )(local, gate, bcs, band_decay, entering, gain, tok, w_out)


def rest_kernel(hidden, tok, w, out, turned):
    columns_out(
        dot(hidden[...].reshape(256, INNER), w[...]),
        tok[...].reshape(256, HALF).astype(F32),
        turned,
        out,
    )


def rest(hidden, tok, w_out):
    return pl.pallas_call(
        rest_kernel,
        grid=(LINE // 32,),
        in_specs=[
            pl.BlockSpec((ROWS, 32, INNER), lambda i: (0, i, 0)),
            pl.BlockSpec((ROWS, 32, HALF), lambda i: (0, i, 1)),
            pl.BlockSpec((INNER, HALF), lambda i: (0, 1)),
        ],
        out_specs=pl.BlockSpec((256, HALF), lambda i: (i, 0)),
        out_shape=jax.ShapeDtypeStruct((LENGTH, HALF), BF16),
        scratch_shapes=[pltpu.VMEM((HALF // 128, 256, 128), F32)],
        compiler_params=params(),
        cost_estimate=pl.CostEstimate(
            flops=2 * LENGTH * D * HALF, bytes_accessed=8 << 20, transcendentals=0
        ),
        name="rest",
    )(hidden, tok, w_out)


def shards(
    tokens,
    in_gain,
    w_xbc,
    w_gate,
    w_dt,
    dt_bias,
    decay_rate,
    conv_w,
    conv_bias,
    skip,
    out_gain,
    w_out,
):
    bands = lax.axis_size("band")
    segments = lax.axis_size("segment")
    cells = tokens[0]
    tok = cells.reshape(LENGTH, D)
    top = lax.ppermute(cells[ROWS - 1], "band", [(i, i + 1) for i in range(bands - 1)])
    bottom = lax.ppermute(cells[0], "band", [(i + 1, i) for i in range(bands - 1)])

    normed, xc, bc, cum, dt, band_tail, band_decay, total = project(
        tok, in_gain, w_xbc[0], w_dt[0], dt_bias, decay_rate
    )
    gate = gate_of(normed, w_gate[0])
    x, bcs, pieces = convolve(
        top, bottom, in_gain, w_xbc[0], xc, bc, conv_w[0], conv_bias, band_tail, total
    )
    swap = functools.partial(
        lax.all_to_all, axis_name="band", split_axis=0, concat_axis=0, tiled=True
    )
    onward = functools.partial(
        lax.ppermute, axis_name="segment", perm=[(i, (i + 1) % segments) for i in range(segments)]
    )
    arrived = swap(pieces.reshape(BANDS, 16, GROUP + 128))
    local = scan(x, bcs, cum, dt, gate, skip)
    entering = swap(relay(arrived))

    grid = lambda a: a.reshape(ROWS, LINE, a.shape[-1])
    hidden, first = finish(
        grid(local), grid(gate), grid(bcs), grid(band_decay), entering, out_gain, cells, w_out[0]
    )
    first = onward(first.reshape(BANDS, LENGTH // BANDS, HALF))
    second = swap(rest(hidden, cells, w_out[0]).reshape(BANDS, LENGTH // BANDS, HALF))
    first = swap(first)
    second = onward(second)
    both = jnp.concatenate([first, second], axis=-1)
    handed = both.reshape(BANDS, LINE // BANDS, ROWS, D).swapaxes(0, 1)
    return handed.reshape(1, LINE // BANDS, BANDS * ROWS, D)


def solution(mesh):
    in_specs = (
        P("segment", "band", None, None),
        P("segment", None),
        P("segment", None, None),
        P("segment", None, None),
        P("segment", None, None),
        P("segment", None),
        P("segment", None),
        P("segment", None, None),
        P("segment", None),
        P("segment", None),
        P("segment", None),
        P("segment", None, None),
    )
    out_specs = P("segment", "band", None, None)
    return jax.shard_map(shards, mesh=mesh, in_specs=in_specs, out_specs=out_specs, check_vma=False)
```

time: 722 us -> 189 us (0.26)
  local copies, waits for them, and re-layouts: 214 us -> 6.09 us
  waiting for transfers between devices: 241 us -> 44.6 us
  Pallas kernels: 0 us -> 96.3 us
  matrix products: 77.2 us -> 0 us
  starting transfers between devices: 96.1 us -> 37.2 us
  blocking collectives: 42.1 us -> 0 us
  other arithmetic: 43.3 us -> 3.36 us
    ppermute x18 -> x4, waiting for transfers between devices: 241 us -> 14.5 us  [the longest x1 14.5 us: shards(): second = onward(second)]
    dynamic_update_slice x8 -> x0, local copies, waits for them, and re-layouts: 166 us -> none  [shards(): lax.scan(block_step, start, (x_all, b_all, c_all, log_all, dt_all))]
    pallas_call x0 -> x7, Pallas kernels: none -> 96.3 us  [the longest x1 35.5 us: scan(): pl.pallas_call(scan_kernel, grid=(ROWS,), in_specs=[line(INNER), line(128...]
    ppermute x18 -> x4, starting transfers between devices: 96.1 us -> 5.88 us  [the longest x1 4.57 us: shards(): lax.ppermute(cells[ROWS - 1], 'band', [(i, i + 1) for i in range(bands -...]
    dot_general x37 -> x0, matrix products: 77.2 us -> none  [the longest x8 15.2 us: block_step(): jnp.einsum('jhp,jn->hpn', scaled, b_block.astype(jnp.float32), precision=...]
    all_to_all x1 -> x0, blocking collectives: 42.1 us -> none  [shards(): lax.all_to_all(section_out, 'band', split_axis=1, concat_axis=0, tiled=True)]
    all_to_all x0 -> x4, starting transfers between devices: none -> 31.3 us  [the longest x1 10.1 us: shards(): arrived = swap(pieces.reshape(BANDS, 16, GROUP + 128))]
    all_to_all x0 -> x4, waiting for transfers between devices: none -> 30.1 us  [the longest x1 21.7 us: shards(): swap(rest(hidden, cells, w_out[0]).reshape(BANDS, LENGTH // BANDS, HALF))]
  transfers between devices with their start and end apart: 18 -> 8, of which waited for: 18 -> 3; matrix products, arithmetic and copies ran while one was open for 0% -> 2% of each run, Pallas kernels for 0% -> 32%
where the time goes in v1:
time: 189 us; the launch traced here: 188 us
  Pallas kernels  96.3 us (51%)
  waiting for transfers between devices  44.6 us (24%)
  starting transfers between devices  37.2 us (20%)
  local copies, waits for them, and re-layouts  6.09 us (3%)
  other arithmetic  3.36 us (2%)
    pallas_call x1, Pallas kernels, scan(): pl.pallas_call(scan_kernel, grid=(ROWS,), in_specs=[line(INNER), line(128...  35.5 us
    all_to_all x1, waiting for transfers between devices, shards(): swap(rest(hidden, cells, w_out[0]).reshape(BANDS, LENGTH // BANDS, HALF))  21.7 us
    pallas_call x1, Pallas kernels, convolve(): pl.pallas_call(conv_kernel, grid=(4,), in_specs=[whole(LINE, D), whole(LI...  16.7 us
    ppermute x1, waiting for transfers between devices, shards(): second = onward(second)  14.5 us
    pallas_call x1, Pallas kernels, project(): pl.pallas_call(project_kernel, grid=(6,), in_specs=[whole(LENGTH, D), who...  13.9 us
    pallas_call x1, Pallas kernels, finish(): pl.pallas_call(finish_kernel, grid=(LINE // 32,), in_specs=[cells(INNER),...  12.2 us
    all_to_all x1, starting transfers between devices, shards(): arrived = swap(pieces.reshape(BANDS, 16, GROUP + 128))  10.1 us
    pallas_call x1, Pallas kernels, gate_of(): pl.pallas_call(gate_kernel, grid=(6,), in_specs=[whole(LENGTH, D), pl.Blo...  10 us
  transfers between devices with their start and end apart: 8, of which 3 were waited for; matrix products, arithmetic and copies ran while one was open for 2% of the time, Pallas kernels for 32%

profile of v1, /device:TPU:0, one launch (start us, length us, event | category | flops | bytes accessed | tf_op | source)
XLA Modules:
  0.0 187.7 jit_solution(2770824320490809920)
XLA Ops:
  0.0 1.2 slice_bitcast_fusion
  1.2 1.3 collective-permute-start.1
  2.5 4.6 %collective-permute-start = (bf16[128,1536]{1,0:T(8,128)(2,1)S(1)}, bf16[128,1536]{1,0:T(8,128)(2,1)S(1)}, u32[]{:S(2)}, u32[]{:S(2)}) collective-permute-start(bf16[128,1536]{1,0:T(8,128)(2,1)S(1)} %get-tuple-element.32), channel_id=1, source_target_pairs={{0,1},{1,2},{2,3},{3,4},{4,5},{5,6},{6,7},{7,8},{8,9},{9,10},{10,1... | collective-permute-start | bytes 1179656 | tf_op jit(solution)/shard_map/ppermute | solution.py:490
  7.0 1.5 copy.18
  8.5 1.8 copy.13
  10.4 13.9 %project.1 = (bf16[1024,1536]{1,0:T(8,128)(2,1)}, bf16[1024,1536]{1,0:T(8,128)(2,1)}, bf16[1024,128]{1,0:T(8,128)(2,1)}, f32[1024,24]{1,0:T(8,128)}, f32[1024,24...) custom-call(bf16[1024,1536]{1,0:T(8,128)(2,1)} %bitcast.33, f32[1,1536]{1,0:T(1,128)} %gain.4, ...), custom_call_target="tpu_custom_call" | custom-call | flops 5309988864 | bytes 16777216 | tf_op jit(solution)/shard_map/project/pallas_call | solution.py:109
  24.3 0.0 collective-permute-done.1.bottom
  24.3 0.0 copy-start.1
  24.3 0.0 collective-permute-done.top
  24.3 0.0 copy-start.2
  24.3 0.7 copy-done.1
  25.0 0.2 copy-done.2
  25.2 16.7 %convolve.1 = (bf16[1024,1536]{1,0:T(8,128)(2,1)}, bf16[1024,128]{1,0:T(8,128)(2,1)}, bf16[4,4,16,512]{3,2,1,0:T(8,128)(2,1)}) custom-call(bf16[128,1536]{1,0:T(8,128)(2,1)} %copy-done.2, bf16[128,1536]{1,0:T(8,128)(2,1)} %copy-done.1, f32[1,1536]{1,0:T(1,128)} %gain.4, bf16[1536,1664]{1,0:T(8,128)(2,1)} %bitcast.29, bf16[1536,1664]{1,0:T(8,128)(2,1)} %bitcast.30, ...), custom_call_target="tpu_custom_call" | custom-call | flops 1376780288 | bytes 14680064 | tf_op jit(solution)/shard_map/convolve/pallas_call | solution.py:249
  41.9 10.1 %all-to-all-start = ((bf16[16,16,512]{2,1,0:T(8,128)(2,1)}), bf16[16,16,512]{2,1,0:T(8,128)(2,1)S(1)}, u32[]{:S(2)}, u32[]{:S(2)}) async-start(bf16[16,16,512]{2,1,0:T(8,128)(2,1)} %bitcast.44), calls=%async_computation | async-start | bytes 524288 | tf_op jit(solution)/shard_map/all_to_all | solution.py:506
  52.0 10.0 %gate.1 = bf16[1024,1536]{1,0:T(8,128)(2,1)} custom-call(bf16[1024,1536]{1,0:T(8,128)(2,1)} %get-tuple-element.26.normed, bf16[1536,1536]{1,0:T(8,128)(2,1)} %bitcast.45), custom_call_target="tpu_custom_call" | custom-call | flops 4831838208 | bytes 11534336 | tf_op jit(solution)/shard_map/gate/pallas_call | solution.py:156
  62.0 0.0 all-to-all-done.arrived
  62.0 0.9 relay.1
  62.9 7.2 %all-to-all-start.1 = ((bf16[16,16,384]{2,1,0:T(8,128)(2,1)}), bf16[16,16,384]{2,1,0:T(8,128)(2,1)S(1)}, u32[]{:S(2)}, u32[]{:S(2)}) async-start(bf16[16,16,384]{2,1,0:T(8,128)(2,1)} %relay.1), calls=%async_computation.1 | async-start | bytes 393216 | tf_op jit(solution)/shard_map/all_to_all | solution.py:508
  70.2 35.5 %scan.1 = bf16[1024,1536]{1,0:T(8,128)(2,1)} custom-call(bf16[1024,1536]{1,0:T(8,128)(2,1)} %get-tuple-element.22.x, bf16[1024,128]{1,0:T(8,128)(2,1)} %get-tuple-element.23.bcs, f32[1024,24]{1,0:T(8,128)} %get-tuple-element.24.cum, f32[1024,24]{1,0:T(8,128)} %get-tuple-element.25.dt, bf16[1024,1536]{1,0:T(8,128)(2,1)} %gate.1, f32[1,24]{1,0:T(1,128)} %skip.1), custom_call_target="tpu_custom_call" | custom-call | flops 4294967296 | bytes 10485760 | tf_op jit(solution)/shard_map/scan/pallas_call | solution.py:341
  105.6 0.0 all-to-all-done.1.entering
  105.7 0.0 copy-start
  105.7 0.7 copy-done
  106.3 12.2 %finish.1 = (bf16[8,128,1536]{2,1,0:T(8,128)(2,1)}, bf16[1024,768]{1,0:T(8,128)(2,1)}) custom-call(bf16[8,128,1536]{2,1,0:T(8,128)(2,1)} %bitcast.38, bf16[8,128,1536]{2,1,0:T(8,128)(2,1)} %bitcast.37, bf16[8,128,128]{2,1,0:T(8,128)(2,1)} %bitcast.43, f32[8,128,24]{2,1,0:T(8,128)} %bitcast.41, bf16[16,16,384]{2,1,0:T(8,128)(2,1)} %copy-done, ...), custom_call_target="tpu_custom_call" | custom-call | flops 2415919104 | bytes 16777216 | tf_op jit(solution)/shard_map/finish/pallas_call | solution.py:412
  118.6 7.1 %rest.1 = bf16[1024,768]{1,0:T(8,128)(2,1)} custom-call(bf16[8,128,1536]{2,1,0:T(8,128)(2,1)} %get-tuple-element.30.hidden, bf16[8,128,1536]{2,1,0:T(8,128)(2,1)} %bitcast.35, bf16[1536,1536]{1,0:T(8,128)(2,1)} %bitcast.32), custom_call_target="tpu_custom_call" | custom-call | flops 2415919104 | bytes 8388608 | tf_op jit(solution)/shard_map/rest/pallas_call | solution.py:453
  125.6 0.0 copy-start.3
  125.6 7.3 %all-to-all-start.3 = ((bf16[16,64,768]{2,1,0:T(8,128)(2,1)}), bf16[16,64,768]{2,1,0:T(8,128)(2,1)S(1)}, u32[]{:S(2)}, u32[]{:S(2)}) async-start(bf16[16,64,768]{2,1,0:T(8,128)(2,1)} %bitcast.36), calls=%async_computation.3 | async-start | bytes 3145728 | tf_op jit(solution)/shard_map/all_to_all | solution.py:515
  133.0 0.0 copy-done.3
  133.0 0.0 collective-permute-start.2
  133.0 21.7 %all-to-all-done.3 = bf16[16,64,768]{2,1,0:T(8,128)(2,1)S(1)} async-done(((bf16[16,64,768]{2,1,0:T(8,128)(2,1)}), bf16[16,64,768]{2,1,0:T(8,128)(2,1)S(1)}, u32[]{:S(2)}, u32[]{:S(2)}) %all-to-all-start.3) | async-done | bytes 1572896 | tf_op jit(solution)/shard_map/all_to_all | solution.py:515
  154.7 0.0 collective-permute-start.3
  154.7 0.0 collective-permute-done.2
  154.7 6.7 %all-to-all-start.2 = ((bf16[16,64,768]{2,1,0:T(8,128)(2,1)}), bf16[16,64,768]{2,1,0:T(8,128)(2,1)S(1)}, u32[]{:S(2)}, u32[]{:S(2)}) async-start(bf16[16,64,768]{2,1,0:T(8,128)(2,1)} %collective-permute-done.2), calls=%async_computation.2 | async-start | bytes 3145728 | tf_op jit(solution)/shard_map/all_to_all | solution.py:516
  161.4 14.5 %collective-permute-done.3 = bf16[16,64,768]{2,1,0:T(8,128)(2,1)} collective-permute-done((bf16[16,64,768]{2,1,0:T(8,128)(2,1)S(1)}, bf16[16,64,768]{2,1,0:T(8,128)(2,1)}, u32[]{:S(2)}, u32[]{:S(2)}) %collective-permute-start.3) | collective-permute-done | bytes 1572896 | tf_op jit(solution)/shard_map/ppermute | solution.py:517
  175.9 8.4 %all-to-all-done.2 = bf16[16,64,768]{2,1,0:T(8,128)(2,1)S(1)} async-done(((bf16[16,64,768]{2,1,0:T(8,128)(2,1)}), bf16[16,64,768]{2,1,0:T(8,128)(2,1)S(1)}, u32[]{:S(2)}, u32[]{:S(2)}) %all-to-all-start.2) | async-done | bytes 1572896 | tf_op jit(solution)/shard_map/all_to_all | solution.py:516
  184.3 3.4 %copy_bitcast_fusion = bf16[1,8,128,1536]{3,2,1,0:T(8,128)(2,1)} fusion(bf16[16,64,768]{2,1,0:T(8,128)(2,1)} %collective-permute-done.3, bf16[16,64,768]{2,1,0:T(8,128)(2,1)S(1)} %all-to-all-done.2), kind=kLoop, calls=%fused_computation.1 | loop fusion | flops 6291456 | bytes 6291456 | tf_op jit(solution)/shard_map/reshape | solution.py:520
Async XLA Ops:
  1.2 23.1 %collective-permute-start.1 = (bf16[128,1536]{1,0:T(8,128)(2,1)S(1)}, bf16[128,1536]{1,0:T(8,128)(2,1)S(1)}, u32[]{:S(2)}, u32[]{:S(2)}) collective-permute-start(bf16[128,1536]{1,0:T(8,128)(2,1)S(1)} %get-tuple-element.31), channel_id=1, source_target_pairs={{1,0},{2,1},{3,2},{4,3},{5,4},{6,5},{7,6},{8,7},{9,8},{10,9},{11,1... | collective-permute-start | bytes 1179656 | tf_op jit(solution)/shard_map/ppermute | solution.py:491
  2.5 21.8 %collective-permute-start = (bf16[128,1536]{1,0:T(8,128)(2,1)S(1)}, bf16[128,1536]{1,0:T(8,128)(2,1)S(1)}, u32[]{:S(2)}, u32[]{:S(2)}) collective-permute-start(bf16[128,1536]{1,0:T(8,128)(2,1)S(1)} %get-tuple-element.32), channel_id=1, source_target_pairs={{0,1},{1,2},{2,3},{3,4},{4,5},{5,6},{6,7},{7,8},{8,9},{9,10},{10,1... | collective-permute-start | bytes 1179656 | tf_op jit(solution)/shard_map/ppermute | solution.py:490
  24.3 0.8 copy-start.1
  24.3 0.9 copy-start.2
  41.9 20.1 %all-to-all-start = ((bf16[16,16,512]{2,1,0:T(8,128)(2,1)}), bf16[16,16,512]{2,1,0:T(8,128)(2,1)S(1)}, u32[]{:S(2)}, u32[]{:S(2)}) async-start(bf16[16,16,512]{2,1,0:T(8,128)(2,1)} %bitcast.44), calls=%async_computation | async-start | bytes 524288 | tf_op jit(solution)/shard_map/all_to_all | solution.py:506
  62.9 42.7 %all-to-all-start.1 = ((bf16[16,16,384]{2,1,0:T(8,128)(2,1)}), bf16[16,16,384]{2,1,0:T(8,128)(2,1)S(1)}, u32[]{:S(2)}, u32[]{:S(2)}) async-start(bf16[16,16,384]{2,1,0:T(8,128)(2,1)} %relay.1), calls=%async_computation.1 | async-start | bytes 393216 | tf_op jit(solution)/shard_map/all_to_all | solution.py:508
  105.7 0.7 copy-start
  125.6 7.4 %copy-start.3 = (bf16[1024,768]{1,0:T(8,128)(2,1)S(1)}, bf16[1024,768]{1,0:T(8,128)(2,1)}, u32[]{:S(2)}) copy-start(bf16[1024,768]{1,0:T(8,128)(2,1)} %get-tuple-element.29) | copy-start | bytes 4718596
  125.6 29.1 %all-to-all-start.3 = ((bf16[16,64,768]{2,1,0:T(8,128)(2,1)}), bf16[16,64,768]{2,1,0:T(8,128)(2,1)S(1)}, u32[]{:S(2)}, u32[]{:S(2)}) async-start(bf16[16,64,768]{2,1,0:T(8,128)(2,1)} %bitcast.36), calls=%async_computation.3 | async-start | bytes 3145728 | tf_op jit(solution)/shard_map/all_to_all | solution.py:515
  133.0 21.7 %collective-permute-start.2 = (bf16[16,64,768]{2,1,0:T(8,128)(2,1)S(1)}, bf16[16,64,768]{2,1,0:T(8,128)(2,1)}, u32[]{:S(2)}, u32[]{:S(2)}) collective-permute-start(bf16[16,64,768]{2,1,0:T(8,128)(2,1)S(1)} %bitcast.46), channel_id=1, source_target_pairs={{0,16},{16,32},{32,48},{48,64},{64,80},{80,96},{96,112},{112,0},{1... | collective-permute-start | bytes 4718600 | tf_op jit(solution)/shard_map/ppermute | solution.py:514
  154.7 21.2 %collective-permute-start.3 = (bf16[16,64,768]{2,1,0:T(8,128)(2,1)S(1)}, bf16[16,64,768]{2,1,0:T(8,128)(2,1)}, u32[]{:S(2)}, u32[]{:S(2)}) collective-permute-start(bf16[16,64,768]{2,1,0:T(8,128)(2,1)S(1)} %all-to-all-done.3), channel_id=1, source_target_pairs={{0,16},{16,32},{32,48},{48,64},{64,80},{80,96},{96,112},{112,0},{1... | collective-permute-start | bytes 4718600 | tf_op jit(solution)/shard_map/ppermute | solution.py:517
  154.7 29.6 %all-to-all-start.2 = ((bf16[16,64,768]{2,1,0:T(8,128)(2,1)}), bf16[16,64,768]{2,1,0:T(8,128)(2,1)S(1)}, u32[]{:S(2)}, u32[]{:S(2)}) async-start(bf16[16,64,768]{2,1,0:T(8,128)(2,1)} %collective-permute-done.2), calls=%async_computation.2 | async-start | bytes 3145728 | tf_op jit(solution)/shard_map/all_to_all | solution.py:516

commit v2 on v1

v2 whole, which is shorter than its diff:
```python
import functools

import jax
import jax.numpy as jnp
from jax import lax
from jax.experimental import pallas as pl
from jax.experimental.pallas import tpu as pltpu
from jax.sharding import PartitionSpec as P

EPSILON = 1e-05
ROWS = 8
LINE = 128
LENGTH = ROWS * LINE
HEADS = 24
WIDTH = 64
STATE = 64
INNER = HEADS * WIDTH
D = 1536
HALF = D // 2
GROUP = 384
GROUP_HEADS = GROUP // WIDTH
BANDS = 16
F32 = jnp.float32
BF16 = jnp.bfloat16
MIB = 1 << 20
LOG2E = 1.4426950408889634


def params(mib):
    return pltpu.CompilerParams(
        dimension_semantics=("arbitrary",), vmem_limit_bytes=mib * MIB
    )


def whole(*shape):
    return pl.BlockSpec(shape, lambda i: (0,) * len(shape), pipeline_mode=pl.Buffered(1))


def dot(a, b):
    return jnp.dot(a, b, preferred_element_type=F32)


def rms(values, gain):
    return values * lax.rsqrt(jnp.mean(values * values, -1, keepdims=True) + EPSILON) * gain


def silu(v):
    half = 0.5 * v
    return half + half * jnp.tanh(half)


def head_spread(channels, first):
    head = lax.broadcasted_iota(jnp.int32, (2 * HEADS, channels), 0)
    head = jnp.where(head < HEADS, head, head - HEADS)
    channel = lax.broadcasted_iota(jnp.int32, (2 * HEADS, channels), 1)
    return jnp.where(head - first == channel // WIDTH, 1.0, 0.0).astype(BF16)


def two_terms(values_t):
    high = values_t.astype(BF16).astype(F32)
    return jnp.concatenate([high, values_t - high], axis=0).T.astype(BF16)


def project_kernel(
    tok, gain, w_x, w_g, w_bc, w_dt, dt_bias, rate, xc, gate, bc, cum, dt, band_tail, band_decay, total, normed
):
    step = pl.program_id(0)

    @pl.when(step == 0)
    def _():
        for r in range(ROWS):
            part = pl.ds(r * LINE, LINE)
            normed[part, :] = rms(tok[part, :].astype(F32), gain[...]).astype(BF16)
        bc[...] = dot(normed[...], w_bc[...]).astype(BF16)
        raw = (
            lax.dot_general(
                w_dt[...], normed[...], (((1,), (1,)), ((), ())), preferred_element_type=F32
            )
            + dt_bias[...]
        )
        steps = jnp.maximum(raw, 0.0) + jnp.log1p(jnp.exp(-jnp.abs(raw)))
        dt[...] = steps
        log_decay = -rate[...] * steps
        i = lax.broadcasted_iota(jnp.int32, (LINE, LINE), 0)
        j = lax.broadcasted_iota(jnp.int32, (LINE, LINE), 1)
        sums = jnp.dot(
            jnp.concatenate([log_decay[:, r * LINE : (r + 1) * LINE] for r in range(ROWS)], axis=0),
            jnp.where(i <= j, 1.0, 0.0).astype(F32),
            precision=lax.Precision.HIGHEST,
            preferred_element_type=F32,
        )
        lines = [sums[r * HEADS : (r + 1) * HEADS] for r in range(ROWS)]
        ends = [line[:, LINE - 1 :] for line in lines]
        before = [jnp.zeros_like(ends[0])]
        after = [jnp.zeros_like(ends[0])]
        for r in range(ROWS - 1):
            before.append(before[-1] + ends[r])
            after.append(after[-1] + ends[ROWS - 1 - r])
        for r in range(ROWS):
            part = slice(r * LINE, (r + 1) * LINE)
            cum[:, part] = lines[r]
            band_decay[:, part] = jnp.exp(lines[r] + before[r])
            band_tail[:, part] = steps[:, part] * jnp.exp((ends[r] - lines[r]) + after[ROWS - 1 - r])
        total[...] = jnp.broadcast_to(before[-1] + ends[-1], (HEADS, LINE)).T[:1]

    @pl.when(step < 3)
    def _():
        for m in range(2):
            part = pl.ds(m * 512, 512)
            xc[part, :] = dot(normed[part, :], w_x[...]).astype(BF16)

    @pl.when(step >= 3)
    def _():
        for m in range(2):
            part = pl.ds(m * 512, 512)
            gate[part, :] = silu(dot(normed[part, :], w_g[...])).astype(BF16)


def project(tok, gain, w_xbc, w_gate, w_dt_t, dt_bias_t, rate_t):
    per_head = jax.ShapeDtypeStruct((HEADS, LENGTH), F32)
    first = lambda i: (0, jnp.minimum(i, 2))
    second = lambda i: (0, jnp.maximum(i - 3, 0))
    return pl.pallas_call(
        project_kernel,
        grid=(6,),
        in_specs=[
            whole(LENGTH, D),
            whole(1, D),
            pl.BlockSpec((D, 512), first),
            pl.BlockSpec((D, 512), second),
            pl.BlockSpec((D, 128), lambda i: (0, INNER // 128), pipeline_mode=pl.Buffered(1)),
            whole(HEADS, D),
            whole(HEADS, 1),
            whole(HEADS, 1),
        ],
        out_specs=[
            pl.BlockSpec((LENGTH, 512), first),
            pl.BlockSpec((LENGTH, 512), second),
            whole(LENGTH, 128),
            whole(HEADS, LENGTH),
            whole(HEADS, LENGTH),
            whole(HEADS, LENGTH),
            whole(HEADS, LENGTH),
            whole(1, HEADS),
        ],
        out_shape=[
            jax.ShapeDtypeStruct((LENGTH, INNER), BF16),
            jax.ShapeDtypeStruct((LENGTH, INNER), BF16),
            jax.ShapeDtypeStruct((LENGTH, 128), BF16),
            per_head,
            per_head,
            per_head,
            per_head,
            jax.ShapeDtypeStruct((1, HEADS), F32),
        ],
        scratch_shapes=[pltpu.VMEM((LENGTH, D), BF16)],
        compiler_params=params(32),
        cost_estimate=pl.CostEstimate(
            flops=2 * LENGTH * D * 3224, bytes_accessed=20 << 20, transcendentals=LENGTH * INNER
        ),
        name="project",
    )(tok, gain, w_xbc, w_gate, w_xbc, w_dt_t, dt_bias_t, rate_t)


def convolved(above, own, below, taps, bias, out):
    channels = bias.shape[1]
    column = lax.broadcasted_iota(jnp.int32, (LINE, channels), 0)

    def line(r):
        if r < 0:
            return above.astype(F32)
        if r >= ROWS:
            return below.astype(F32)
        return own[pl.ds(r * LINE, LINE), :].astype(F32)

    for r in range(ROWS):
        lines = [line(r - 1), line(r), line(r + 1)]
        west, here, east = (
            lines[0] * taps[j] + lines[1] * taps[3 + j] + lines[2] * taps[6 + j] for j in range(3)
        )
        west = jnp.where(column == 0, 0.0, pltpu.roll(west, 1, 0))
        east = jnp.where(column == LINE - 1, 0.0, pltpu.roll(east, LINE - 1, 0))
        out[pl.ds(r * LINE, LINE), :] = silu(west + here + east + bias).astype(BF16)


def conv_kernel(
    top,
    bottom,
    gain,
    w_x,
    w_bc,
    xc,
    bc,
    taps_x,
    taps_bc,
    bias_x,
    bias_bc,
    band_tail,
    total,
    x,
    bcs,
    pieces,
    edge,
    b_t,
    tails,
):
    g = pl.program_id(0)

    @pl.when(g == 0)
    def _():
        edge[pl.ds(0, LINE), :] = rms(top[...].astype(F32), gain[...]).astype(BF16)
        edge[pl.ds(LINE, LINE), :] = rms(bottom[...].astype(F32), gain[...]).astype(BF16)
        side = dot(edge[...], w_bc[...]).astype(BF16)
        convolved(side[:LINE], bc, side[LINE:], [taps_bc[k] for k in range(9)], bias_bc[...], bcs)
        for r in range(ROWS):
            part = pl.ds(r * LINE, LINE)
            b_t[:, part] = bcs[part, :].astype(F32).T.astype(BF16)
            tails[part, :] = two_terms(band_tail[:, part])

    side = dot(edge[...], w_x[...]).astype(BF16)
    convolved(side[:LINE], xc, side[LINE:], [taps_x[k] for k in range(9)], bias_x[...], x)
    spread = head_spread(GROUP, g * GROUP_HEADS)
    state = jnp.zeros((STATE, GROUP), F32)
    for r in range(ROWS // 2):
        part = pl.ds(r * 2 * LINE, 2 * LINE)
        weighted = x[part, :].astype(F32) * dot(tails[part, :], spread)
        state = state + dot(b_t[pl.ds(0, STATE), part], weighted.astype(BF16))
    head = lax.broadcasted_iota(jnp.int32, (HEADS, 128), 0)
    lane = lax.broadcasted_iota(jnp.int32, (HEADS, 128), 1)
    pick = jnp.where(head == lane + g * GROUP_HEADS, 1.0, 0.0).astype(BF16)
    first = total[...].astype(BF16)
    rest = total[...] - first.astype(F32)
    second = rest.astype(BF16)
    third = (rest - second.astype(F32)).astype(BF16)
    terms = jnp.concatenate(
        [dot(jnp.broadcast_to(t, (8, HEADS)), pick)[:1] for t in (first, second, third)]
        + [jnp.zeros((13, 128), F32)],
        axis=0,
    ).astype(BF16)
    for a in range(4):
        pieces[a, 0, :, pl.ds(0, GROUP)] = state[16 * a : 16 * a + 16].astype(BF16)
        pieces[a, 0, :, pl.ds(GROUP, 128)] = terms


def convolve(top, bottom, gain, w_xbc, xc, bc, taps, conv_bias, band_tail, total):
    return pl.pallas_call(
        conv_kernel,
        grid=(4,),
        in_specs=[
            whole(LINE, D),
            whole(LINE, D),
            whole(1, D),
            pl.BlockSpec((D, GROUP), lambda i: (0, i)),
            pl.BlockSpec((D, 128), lambda i: (0, INNER // 128), pipeline_mode=pl.Buffered(1)),
            pl.BlockSpec((LENGTH, GROUP), lambda i: (0, i)),
            whole(LENGTH, 128),
            pl.BlockSpec((9, 1, GROUP), lambda i: (0, 0, i)),
            pl.BlockSpec((9, 1, 128), lambda i: (0, 0, INNER // 128)),
            pl.BlockSpec((1, GROUP), lambda i: (0, i)),
            pl.BlockSpec((1, 128), lambda i: (0, INNER // 128)),
            whole(HEADS, LENGTH),
            whole(1, HEADS),
        ],
        out_specs=[
            pl.BlockSpec((LENGTH, GROUP), lambda i: (0, i)),
            whole(LENGTH, 128),
            pl.BlockSpec((4, 1, 16, GROUP + 128), lambda i: (0, i, 0, 0)),
        ],
        out_shape=[
            jax.ShapeDtypeStruct((LENGTH, INNER), BF16),
            jax.ShapeDtypeStruct((LENGTH, 128), BF16),
            jax.ShapeDtypeStruct((4, 4, 16, GROUP + 128), BF16),
        ],
        scratch_shapes=[
            pltpu.VMEM((2 * LINE, D), BF16),
            pltpu.VMEM((128, LENGTH), BF16),
            pltpu.VMEM((LENGTH, 2 * HEADS), BF16),
        ],
        compiler_params=params(20),
        cost_estimate=pl.CostEstimate(
            flops=2 * 256 * D * 1664 + 40 * LENGTH * 1664,
            bytes_accessed=14 << 20,
            transcendentals=LENGTH * 1664,
        ),
        name="convolve",
    )(top, bottom, gain, w_xbc, w_xbc, xc, bc, taps, taps, conv_bias, conv_bias, band_tail, total)


def scan_kernel(x, bcs, cum, dt, gate, skip, out, direct, state):
    @pl.when(pl.program_id(0) == 0)
    def _():
        direct[...] = dot(
            two_terms(jnp.broadcast_to(skip[...], (HEADS, 8))), head_spread(INNER, 0)
        )
        state[...] = jnp.zeros_like(state)

    sums_t = cum[...] * LOG2E
    step_t = dt[...]
    sums = sums_t.T
    step = step_t.T
    both = bcs[...].astype(F32)
    lane = lax.broadcasted_iota(jnp.int32, (LINE, LINE), 1)
    row = lax.broadcasted_iota(jnp.int32, (LINE, LINE), 0)
    left = lane < WIDTH
    b_t = both.T.astype(BF16)[:STATE]
    c = pltpu.roll(both, STATE, 1).astype(BF16)[:, :STATE]
    weights = jnp.where(row >= lane, dot(c, b_t), 0.0)

    def mixing(h):
        along = jnp.broadcast_to(sums[:, h : h + 1], (LINE, LINE))
        decay = jnp.exp2(jnp.minimum(along - sums_t[h : h + 1], 0.0))
        return along, (decay * (weights * step_t[h : h + 1])).astype(BF16)

    for q in range(HEADS // 4):
        quad = pl.ds(q * 256, 256)
        carried = dot(c, state[:, quad].astype(BF16))
        tails, decays = [], []
        for p in (2 * q, 2 * q + 1):
            part = pl.ds(p * 128, 128)
            values = x[:, part].astype(F32)
            (along_a, mixing_a), (along_b, mixing_b) = mixing(2 * p), mixing(2 * p + 1)
            columns = jnp.concatenate(
                [jnp.where(left, values, 0.0), jnp.where(left, 0.0, values)], axis=0
            ).astype(BF16)
            inner = dot(jnp.concatenate([mixing_a, mixing_b], axis=1), columns)
            here = jnp.where(left, along_a, along_b)
            carry = jnp.exp2(here)
            stepped = jnp.where(left, step[:, 2 * p : 2 * p + 1], step[:, 2 * p + 1 : 2 * p + 2])
            tails.append((values * stepped * jnp.exp2(here[LINE - 1 :] - here)).astype(BF16))
            decays.append(carry[LINE - 1 :])
            side = slice((p % 2) * 128, (p % 2) * 128 + 128)
            y = inner + carry * carried[:, side] + direct[0:1, part] * values
            out[:, part] = (y * gate[:, part].astype(F32)).astype(BF16)
        state[:, quad] = jnp.concatenate(decays, axis=1) * state[:, quad] + dot(
            b_t, jnp.concatenate(tails, axis=1)
        )


def scan(x, bcs, cum, dt, gate, skip_t):
    line = lambda n: pl.BlockSpec((LINE, n), lambda i: (i, 0))
    heads = pl.BlockSpec((HEADS, LINE), lambda i: (0, i))
    return pl.pallas_call(
        scan_kernel,
        grid=(ROWS,),
        in_specs=[line(INNER), line(128), heads, heads, line(INNER), whole(HEADS, 1)],
        out_specs=line(INNER),
        out_shape=jax.ShapeDtypeStruct((LENGTH, INNER), BF16),
        scratch_shapes=[pltpu.VMEM((8, INNER), F32), pltpu.VMEM((STATE, INNER), F32)],
        compiler_params=params(12),
        cost_estimate=pl.CostEstimate(
            flops=4 << 30, bytes_accessed=10 << 20, transcendentals=LENGTH * LINE * HEADS
        ),
        name="scan",
    )(x, bcs, cum, dt, gate, skip_t)


def relay_kernel(arrived, out):
    logs = jnp.concatenate(
        [
            jnp.sum(arrived[j, :, pl.ds(GROUP, 128)].astype(F32), axis=0, keepdims=True)
            for j in range(BANDS)
        ],
        axis=0,
    )
    decay = jnp.exp(logs)
    high = decay.astype(BF16)
    low = (decay - high.astype(F32)).astype(BF16)
    lane = lax.broadcasted_iota(jnp.int32, (128, GROUP), 0)
    channel = lax.broadcasted_iota(jnp.int32, (128, GROUP), 1)
    spread = jnp.where(lane == channel // WIDTH, 1.0, 0.0).astype(BF16)
    wide = dot(high, spread) + dot(low, spread)
    state = jnp.zeros((16, GROUP), F32)
    for j in range(BANDS):
        out[j] = state.astype(BF16)
        state = wide[j : j + 1] * state + arrived[j, :, pl.ds(0, GROUP)].astype(F32)


def relay(arrived):
    return pl.pallas_call(
        relay_kernel,
        out_shape=jax.ShapeDtypeStruct((BANDS, 16, GROUP), BF16),
        compiler_params=pltpu.CompilerParams(vmem_limit_bytes=4 * MIB),
        name="relay",
    )(arrived)


def columns_out(values, tokens, turned, out):
    values = values + tokens
    for k in range(HALF // 128):
        part = slice(k * 128, (k + 1) * 128)
        for r in range(ROWS):
            turned[k, pl.ds(r, 32, stride=ROWS), :] = values[r * 32 : (r + 1) * 32, part]
        out[:, part] = turned[k].astype(BF16)


def finish_kernel(
    local, gate, bcs, band_decay, entering, gain, tok, w, hidden, out, spread, state, decays, turned
):
    step = pl.program_id(0)

    @pl.when(step == 0)
    def _():
        spread[...] = head_spread(INNER, 0)
        state[pl.ds(0, STATE), :] = jnp.zeros((STATE, INNER), BF16)
        for a in range(4):
            for g in range(4):
                state[pl.ds(STATE + 16 * a, 16), pl.ds(g * GROUP, GROUP)] = entering[4 * a + g]
        for r in range(ROWS):
            decays[r] = two_terms(band_decay[:, r * LINE : (r + 1) * LINE])

    both = bcs[...].reshape(256, 128)
    here = pl.ds(pl.multiple_of(step * 32, 32), 32)
    decay = dot(decays[:, here, :].reshape(256, 2 * HEADS), spread[...])
    gated = local[...].reshape(256, INNER).astype(F32) + (
        dot(both, state[...]) * decay * gate[...].reshape(256, INNER).astype(F32)
    )
    normed = rms(gated, gain[...]).astype(BF16)
    hidden[...] = normed.reshape(ROWS, 32, INNER)
    columns_out(dot(normed, w[...]), tok[...].reshape(256, HALF).astype(F32), turned, out)


def finish(local, gate, bcs, band_decay, entering, gain, tok, w_out):
    cells = lambda n: pl.BlockSpec((ROWS, 32, n), lambda i: (0, i, 0))
    return pl.pallas_call(
        finish_kernel,
        grid=(LINE // 32,),
        in_specs=[
            cells(INNER),
            cells(INNER),
            cells(128),
            whole(HEADS, LENGTH),
            whole(BANDS, 16, GROUP),
            whole(1, INNER),
            cells(HALF),
            whole(INNER, HALF),
        ],
        out_specs=[cells(INNER), pl.BlockSpec((256, HALF), lambda i: (i, 0))],
        out_shape=[
            jax.ShapeDtypeStruct((ROWS, LINE, INNER), BF16),
            jax.ShapeDtypeStruct((LENGTH, HALF), BF16),
        ],
        scratch_shapes=[
            pltpu.VMEM((2 * HEADS, INNER), BF16),
            pltpu.VMEM((2 * STATE, INNER), BF16),
            pltpu.VMEM((ROWS, LINE, 2 * HEADS), BF16),
            pltpu.VMEM((HALF // 128, 256, 128), F32),
        ],
        compiler_params=params(24),
        cost_estimate=pl.CostEstimate(
            flops=2 * LENGTH * D * HALF, bytes_accessed=16 << 20, transcendentals=LENGTH
        ),
        name="finish",
    )(local, gate, bcs, band_decay, entering, gain, tok, w_out)


def rest_kernel(hidden, tok, w, out, turned):
    columns_out(
        dot(hidden[...].reshape(256, INNER), w[...]),
        tok[...].reshape(256, HALF).astype(F32),
        turned,
        out,
    )


def rest(hidden, tok, w_out):
    return pl.pallas_call(
        rest_kernel,
        grid=(LINE // 32,),
        in_specs=[
            pl.BlockSpec((ROWS, 32, INNER), lambda i: (0, i, 0)),
            pl.BlockSpec((ROWS, 32, HALF), lambda i: (0, i, 1)),
            pl.BlockSpec((INNER, HALF), lambda i: (0, 1), pipeline_mode=pl.Buffered(1)),
        ],
        out_specs=pl.BlockSpec((256, HALF), lambda i: (i, 0)),
        out_shape=jax.ShapeDtypeStruct((LENGTH, HALF), BF16),
        scratch_shapes=[pltpu.VMEM((HALF // 128, 256, 128), F32)],
        compiler_params=params(12),
        cost_estimate=pl.CostEstimate(flops=1 << 20, bytes_accessed=1 << 20, transcendentals=0),
        name="rest",
    )(hidden, tok, w_out)


def shards(
    tokens,
    in_gain,
    w_xbc,
    w_gate,
    w_dt,
    dt_bias,
    decay_rate,
    conv_w,
    conv_bias,
    skip,
    out_gain,
    w_out,
):
    bands = lax.axis_size("band")
    segments = lax.axis_size("segment")
    cells = tokens[0]
    tok = cells.reshape(LENGTH, D)
    top = lax.ppermute(cells[ROWS - 1], "band", [(i, i + 1) for i in range(bands - 1)])
    bottom = lax.ppermute(cells[0], "band", [(i + 1, i) for i in range(bands - 1)])

    xc, gate, bc, cum, dt, band_tail, band_decay, total = project(
        tok, in_gain, w_xbc[0], w_gate[0], w_dt[0].T, dt_bias.T, decay_rate.T
    )
    x, bcs, pieces = convolve(
        top, bottom, in_gain, w_xbc[0], xc, bc, conv_w.swapaxes(0, 1), conv_bias, band_tail, total
    )
    swap = functools.partial(
        lax.all_to_all, axis_name="band", split_axis=0, concat_axis=0, tiled=True
    )
    onward = functools.partial(
        lax.ppermute, axis_name="segment", perm=[(i, (i + 1) % segments) for i in range(segments)]
    )
    arrived = swap(pieces.reshape(BANDS, 16, GROUP + 128))
    local = scan(x, bcs, cum, dt, gate, skip.T)
    entering = swap(relay(arrived))

    grid = lambda a: a.reshape(ROWS, LINE, a.shape[-1])
    hidden, first = finish(
        grid(local), grid(gate), grid(bcs), band_decay, entering, out_gain, cells, w_out[0]
    )
    first = onward(first.reshape(BANDS, LENGTH // BANDS, HALF))
    second = swap(rest(hidden, cells, w_out[0]).reshape(BANDS, LENGTH // BANDS, HALF))
    first = swap(first)
    second = onward(second)
    both = jnp.concatenate([first, second], axis=-1)
    handed = both.reshape(BANDS, LINE // BANDS, ROWS, D).swapaxes(0, 1)
    return handed.reshape(1, LINE // BANDS, BANDS * ROWS, D)


def solution(mesh):
    in_specs = (
        P("segment", "band", None, None),
        P("segment", None),
        P("segment", None, None),
        P("segment", None, None),
        P("segment", None, None),
        P("segment", None),
        P("segment", None),
        P("segment", None, None),
        P("segment", None),
        P("segment", None),
        P("segment", None),
        P("segment", None, None),
    )
    out_specs = P("segment", "band", None, None)
    return jax.shard_map(shards, mesh=mesh, in_specs=in_specs, out_specs=out_specs, check_vma=False)
```

time: 189 us -> 174 us (0.921)
  Pallas kernels: 96.3 us -> 54.4 us
  local copies, waits for them, and re-layouts: 6.09 us -> 29.7 us
  waiting for transfers between devices: 44.6 us -> 51 us
  starting transfers between devices: 37.2 us -> 34.1 us
    pallas_call x1, Pallas kernels: 35.5 us -> 11.2 us  [scan(): pl.pallas_call(scan_kernel, grid=(ROWS,), in_specs=[line(INNER), line(128...]
    unnamed x10 -> x56, local copies, waits for them, and re-layouts: 4.93 us -> 27 us
    pallas_call x1 -> x0, Pallas kernels: 10 us -> none  [gate_of(): pl.pallas_call(gate_kernel, grid=(6,), in_specs=[whole(LENGTH, D), pl.Blo...]
    all_to_all x1, waiting for transfers between devices: 0.01 us -> 8.42 us  [shards(): arrived = swap(pieces.reshape(BANDS, 16, GROUP + 128))]
    all_to_all x1, starting transfers between devices: 7.22 us -> 3.73 us  [shards(): entering = swap(relay(arrived))]
    pallas_call x1, Pallas kernels: 12.2 us -> 8.92 us  [finish(): pl.pallas_call(finish_kernel, grid=(LINE // 32,), in_specs=[cells(INNER),...]
    pallas_call x1, Pallas kernels: 16.7 us -> 13.7 us  [convolve(): pl.pallas_call(conv_kernel, grid=(4,), in_specs=[whole(LINE, D), whole(LI...]
    pallas_call x1, Pallas kernels: 7.09 us -> 4.25 us  [rest(): pl.pallas_call(rest_kernel, grid=(LINE // 32,), in_specs=[pl.BlockSpec((R...]
  transfers between devices with their start and end apart: 8 -> 8, of which waited for: 3 -> 5; matrix products, arithmetic and copies ran while one was open for 2% -> 1% of each run, Pallas kernels for 32% -> 15%
where the time goes in v2:
time: 174 us; the launch traced here: 173 us
  Pallas kernels  54.4 us (31%)
  waiting for transfers between devices  51 us (29%)
  starting transfers between devices  34.1 us (20%)
  local copies, waits for them, and re-layouts  29.7 us (17%)
  other arithmetic  3.36 us (2%)
    unnamed x56, local copies, waits for them, and re-layouts  27 us
    all_to_all x1, waiting for transfers between devices, shards(): swap(rest(hidden, cells, w_out[0]).reshape(BANDS, LENGTH // BANDS, HALF))  20.7 us
    pallas_call x1, Pallas kernels, project(): pl.pallas_call(project_kernel, grid=(6,), in_specs=[whole(LENGTH, D), who...  15.4 us
    pallas_call x1, Pallas kernels, convolve(): pl.pallas_call(conv_kernel, grid=(4,), in_specs=[whole(LINE, D), whole(LI...  13.7 us
    ppermute x1, waiting for transfers between devices, shards(): second = onward(second)  13.5 us
    pallas_call x1, Pallas kernels, scan(): pl.pallas_call(scan_kernel, grid=(ROWS,), in_specs=[line(INNER), line(128...  11.2 us
    all_to_all x1, starting transfers between devices, shards(): arrived = swap(pieces.reshape(BANDS, 16, GROUP + 128))  10.1 us
    pallas_call x1, Pallas kernels, finish(): pl.pallas_call(finish_kernel, grid=(LINE // 32,), in_specs=[cells(INNER),...  8.92 us
  transfers between devices with their start and end apart: 8, of which 5 were waited for; matrix products, arithmetic and copies ran while one was open for 1% of the time, Pallas kernels for 15%

profile of v2, /device:TPU:0, one launch (start us, length us, event | category | flops | bytes accessed | tf_op | source)
XLA Modules:
  0.0 172.9 jit_solution(16841279220611830184)
XLA Ops:
  0.0 1.2 slice_bitcast_fusion
  1.2 1.3 collective-permute-start.1
  2.5 4.6 %collective-permute-start = (bf16[128,1536]{1,0:T(8,128)(2,1)S(1)}, bf16[128,1536]{1,0:T(8,128)(2,1)S(1)}, u32[]{:S(2)}, u32[]{:S(2)}) collective-permute-start(bf16[128,1536]{1,0:T(8,128)(2,1)S(1)} %get-tuple-element.32), channel_id=1, source_target_pairs={{0,1},{1,2},{2,3},{3,4},{4,5},{5,6},{6,7},{7,8},{8,9},{9,10},{10,1... | collective-permute-start | bytes 1179656 | tf_op jit(solution)/shard_map/ppermute | solution.py:501
  7.0 0.7 copy.13.dt_bias
  7.8 0.7 copy.14.rate
  8.5 2.4 %copy-done = bf16[1,1536,1664]{2,1,0:T(8,128)(2,1)S(1)} copy-done((bf16[1,1536,1664]{2,1,0:T(8,128)(2,1)S(1)}, bf16[1,1536,1664]{2,1,0:T(8,128)(2,1)}, u32[]{:S(2)}) %copy-start) | copy-done | bytes 5111832
  11.0 1.9 %copy-done.2 = bf16[1,8,128,1536]{3,2,1,0:T(8,128)(2,1)S(1)} copy-done((bf16[1,8,128,1536]{3,2,1,0:T(8,128)(2,1)S(1)}, bf16[1,8,128,1536]{3,2,1,0:T(8,128)(2,1)}, u32[]{:S(2)}) %copy-start.2) | copy-done | bytes 3145752
  12.9 0.7 copy-done.15
  13.6 2.3 %copy-done.17 = bf16[1,1536,1536]{2,1,0:T(8,128)(2,1)S(1)} copy-done((bf16[1,1536,1536]{2,1,0:T(8,128)(2,1)S(1)}, bf16[1,1536,1536]{2,1,0:T(8,128)(2,1)}, u32[]{:S(2)}) %copy-start.17) | copy-done | bytes 4718616
  15.9 0.9 copy-done.22
  16.8 15.4 %project.1 = (bf16[1024,1536]{1,0:T(8,128)(2,1)S(1)}, bf16[1024,1536]{1,0:T(8,128)(2,1)S(1)}, bf16[1024,128]{1,0:T(8,128)(2,1)S(1)}, f32[24,1024]{1,0:T(8,128)S(...) custom-call(bf16[1024,1536]{1,0:T(8,128)(2,1)S(1)} %bitcast.35, ...), custom_call_target="tpu_custom_call" | custom-call | flops 10141827072 | bytes 20971520 | tf_op jit(solution)/shard_map/project/pallas_call | solution.py:123
  32.2 0.0 copy-start.5
  32.2 0.0 copy-start.23
  32.2 0.0 copy-start.25
  32.2 0.0 collective-permute-done.1.bottom
  32.2 0.0 collective-permute-done.top
  32.2 0.0 copy-done.13
  32.2 0.0 copy-done.14
  32.2 0.0 copy-start.27
  32.2 13.7 %convolve.1 = (bf16[1024,1536]{1,0:T(8,128)(2,1)S(1)}, bf16[1024,128]{1,0:T(8,128)(2,1)S(1)}, bf16[4,4,16,512]{3,2,1,0:T(8,128)(2,1)}) custom-call(bf16[128,1536]{1,0:T(8,128)(2,1)S(1)} %collective-permute-done.top, bf16[128,1536]{1,0:T(8,128)(2,1)S(1)} %collective-permute-done.1.bottom, f32[1,1536]{1,0:T(1,128)S(1)} %copy-done.15, ...), custom_call_target="tpu_custom_call" | custom-call | flops 1376780288 | bytes 14680064 | tf_op jit(solution)/shard_map/convolve/pallas_call | solution.py:246
  46.0 0.0 copy-done.5
  46.0 0.0 copy-done.23
  46.0 0.0 copy-done.25
  46.0 0.0 copy-start.10
  46.0 0.7 copy-done.10
  46.7 1.7 copy-done.18
  48.4 10.1 %all-to-all-start = ((bf16[16,16,512]{2,1,0:T(8,128)(2,1)}), bf16[16,16,512]{2,1,0:T(8,128)(2,1)S(1)}, u32[]{:S(2)}, u32[]{:S(2)}) async-start(bf16[16,16,512]{2,1,0:T(8,128)(2,1)} %bitcast.14), calls=%async_computation | async-start | bytes 524288 | tf_op jit(solution)/shard_map/all_to_all | solution.py:516
  58.4 0.0 copy-done.27
  58.4 0.1 copy.15.skip
  58.5 8.4 %all-to-all-done.arrived = bf16[16,16,512]{2,1,0:T(8,128)(2,1)S(1)} async-done(((bf16[16,16,512]{2,1,0:T(8,128)(2,1)}), bf16[16,16,512]{2,1,0:T(8,128)(2,1)S(1)}, u32[]{:S(2)}, u32[]{:S(2)}) %all-to-all-start) | async-done | bytes 262176 | tf_op jit(solution)/shard_map/all_to_all | solution.py:516
  66.9 0.9 relay.1
  67.8 3.7 %all-to-all-start.1 = ((bf16[16,16,384]{2,1,0:T(8,128)(2,1)}), bf16[16,16,384]{2,1,0:T(8,128)(2,1)S(1)}, u32[]{:S(2)}, u32[]{:S(2)}) async-start(bf16[16,16,384]{2,1,0:T(8,128)(2,1)} %relay.1), calls=%async_computation.1 | async-start | bytes 393216 | tf_op jit(solution)/shard_map/all_to_all | solution.py:518
  71.6 0.0 copy-start.6
  71.6 1.9 %copy-done.6 = bf16[1024,1536]{1,0:T(8,128)(2,1)S(1)} copy-done((bf16[1024,1536]{1,0:T(8,128)(2,1)S(1)}, bf16[1024,1536]{1,0:T(8,128)(2,1)}, u32[]{:S(2)}) %copy-start.6) | copy-done | bytes 3145752
  73.5 0.9 copy-done.11
  74.4 1.9 %copy-done.19 = bf16[1024,1536]{1,0:T(8,128)(2,1)S(1)} copy-done((bf16[1024,1536]{1,0:T(8,128)(2,1)S(1)}, bf16[1024,1536]{1,0:T(8,128)(2,1)}, u32[]{:S(2)}) %copy-start.19) | copy-done | bytes 3145752
  76.3 0.9 copy-done.24
  77.2 0.9 copy-done.26
  78.1 11.2 %scan.1 = bf16[1024,1536]{1,0:T(8,128)(2,1)S(1)} custom-call(bf16[1024,1536]{1,0:T(8,128)(2,1)S(1)} %copy-done.19, bf16[1024,128]{1,0:T(8,128)(2,1)S(1)} %copy-done.11, f32[24,1024]{1,0:T(8,128)S(1)} %copy-done.24, f32[24,1024]{1,0:T(8,128)S(1)} %copy-done.26, bf16[1024,1536]{1,0:T(8,128)(2,1)S(1)} %copy-done.6, f32[24,1]{1,0:T(8,128)S(1)} %copy.15.skip), custom_call_target="tpu_custom_call" | custom-call | flops 4294967296 | bytes 10485760 | tf_op jit(solution)/shard_map/scan/pallas_call | solution.py:342
  89.3 0.0 copy-start.8
  89.3 1.7 copy-done.8
  91.0 0.0 all-to-all-done.1.entering
  91.0 0.0 copy-done.3
  91.0 0.0 copy-done.16
  91.0 0.0 copy-start.1
  91.0 2.3 %copy-done.1 = bf16[1,1536,1536]{2,1,0:T(8,128)(2,1)S(1)} copy-done((bf16[1,1536,1536]{2,1,0:T(8,128)(2,1)S(1)}, bf16[1,1536,1536]{2,1,0:T(8,128)(2,1)}, u32[]{:S(2)}) %copy-start.1) | copy-done | bytes 4718616
  93.3 1.9 %copy-done.7 = bf16[1024,1536]{1,0:T(8,128)(2,1)S(1)} copy-done((bf16[1024,1536]{1,0:T(8,128)(2,1)S(1)}, bf16[1024,1536]{1,0:T(8,128)(2,1)}, u32[]{:S(2)}) %copy-start.7) | copy-done | bytes 3145752
  95.2 1.9 %copy-done.9 = bf16[1024,1536]{1,0:T(8,128)(2,1)S(1)} copy-done((bf16[1024,1536]{1,0:T(8,128)(2,1)S(1)}, bf16[1024,1536]{1,0:T(8,128)(2,1)}, u32[]{:S(2)}) %copy-start.9) | copy-done | bytes 3145752
  97.1 0.9 copy-done.12
  98.0 8.9 %finish.1 = (bf16[8,128,1536]{2,1,0:T(8,128)(2,1)S(1)}, bf16[1024,768]{1,0:T(8,128)(2,1)S(1)}) custom-call(bf16[8,128,1536]{2,1,0:T(8,128)(2,1)S(1)} %bitcast.40, bf16[8,128,1536]{2,1,0:T(8,128)(2,1)S(1)} %bitcast.39, bf16[8,128,128]{2,1,0:T(8,128)(2,1)S(1)} %bitcast.41, f32[24,1024]{1,0:T(8,128)S(1)} %get-tuple-element.27.band_decay, ...), custom_call_target="tpu_custom_call" | custom-call | flops 2415919104 | bytes 16777216 | tf_op jit(solution)/shard_map/finish/pallas_call | solution.py:424
  107.0 0.0 copy-start.20
  107.0 4.3 %rest.1 = bf16[1024,768]{1,0:T(8,128)(2,1)S(1)} custom-call(bf16[8,128,1536]{2,1,0:T(8,128)(2,1)S(1)} %get-tuple-element.30.hidden, bf16[8,128,1536]{2,1,0:T(8,128)(2,1)S(1)} %bitcast.37, bf16[1536,1536]{1,0:T(8,128)(2,1)S(1)} %bitcast.34), custom_call_target="tpu_custom_call" | custom-call | flops 1048576 | bytes 1048576 | tf_op jit(solution)/shard_map/rest/pallas_call | solution.py:466
  111.2 0.0 copy-done.20
  111.2 0.0 copy-start.4
  111.3 1.1 copy-done.4
  112.4 7.2 %all-to-all-start.3 = ((bf16[16,64,768]{2,1,0:T(8,128)(2,1)}), bf16[16,64,768]{2,1,0:T(8,128)(2,1)S(1)}, u32[]{:S(2)}, u32[]{:S(2)}) async-start(bf16[16,64,768]{2,1,0:T(8,128)(2,1)} %bitcast.38), calls=%async_computation.3 | async-start | bytes 3145728 | tf_op jit(solution)/shard_map/all_to_all | solution.py:525
  119.7 0.0 collective-permute-start.2
  119.7 20.7 %all-to-all-done.3 = bf16[16,64,768]{2,1,0:T(8,128)(2,1)S(1)} async-done(((bf16[16,64,768]{2,1,0:T(8,128)(2,1)}), bf16[16,64,768]{2,1,0:T(8,128)(2,1)S(1)}, u32[]{:S(2)}, u32[]{:S(2)}) %all-to-all-start.3) | async-done | bytes 1572896 | tf_op jit(solution)/shard_map/all_to_all | solution.py:525
  140.4 0.0 collective-permute-start.3
  140.4 0.4 collective-permute-done.2
  140.8 7.2 %all-to-all-start.2 = ((bf16[16,64,768]{2,1,0:T(8,128)(2,1)}), bf16[16,64,768]{2,1,0:T(8,128)(2,1)S(1)}, u32[]{:S(2)}, u32[]{:S(2)}) async-start(bf16[16,64,768]{2,1,0:T(8,128)(2,1)} %collective-permute-done.2), calls=%async_computation.2 | async-start | bytes 3145728 | tf_op jit(solution)/shard_map/all_to_all | solution.py:526
  148.0 13.5 %collective-permute-done.3 = bf16[16,64,768]{2,1,0:T(8,128)(2,1)} collective-permute-done((bf16[16,64,768]{2,1,0:T(8,128)(2,1)S(1)}, bf16[16,64,768]{2,1,0:T(8,128)(2,1)}, u32[]{:S(2)}, u32[]{:S(2)}) %collective-permute-start.3) | collective-permute-done | bytes 1572896 | tf_op jit(solution)/shard_map/ppermute | solution.py:527
  161.6 8.0 %all-to-all-done.2 = bf16[16,64,768]{2,1,0:T(8,128)(2,1)S(1)} async-done(((bf16[16,64,768]{2,1,0:T(8,128)(2,1)}), bf16[16,64,768]{2,1,0:T(8,128)(2,1)S(1)}, u32[]{:S(2)}, u32[]{:S(2)}) %all-to-all-start.2) | async-done | bytes 1572896 | tf_op jit(solution)/shard_map/all_to_all | solution.py:526
  169.5 3.4 %copy_bitcast_fusion = bf16[1,8,128,1536]{3,2,1,0:T(8,128)(2,1)} fusion(bf16[16,64,768]{2,1,0:T(8,128)(2,1)} %collective-permute-done.3, bf16[16,64,768]{2,1,0:T(8,128)(2,1)S(1)} %all-to-all-done.2), kind=kLoop, calls=%fused_computation.1 | loop fusion | flops 6291456 | bytes 6291456 | tf_op jit(solution)/shard_map/reshape | solution.py:530
  (19 shorter events, 0.0 us)
Async XLA Ops:
  1.2 31.0 %collective-permute-start.1 = (bf16[128,1536]{1,0:T(8,128)(2,1)S(1)}, bf16[128,1536]{1,0:T(8,128)(2,1)S(1)}, u32[]{:S(2)}, u32[]{:S(2)}) collective-permute-start(bf16[128,1536]{1,0:T(8,128)(2,1)S(1)} %get-tuple-element.31), channel_id=1, source_target_pairs={{1,0},{2,1},{3,2},{4,3},{5,4},{6,5},{7,6},{8,7},{9,8},{10,9},{11,1... | collective-permute-start | bytes 1179656 | tf_op jit(solution)/shard_map/ppermute | solution.py:502
  2.5 29.7 %collective-permute-start = (bf16[128,1536]{1,0:T(8,128)(2,1)S(1)}, bf16[128,1536]{1,0:T(8,128)(2,1)S(1)}, u32[]{:S(2)}, u32[]{:S(2)}) collective-permute-start(bf16[128,1536]{1,0:T(8,128)(2,1)S(1)} %get-tuple-element.32), channel_id=1, source_target_pairs={{0,1},{1,2},{2,3},{3,4},{4,5},{5,6},{6,7},{7,8},{8,9},{9,10},{10,1... | collective-permute-start | bytes 1179656 | tf_op jit(solution)/shard_map/ppermute | solution.py:501
  8.5 2.4 %copy-start = (bf16[1,1536,1664]{2,1,0:T(8,128)(2,1)S(1)}, bf16[1,1536,1664]{2,1,0:T(8,128)(2,1)}, u32[]{:S(2)}) copy-start(bf16[1,1536,1664]{2,1,0:T(8,128)(2,1)} %param.14) | copy-start | bytes 15335428
  11.0 1.9 %copy-start.2 = (bf16[1,8,128,1536]{3,2,1,0:T(8,128)(2,1)S(1)}, bf16[1,8,128,1536]{3,2,1,0:T(8,128)(2,1)}, u32[]{:S(2)}) copy-start(bf16[1,8,128,1536]{3,2,1,0:T(8,128)(2,1)} %param.12) | copy-start | bytes 9437188
  12.9 0.7 copy-start.15
  13.5 2.3 %copy-start.17 = (bf16[1,1536,1536]{2,1,0:T(8,128)(2,1)S(1)}, bf16[1,1536,1536]{2,1,0:T(8,128)(2,1)}, u32[]{:S(2)}) copy-start(bf16[1,1536,1536]{2,1,0:T(8,128)(2,1)} %param.15) | copy-start | bytes 14155780
  15.9 0.9 copy-start.22
  16.8 15.4 %copy-start.13 = (f32[1,9,1664]{2,0,1:T(1,128)S(1)}, f32[1,9,1664]{2,0,1:T(1,128)}, u32[]{:S(2)}) copy-start(f32[1,9,1664]{2,0,1:T(1,128)} %param.19) | copy-start | bytes 179716
  16.8 15.4 %copy-start.14 = (f32[1,1664]{1,0:T(1,128)S(1)}, f32[1,1664]{1,0:T(1,128)}, u32[]{:S(2)}) copy-start(f32[1,1664]{1,0:T(1,128)} %bias_bc.1) | copy-start | bytes 19972
  32.2 13.8 %copy-start.5 = (bf16[1024,1536]{1,0:T(8,128)(2,1)}, bf16[1024,1536]{1,0:T(8,128)(2,1)S(1)}, u32[]{:S(2)}) copy-start(bf16[1024,1536]{1,0:T(8,128)(2,1)S(1)} %get-tuple-element.26.gate) | copy-start | bytes 9437188
  32.2 13.8 %copy-start.23 = (f32[24,1024]{1,0:T(8,128)}, f32[24,1024]{1,0:T(8,128)S(1)}, u32[]{:S(2)}) copy-start(f32[24,1024]{1,0:T(8,128)S(1)} %get-tuple-element.24.cum) | copy-start | bytes 294916
  32.2 13.8 %copy-start.25 = (f32[24,1024]{1,0:T(8,128)}, f32[24,1024]{1,0:T(8,128)S(1)}, u32[]{:S(2)}) copy-start(f32[24,1024]{1,0:T(8,128)S(1)} %get-tuple-element.25.dt) | copy-start | bytes 294916
  32.2 26.2 %copy-start.27 = (f32[1,24]{1,0:T(1,128)S(1)}, f32[1,24]{1,0:T(1,128)}, u32[]{:S(2)}) copy-start(f32[1,24]{1,0:T(1,128)} %param.21) | copy-start | bytes 292
  46.0 0.7 copy-start.10
  46.7 1.7 copy-start.18
  48.4 18.6 %all-to-all-start = ((bf16[16,16,512]{2,1,0:T(8,128)(2,1)}), bf16[16,16,512]{2,1,0:T(8,128)(2,1)S(1)}, u32[]{:S(2)}, u32[]{:S(2)}) async-start(bf16[16,16,512]{2,1,0:T(8,128)(2,1)} %bitcast.14), calls=%async_computation | async-start | bytes 524288 | tf_op jit(solution)/shard_map/all_to_all | solution.py:516
  67.8 23.1 %all-to-all-start.1 = ((bf16[16,16,384]{2,1,0:T(8,128)(2,1)}), bf16[16,16,384]{2,1,0:T(8,128)(2,1)S(1)}, u32[]{:S(2)}, u32[]{:S(2)}) async-start(bf16[16,16,384]{2,1,0:T(8,128)(2,1)} %relay.1), calls=%async_computation.1 | async-start | bytes 393216 | tf_op jit(solution)/shard_map/all_to_all | solution.py:518
  71.6 1.9 %copy-start.6 = (bf16[1024,1536]{1,0:T(8,128)(2,1)S(1)}, bf16[1024,1536]{1,0:T(8,128)(2,1)}, u32[]{:S(2)}) copy-start(bf16[1024,1536]{1,0:T(8,128)(2,1)} %copy-done.5) | copy-start | bytes 9437188
  73.4 0.9 copy-start.11
  74.4 1.9 %copy-start.19 = (bf16[1024,1536]{1,0:T(8,128)(2,1)S(1)}, bf16[1024,1536]{1,0:T(8,128)(2,1)}, u32[]{:S(2)}) copy-start(bf16[1024,1536]{1,0:T(8,128)(2,1)} %copy-done.18) | copy-start | bytes 9437188
  76.3 0.9 copy-start.24
  77.2 0.9 copy-start.26
  78.1 12.9 %copy-start.3 = (bf16[1,8,128,1536]{3,2,1,0:T(8,128)(2,1)S(1)}, bf16[1,8,128,1536]{3,2,1,0:T(8,128)(2,1)}, u32[]{:S(2)}) copy-start(bf16[1,8,128,1536]{3,2,1,0:T(8,128)(2,1)} %param.12) | copy-start | bytes 9437188
  78.1 12.9 %copy-start.16 = (f32[1,1536]{1,0:T(1,128)S(1)}, f32[1,1536]{1,0:T(1,128)}, u32[]{:S(2)}) copy-start(f32[1,1536]{1,0:T(1,128)} %gain.5) | copy-start | bytes 18436
  89.3 1.7 copy-start.8
  91.0 2.3 %copy-start.1 = (bf16[1,1536,1536]{2,1,0:T(8,128)(2,1)S(1)}, bf16[1,1536,1536]{2,1,0:T(8,128)(2,1)}, u32[]{:S(2)}) copy-start(bf16[1,1536,1536]{2,1,0:T(8,128)(2,1)} %param.23) | copy-start | bytes 14155780
  93.3 1.9 %copy-start.7 = (bf16[1024,1536]{1,0:T(8,128)(2,1)S(1)}, bf16[1024,1536]{1,0:T(8,128)(2,1)}, u32[]{:S(2)}) copy-start(bf16[1024,1536]{1,0:T(8,128)(2,1)} %copy-done.5) | copy-start | bytes 9437188
  95.2 1.9 %copy-start.9 = (bf16[1024,1536]{1,0:T(8,128)(2,1)S(1)}, bf16[1024,1536]{1,0:T(8,128)(2,1)}, u32[]{:S(2)}) copy-start(bf16[1024,1536]{1,0:T(8,128)(2,1)} %copy-done.8) | copy-start | bytes 9437188
  97.1 0.9 copy-start.12
  107.0 4.3 %copy-start.20 = (bf16[1024,768]{1,0:T(8,128)(2,1)}, bf16[1024,768]{1,0:T(8,128)(2,1)S(1)}, u32[]{:S(2)}) copy-start(bf16[1024,768]{1,0:T(8,128)(2,1)S(1)} %get-tuple-element.29) | copy-start | bytes 4718596
  111.2 1.1 copy-start.4
  112.4 7.3 %copy-start.21 = (bf16[1024,768]{1,0:T(8,128)(2,1)S(1)}, bf16[1024,768]{1,0:T(8,128)(2,1)}, u32[]{:S(2)}) copy-start(bf16[1024,768]{1,0:T(8,128)(2,1)} %copy-done.20) | copy-start | bytes 4718596
  112.4 28.0 %all-to-all-start.3 = ((bf16[16,64,768]{2,1,0:T(8,128)(2,1)}), bf16[16,64,768]{2,1,0:T(8,128)(2,1)S(1)}, u32[]{:S(2)}, u32[]{:S(2)}) async-start(bf16[16,64,768]{2,1,0:T(8,128)(2,1)} %bitcast.38), calls=%async_computation.3 | async-start | bytes 3145728 | tf_op jit(solution)/shard_map/all_to_all | solution.py:525
  119.7 21.2 %collective-permute-start.2 = (bf16[16,64,768]{2,1,0:T(8,128)(2,1)S(1)}, bf16[16,64,768]{2,1,0:T(8,128)(2,1)}, u32[]{:S(2)}, u32[]{:S(2)}) collective-permute-start(bf16[16,64,768]{2,1,0:T(8,128)(2,1)S(1)} %bitcast.45), channel_id=1, source_target_pairs={{0,16},{16,32},{32,48},{48,64},{64,80},{80,96},{96,112},{112,0},{1... | collective-permute-start | bytes 4718600 | tf_op jit(solution)/shard_map/ppermute | solution.py:524
  140.4 21.2 %collective-permute-start.3 = (bf16[16,64,768]{2,1,0:T(8,128)(2,1)S(1)}, bf16[16,64,768]{2,1,0:T(8,128)(2,1)}, u32[]{:S(2)}, u32[]{:S(2)}) collective-permute-start(bf16[16,64,768]{2,1,0:T(8,128)(2,1)S(1)} %all-to-all-done.3), channel_id=1, source_target_pairs={{0,16},{16,32},{32,48},{48,64},{64,80},{80,96},{96,112},{112,0},{1... | collective-permute-start | bytes 4718600 | tf_op jit(solution)/shard_map/ppermute | solution.py:527
  140.8 28.7 %all-to-all-start.2 = ((bf16[16,64,768]{2,1,0:T(8,128)(2,1)}), bf16[16,64,768]{2,1,0:T(8,128)(2,1)S(1)}, u32[]{:S(2)}, u32[]{:S(2)}) async-start(bf16[16,64,768]{2,1,0:T(8,128)(2,1)} %collective-permute-done.2), calls=%async_computation.2 | async-start | bytes 3145728 | tf_op jit(solution)/shard_map/all_to_all | solution.py:526

commit v3 on v2

v3 whole, which is shorter than its diff:
```python
import functools

import jax
import jax.numpy as jnp
from jax import lax
from jax.experimental import pallas as pl
from jax.experimental.pallas import tpu as pltpu
from jax.sharding import PartitionSpec as P

EPSILON = 1e-05
ROWS = 8
LINE = 128
LENGTH = ROWS * LINE
HEADS = 24
WIDTH = 64
STATE = 64
INNER = HEADS * WIDTH
D = 1536
HALF = D // 2
GROUP = 384
GROUP_HEADS = GROUP // WIDTH
BANDS = 16
F32 = jnp.float32
BF16 = jnp.bfloat16
MIB = 1 << 20
LOG2E = 1.4426950408889634


def params():
    return pltpu.CompilerParams(dimension_semantics=("arbitrary",), vmem_limit_bytes=60 * MIB)


def upright(row):
    return jnp.broadcast_to(row, (LINE, HEADS)).T[:, :1]


def whole(*shape):
    return pl.BlockSpec(shape, lambda i: (0,) * len(shape), pipeline_mode=pl.Buffered(1))


def dot(a, b):
    return jnp.dot(a, b, preferred_element_type=F32)


def rms(values, gain):
    return values * lax.rsqrt(jnp.mean(values * values, -1, keepdims=True) + EPSILON) * gain


def silu(v):
    half = 0.5 * v
    return half + half * jnp.tanh(half)


def head_spread(channels, first):
    head = lax.broadcasted_iota(jnp.int32, (2 * HEADS, channels), 0)
    head = jnp.where(head < HEADS, head, head - HEADS)
    channel = lax.broadcasted_iota(jnp.int32, (2 * HEADS, channels), 1)
    return jnp.where(head - first == channel // WIDTH, 1.0, 0.0).astype(BF16)


def two_terms(values_t):
    high = values_t.astype(BF16).astype(F32)
    return jnp.concatenate([high, values_t - high], axis=0).T.astype(BF16)


def place(r):
    return (r + 1) % ROWS * LINE


def fill(padded, tile, slot, line):
    padded[tile, slot, pl.ds(8, LINE), :] = line.astype(F32)


def convolved(padded, tile, slot, taps, bias):
    total = bias
    for i in range(3):
        for j in range(3):
            total = total + padded[tile, slot - 1 + i, pl.ds(7 + j, LINE), :] * taps[3 * i + j]
    return silu(total).astype(BF16)


def lanes(refs, k):
    return [ref[:, k * 128 : (k + 1) * 128] for ref in refs]


def project_kernel(
    tok,
    gain,
    w_x,
    w_g,
    w_bc,
    w_dt,
    dt_bias,
    rate,
    taps_x,
    taps_bc,
    bias_x,
    bias_bc,
    x,
    gate,
    rim,
    bcs,
    rim_bc,
    cum,
    dt,
    band_tail,
    band_decay,
    total,
    mid,
    normed,
    lines_a,
    lines_b,
    lines_bc,
    x_keep,
    b_t,
    tails,
    tok_here,
    w_g_here,
    tok_sem,
    w_g_sem,
):
    step = pl.program_id(0)

    def tokens_in(m):
        part = pl.ds(m * 256, 256)
        return pltpu.make_async_copy(tok.at[part, :], tok_here.at[part, :], tok_sem.at[m])

    def gate_in(n):
        return pltpu.make_async_copy(w_g.at[:, pl.ds(n * 512, 512)], w_g_here.at[n], w_g_sem.at[n])

    def store(m, values, padded, out, tiles):
        for n in range(m * 2, m * 2 + 2):
            line = values[(n - m * 2) * LINE : (n - m * 2 + 1) * LINE]
            for k in range(tiles):
                fill(padded, k, n, line[:, k * 128 : (k + 1) * 128])
            if n in (0, 1, 6, 7):
                out[pl.ds((n if n < 2 else n - 4) * LINE, LINE), :] = line

    def multiply_x(m, padded):
        here = normed[pl.ds(m * 256, 256), :]
        store(m, dot(here, w_x[...]).astype(BF16), padded, rim, 4)

    def multiply_gate(m, n):
        part = pl.ds(m * 256, 256)
        gate[part, :] = silu(dot(normed[part, :], w_g_here[n])).astype(BF16)

    def inside(k, padded, chunk):
        taps, bias = lanes([taps_x[n] for n in range(9)], k), bias_x[:, k * 128 : (k + 1) * 128]
        for r in range(1, ROWS - 1):
            values = convolved(padded, k, r, taps, bias)
            x[pl.ds(place(r), LINE), pl.ds(k * 128, 128)] = values
            x_keep[pl.ds((r - 1) * LINE, LINE), pl.ds(chunk * 512 + k * 128, 128)] = values

    def add_state(piece):
        part = pl.ds(piece * 256, 256)
        spread = head_spread(256, piece * 4)
        weighted = x_keep[:, part].astype(F32) * dot(tails[...], spread)
        mid[:, part] = dot(b_t[pl.ds(0, STATE), :], weighted.astype(BF16))

    @pl.when(step == 0)
    def _():
        for m in range(4):
            tokens_in(m).start()
        for padded in (lines_a, lines_b, lines_bc):
            for n in range(ROWS):
                for k in range(padded.shape[0]):
                    padded[k, n, pl.ds(0, 8), :] = jnp.zeros((8, 128), F32)
                    padded[k, n, pl.ds(LINE + 8, 8), :] = jnp.zeros((8, 128), F32)
        for m in range(4):
            tokens_in(m).wait()
            part = pl.ds(m * 256, 256)
            here = rms(tok_here[part, :].astype(F32), gain[...]).astype(BF16)
            normed[part, :] = here
            store(m, dot(here, w_bc[...]).astype(BF16), lines_bc, rim_bc, 1)
            store(m, dot(here, w_x[...]).astype(BF16), lines_a, rim, 4)
        for n in range(3):
            gate_in(n).start()

    @pl.when(step == 1)
    def _():
        taps = [taps_bc[n] for n in range(9)]
        for r in range(1, ROWS - 1):
            values = convolved(lines_bc, 0, r, taps, bias_bc[...])
            bcs[pl.ds(place(r), LINE), :] = values
            b_t[:, pl.ds((r - 1) * LINE, LINE)] = values.astype(F32).T.astype(BF16)
        raw = lax.dot_general(
            w_dt[...], normed[...], (((1,), (1,)), ((), ())), preferred_element_type=F32
        ) + upright(dt_bias[...])
        dt[...] = jnp.maximum(raw, 0.0) + jnp.log1p(jnp.exp(-jnp.abs(raw)))
        for m in range(4):
            multiply_x(m, lines_b)
            inside(m, lines_a, 0)

    @pl.when(step == 2)
    def _():
        steps = dt[...]
        log_decay = -upright(rate[...]) * steps
        i = lax.broadcasted_iota(jnp.int32, (LINE, LINE), 0)
        j = lax.broadcasted_iota(jnp.int32, (LINE, LINE), 1)
        sums = jnp.dot(
            jnp.concatenate([log_decay[:, r * LINE : (r + 1) * LINE] for r in range(ROWS)], axis=0),
            jnp.where(i <= j, 1.0, 0.0).astype(F32),
            precision=lax.Precision.HIGHEST,
            preferred_element_type=F32,
        )
        lines = [sums[r * HEADS : (r + 1) * HEADS] for r in range(ROWS)]
        ends = [line[:, LINE - 1 :] for line in lines]
        before = [jnp.zeros_like(ends[0])]
        after = [jnp.zeros_like(ends[0])]
        for r in range(ROWS - 1):
            before.append(before[-1] + ends[r])
            after.append(after[-1] + ends[ROWS - 1 - r])
        for r in range(ROWS):
            part = slice(r * LINE, (r + 1) * LINE)
            cum[:, part] = lines[r]
            band_decay[:, part] = jnp.exp(lines[r] + before[r])
            tail = steps[:, part] * jnp.exp((ends[r] - lines[r]) + after[ROWS - 1 - r])
            band_tail[:, part] = tail
            if 0 < r < ROWS - 1:
                tails[pl.ds((r - 1) * LINE, LINE), :] = two_terms(tail)
        total[...] = jnp.broadcast_to(before[-1] + ends[-1], (HEADS, LINE)).T[:1]
        for m in range(4):
            multiply_x(m, lines_a)
            inside(m, lines_b, 1)

    @pl.when(step == 3)
    def _():
        gate_in(0).wait()
        for m in range(4):
            multiply_gate(m, 0)
            inside(m, lines_a, 2)

    for late in (4, 5):

        @pl.when(step == late)
        def _():
            gate_in(late - 3).wait()
            for m in range(4):
                multiply_gate(m, late - 3)
                if m < 3:
                    add_state((late - 4) * 3 + m)


def project(tok, gain, w_xbc, w_gate, w_dt_t, dt_bias, rate, taps, conv_bias):
    per_head = jax.ShapeDtypeStruct((HEADS, LENGTH), F32)
    first = lambda i: (0, jnp.minimum(i, 2))
    second = lambda i: (0, jnp.maximum(i - 3, 0))
    behind = lambda i: jnp.clip(i - 1, 0, 2)
    last = INNER // 128
    return pl.pallas_call(
        project_kernel,
        grid=(6,),
        in_specs=[
            pl.BlockSpec(memory_space=pl.ANY),
            whole(1, D),
            pl.BlockSpec((D, 512), first),
            pl.BlockSpec(memory_space=pl.ANY),
            pl.BlockSpec((D, 128), lambda i: (0, last), pipeline_mode=pl.Buffered(1)),
            whole(HEADS, D),
            whole(1, HEADS),
            whole(1, HEADS),
            pl.BlockSpec((9, 1, 512), lambda i: (0, 0, behind(i))),
            pl.BlockSpec((9, 1, 128), lambda i: (0, 0, last)),
            pl.BlockSpec((1, 512), lambda i: (0, behind(i))),
            pl.BlockSpec((1, 128), lambda i: (0, last)),
        ],
        out_specs=[
            pl.BlockSpec((LENGTH, 512), lambda i: (0, behind(i))),
            pl.BlockSpec((LENGTH, 512), second),
            pl.BlockSpec((4 * LINE, 512), first),
            whole(LENGTH, 128),
            whole(4 * LINE, 128),
            whole(HEADS, LENGTH),
            whole(HEADS, LENGTH),
            whole(HEADS, LENGTH),
            whole(HEADS, LENGTH),
            whole(1, HEADS),
            whole(STATE, INNER),
        ],
        out_shape=[
            jax.ShapeDtypeStruct((LENGTH, INNER), BF16),
            jax.ShapeDtypeStruct((LENGTH, INNER), BF16),
            jax.ShapeDtypeStruct((4 * LINE, INNER), BF16),
            jax.ShapeDtypeStruct((LENGTH, 128), BF16),
            jax.ShapeDtypeStruct((4 * LINE, 128), BF16),
            per_head,
            per_head,
            per_head,
            per_head,
            jax.ShapeDtypeStruct((1, HEADS), F32),
            jax.ShapeDtypeStruct((STATE, INNER), F32),
        ],
        scratch_shapes=[
            pltpu.VMEM((LENGTH, D), BF16),
            pltpu.VMEM((4, ROWS, LINE + 16, 128), F32),
            pltpu.VMEM((4, ROWS, LINE + 16, 128), F32),
            pltpu.VMEM((1, ROWS, LINE + 16, 128), F32),
            pltpu.VMEM(((ROWS - 2) * LINE, INNER), BF16),
            pltpu.VMEM((128, (ROWS - 2) * LINE), BF16),
            pltpu.VMEM(((ROWS - 2) * LINE, 2 * HEADS), BF16),
            pltpu.VMEM((LENGTH, D), BF16),
            pltpu.VMEM((3, D, 512), BF16),
            pltpu.SemaphoreType.DMA((4,)),
            pltpu.SemaphoreType.DMA((3,)),
        ],
        compiler_params=params(),
        cost_estimate=pl.CostEstimate(
            flops=2 * LENGTH * D * 3224, bytes_accessed=20 << 20, transcendentals=LENGTH * INNER
        ),
        name="project",
    )(tok, gain, w_xbc, w_gate, w_xbc, w_dt_t, dt_bias, rate, taps, taps, conv_bias, conv_bias)


def edge_kernel(
    top,
    bottom,
    gain,
    w_x,
    w_bc,
    rim,
    rim_bc,
    taps_x,
    taps_bc,
    bias_x,
    bias_bc,
    band_tail,
    total,
    mid,
    x_in,
    bcs_in,
    x,
    bcs,
    pieces,
    edge,
    lines,
    b_t,
    tails,
):
    del x_in, bcs_in
    g = pl.program_id(0)

    def both(side, own, taps, bias, out, tiles):
        for k in range(tiles):
            part = slice(k * 128, (k + 1) * 128)
            for slot, line in enumerate(
                [side[:LINE], own[pl.ds(0, LINE), :], own[pl.ds(LINE, LINE), :]]
                + [own[pl.ds(2 * LINE, LINE), :], own[pl.ds(3 * LINE, LINE), :], side[LINE:]]
            ):
                fill(lines, k, slot, line[:, part])
            for slot, r in ((1, 0), (4, ROWS - 1)):
                out[pl.ds(place(r), LINE), part] = convolved(lines, k, slot, lanes(taps, k), bias[:, part])

    @pl.when(g == 0)
    def _():
        for slot in range(6):
            for k in range(GROUP // 128):
                lines[k, slot, pl.ds(0, 8), :] = jnp.zeros((8, 128), F32)
                lines[k, slot, pl.ds(LINE + 8, 8), :] = jnp.zeros((8, 128), F32)
        edge[pl.ds(0, LINE), :] = rms(top[...].astype(F32), gain[...]).astype(BF16)
        edge[pl.ds(LINE, LINE), :] = rms(bottom[...].astype(F32), gain[...]).astype(BF16)
        both(
            dot(edge[...], w_bc[...]).astype(BF16),
            rim_bc,
            [taps_bc[k] for k in range(9)],
            bias_bc[...],
            bcs,
            1,
        )
        b_t[...] = bcs[...].astype(F32).T.astype(BF16)
        tails[pl.ds(place(0), LINE), :] = two_terms(band_tail[:, :LINE])
        tails[pl.ds(place(ROWS - 1), LINE), :] = two_terms(band_tail[:, LENGTH - LINE :])

    both(
        dot(edge[...], w_x[...]).astype(BF16),
        rim,
        [taps_x[k] for k in range(9)],
        bias_x[...],
        x,
        GROUP // 128,
    )
    weighted = x[...].astype(F32) * dot(tails[...], head_spread(GROUP, g * GROUP_HEADS))
    state = mid[...] + dot(b_t[pl.ds(0, STATE), :], weighted.astype(BF16))
    head = lax.broadcasted_iota(jnp.int32, (HEADS, 128), 0)
    lane = lax.broadcasted_iota(jnp.int32, (HEADS, 128), 1)
    pick = jnp.where(head == lane + g * GROUP_HEADS, 1.0, 0.0).astype(BF16)
    first = total[...].astype(BF16)
    rest = total[...] - first.astype(F32)
    second = rest.astype(BF16)
    third = (rest - second.astype(F32)).astype(BF16)
    terms = jnp.concatenate(
        [dot(jnp.broadcast_to(t, (8, HEADS)), pick)[:1] for t in (first, second, third)]
        + [jnp.zeros((13, 128), F32)],
        axis=0,
    ).astype(BF16)
    for a in range(4):
        pieces[a, 0, :, pl.ds(0, GROUP)] = state[16 * a : 16 * a + 16].astype(BF16)
        pieces[a, 0, :, pl.ds(GROUP, 128)] = terms


def edges(top, bottom, gain, w_xbc, rim, rim_bc, taps, conv_bias, band_tail, total, mid, x, bcs):
    last = INNER // 128
    return pl.pallas_call(
        edge_kernel,
        grid=(4,),
        in_specs=[
            whole(LINE, D),
            whole(LINE, D),
            whole(1, D),
            pl.BlockSpec((D, GROUP), lambda i: (0, i)),
            pl.BlockSpec((D, 128), lambda i: (0, last), pipeline_mode=pl.Buffered(1)),
            pl.BlockSpec((4 * LINE, GROUP), lambda i: (0, i)),
            whole(4 * LINE, 128),
            pl.BlockSpec((9, 1, GROUP), lambda i: (0, 0, i)),
            pl.BlockSpec((9, 1, 128), lambda i: (0, 0, last)),
            pl.BlockSpec((1, GROUP), lambda i: (0, i)),
            pl.BlockSpec((1, 128), lambda i: (0, last)),
            whole(HEADS, LENGTH),
            whole(1, HEADS),
            pl.BlockSpec((STATE, GROUP), lambda i: (0, i)),
            pl.BlockSpec(memory_space=pl.ANY),
            pl.BlockSpec(memory_space=pl.ANY),
        ],
        out_specs=[
            pl.BlockSpec((2 * LINE, GROUP), lambda i: (0, i)),
            whole(2 * LINE, 128),
            pl.BlockSpec((4, 1, 16, GROUP + 128), lambda i: (0, i, 0, 0)),
        ],
        out_shape=[
            jax.ShapeDtypeStruct((LENGTH, INNER), BF16),
            jax.ShapeDtypeStruct((LENGTH, 128), BF16),
            jax.ShapeDtypeStruct((4, 4, 16, GROUP + 128), BF16),
        ],
        input_output_aliases={14: 0, 15: 1},
        scratch_shapes=[
            pltpu.VMEM((2 * LINE, D), BF16),
            pltpu.VMEM((GROUP // 128, 6, LINE + 16, 128), F32),
            pltpu.VMEM((128, 2 * LINE), BF16),
            pltpu.VMEM((2 * LINE, 2 * HEADS), BF16),
        ],
        compiler_params=params(),
        cost_estimate=pl.CostEstimate(
            flops=2 * 256 * D * 1664 + 10 * LENGTH * 1664,
            bytes_accessed=10 << 20,
            transcendentals=256 * 1664,
        ),
        name="edges",
    )(
        top,
        bottom,
        gain,
        w_xbc,
        w_xbc,
        rim,
        rim_bc,
        taps,
        taps,
        conv_bias,
        conv_bias,
        band_tail,
        total,
        mid,
        x,
        bcs,
    )


def scan_kernel(
    half, x_even, x_odd, bcs, cum, dt, gate, skip, out, direct, state, sums, steps, weights, b_t, c
):
    lane = lax.broadcasted_iota(jnp.int32, (LINE, LINE), 1)
    left = lane < WIDTH

    @pl.when(pl.program_id(0) == 0)
    def _():
        direct[...] = dot(
            two_terms(jnp.broadcast_to(upright(skip[...]), (HEADS, 8))),
            head_spread(HALF, half * HEADS // 2),
        )
        state[...] = jnp.zeros_like(state)
        row = lax.broadcasted_iota(jnp.int32, (LINE, LINE), 0)
        for r in range(ROWS):
            part = slice(r * LINE, (r + 1) * LINE)
            sums[r] = (cum[:, part] * LOG2E).T
            steps[r] = dt[:, part].T
            both = bcs[pl.ds(place(r), LINE), :].astype(F32)
            b_t[r] = both.T.astype(BF16)[:STATE]
            c[r] = pltpu.roll(both, STATE, 1).astype(BF16)[:, :STATE]
        for r in range(ROWS):
            weights[r] = jnp.where(row >= lane, dot(c[r], b_t[r]), 0.0)

    def line(r, x, out_part):
        sums_here, steps_here, weights_here = sums[r], steps[r], weights[r]
        columns_t = pl.ds(pl.multiple_of(r * LINE, LINE), LINE)
        sums_t = cum[:, columns_t] * LOG2E
        steps_t = dt[:, columns_t]

        def mixing(h):
            along = jnp.broadcast_to(sums_here[:, h : h + 1], (LINE, LINE))
            decay = jnp.exp2(jnp.minimum(along - sums_t[h : h + 1], 0.0))
            return along, (decay * (weights_here * steps_t[h : h + 1])).astype(BF16)

        for q in range(HEADS // 8):
            quad = pl.ds(q * 256, 256)
            carried = dot(c[r], state[:, quad].astype(BF16))
            tails, decays = [], []
            for p in (2 * q, 2 * q + 1):
                part = pl.ds(p * 128, 128)
                h = half * HEADS // 2 + 2 * p
                values = x[:, part].astype(F32)
                (along_a, mixing_a), (along_b, mixing_b) = mixing(h), mixing(h + 1)
                columns = jnp.concatenate(
                    [jnp.where(left, values, 0.0), jnp.where(left, 0.0, values)], axis=0
                ).astype(BF16)
                inner = dot(jnp.concatenate([mixing_a, mixing_b], axis=1), columns)
                here = jnp.where(left, along_a, along_b)
                carry = jnp.exp2(here)
                stepped = jnp.where(left, steps_here[:, h : h + 1], steps_here[:, h + 1 : h + 2])
                tails.append((values * stepped * jnp.exp2(here[LINE - 1 :] - here)).astype(BF16))
                decays.append(carry[LINE - 1 :])
                side = slice((p % 2) * 128, (p % 2) * 128 + 128)
                y = inner + carry * carried[:, side] + direct[0:1, part] * values
                out[out_part, part] = (y * gate[out_part, part].astype(F32)).astype(BF16)
            state[:, quad] = jnp.concatenate(decays, axis=1) * state[:, quad] + dot(
                b_t[r], jnp.concatenate(tails, axis=1)
            )

    first = pl.program_id(0) * 2
    line(first, x_even, pl.ds(0, LINE))
    line(first + 1, x_odd, pl.ds(LINE, LINE))


def scan(half, x, bcs, cum, dt, gate, skip):
    return pl.pallas_call(
        functools.partial(scan_kernel, half),
        grid=(ROWS // 2,),
        in_specs=[
            pl.BlockSpec((LINE, HALF), lambda i: ((2 * i + 1) % ROWS, half)),
            pl.BlockSpec((LINE, HALF), lambda i: ((2 * i + 2) % ROWS, half)),
            whole(LENGTH, 128),
            whole(HEADS, LENGTH),
            whole(HEADS, LENGTH),
            pl.BlockSpec((2 * LINE, HALF), lambda i: (i, half)),
            whole(1, HEADS),
        ],
        out_specs=pl.BlockSpec((2 * LINE, HALF), lambda i: (i, 0)),
        out_shape=jax.ShapeDtypeStruct((LENGTH, HALF), BF16),
        scratch_shapes=[
            pltpu.VMEM((8, HALF), F32),
            pltpu.VMEM((STATE, HALF), F32),
            pltpu.VMEM((ROWS, LINE, HEADS), F32),
            pltpu.VMEM((ROWS, LINE, HEADS), F32),
            pltpu.VMEM((ROWS, LINE, LINE), F32),
            pltpu.VMEM((ROWS, STATE, LINE), BF16),
            pltpu.VMEM((ROWS, LINE, STATE), BF16),
        ],
        compiler_params=params(),
        cost_estimate=pl.CostEstimate(
            flops=2 << 30, bytes_accessed=5 << 20, transcendentals=LENGTH * LINE * HEADS // 2
        ),
        name="scan",
    )(x, x, bcs, cum, dt, gate, skip)


def relay_kernel(arrived, out):
    logs = jnp.concatenate(
        [
            jnp.sum(arrived[j, :, pl.ds(GROUP, 128)].astype(F32), axis=0, keepdims=True)
            for j in range(BANDS)
        ],
        axis=0,
    )
    decay = jnp.exp(logs)
    high = decay.astype(BF16)
    low = (decay - high.astype(F32)).astype(BF16)
    lane = lax.broadcasted_iota(jnp.int32, (128, GROUP), 0)
    channel = lax.broadcasted_iota(jnp.int32, (128, GROUP), 1)
    spread = jnp.where(lane == channel // WIDTH, 1.0, 0.0).astype(BF16)
    wide = dot(high, spread) + dot(low, spread)
    state = jnp.zeros((16, GROUP), F32)
    for j in range(BANDS):
        out[j] = state.astype(BF16)
        state = wide[j : j + 1] * state + arrived[j, :, pl.ds(0, GROUP)].astype(F32)


def relay(arrived):
    return pl.pallas_call(
        relay_kernel,
        out_shape=jax.ShapeDtypeStruct((BANDS, 16, GROUP), BF16),
        compiler_params=pltpu.CompilerParams(vmem_limit_bytes=60 * MIB),
        name="relay",
    )(arrived)


def columns_out(values, tokens, turned, out):
    values = values + tokens
    for k in range(HALF // 128):
        part = slice(k * 128, (k + 1) * 128)
        for r in range(ROWS):
            turned[k, pl.ds(r, 32, stride=ROWS), :] = values[r * 32 : (r + 1) * 32, part]
        out[:, part] = turned[k].astype(BF16)


def finish_kernel(
    local_a, local_b, gate, bcs, band_decay, entering, gain, tok, w, hidden, out, spread, state, decays, turned
):
    step = pl.program_id(0)

    @pl.when(step == 0)
    def _():
        spread[...] = head_spread(INNER, 0)
        state[pl.ds(0, STATE), :] = jnp.zeros((STATE, INNER), BF16)
        for a in range(4):
            for g in range(4):
                state[pl.ds(STATE + 16 * a, 16), pl.ds(g * GROUP, GROUP)] = entering[4 * a + g]
        for r in range(ROWS):
            decays[r] = two_terms(band_decay[:, r * LINE : (r + 1) * LINE])

    both = jnp.concatenate([bcs[1:], bcs[:1]], axis=0).reshape(256, 128)
    here = pl.ds(pl.multiple_of(step * 32, 32), 32)
    decay = dot(decays[:, here, :].reshape(256, 2 * HEADS), spread[...])
    local = jnp.concatenate([local_a[...], local_b[...]], axis=2)
    gated = local.reshape(256, INNER).astype(F32) + (
        dot(both, state[...]) * decay * gate[...].reshape(256, INNER).astype(F32)
    )
    normed = rms(gated, gain[...]).astype(BF16)
    hidden[...] = normed.reshape(ROWS, 32, INNER)
    columns_out(dot(normed, w[...]), tok[...].reshape(256, HALF).astype(F32), turned, out)


def finish(local_a, local_b, gate, bcs, band_decay, entering, gain, tok, w_out):
    cells = lambda n: pl.BlockSpec((ROWS, 32, n), lambda i: (0, i, 0))
    return pl.pallas_call(
        finish_kernel,
        grid=(LINE // 32,),
        in_specs=[
            cells(HALF),
            cells(HALF),
            cells(INNER),
            cells(128),
            whole(HEADS, LENGTH),
            whole(BANDS, 16, GROUP),
            whole(1, INNER),
            cells(HALF),
            whole(INNER, HALF),
        ],
        out_specs=[cells(INNER), pl.BlockSpec((256, HALF), lambda i: (i, 0))],
        out_shape=[
            jax.ShapeDtypeStruct((ROWS, LINE, INNER), BF16),
            jax.ShapeDtypeStruct((LENGTH, HALF), BF16),
        ],
        scratch_shapes=[
            pltpu.VMEM((2 * HEADS, INNER), BF16),
            pltpu.VMEM((2 * STATE, INNER), BF16),
            pltpu.VMEM((ROWS, LINE, 2 * HEADS), BF16),
            pltpu.VMEM((HALF // 128, 256, 128), F32),
        ],
        compiler_params=params(),
        cost_estimate=pl.CostEstimate(
            flops=2 * LENGTH * D * HALF, bytes_accessed=16 << 20, transcendentals=LENGTH
        ),
        name="finish",
    )(local_a, local_b, gate, bcs, band_decay, entering, gain, tok, w_out)


def rest_kernel(hidden, tok, w, out, turned):
    columns_out(
        dot(hidden[...].reshape(256, INNER), w[...]),
        tok[...].reshape(256, HALF).astype(F32),
        turned,
        out,
    )


def rest(hidden, tok, w_out):
    return pl.pallas_call(
        rest_kernel,
        grid=(LINE // 32,),
        in_specs=[
            pl.BlockSpec((ROWS, 32, INNER), lambda i: (0, i, 0)),
            pl.BlockSpec((ROWS, 32, HALF), lambda i: (0, i, 1)),
            pl.BlockSpec((INNER, HALF), lambda i: (0, 1), pipeline_mode=pl.Buffered(1)),
        ],
        out_specs=pl.BlockSpec((256, HALF), lambda i: (i, 0)),
        out_shape=jax.ShapeDtypeStruct((LENGTH, HALF), BF16),
        scratch_shapes=[pltpu.VMEM((HALF // 128, 256, 128), F32)],
        compiler_params=params(),
        cost_estimate=pl.CostEstimate(flops=1 << 20, bytes_accessed=1 << 20, transcendentals=0),
        name="rest",
    )(hidden, tok, w_out)


def shards(
    tokens,
    in_gain,
    w_xbc,
    w_gate,
    w_dt,
    dt_bias,
    decay_rate,
    conv_w,
    conv_bias,
    skip,
    out_gain,
    w_out,
):
    bands = lax.axis_size("band")
    segments = lax.axis_size("segment")
    cells = tokens[0]
    tok = cells.reshape(LENGTH, D)
    top = lax.ppermute(cells[ROWS - 1], "band", [(i, i + 1) for i in range(bands - 1)])
    bottom = lax.ppermute(cells[0], "band", [(i + 1, i) for i in range(bands - 1)])

    taps = conv_w.swapaxes(0, 1)
    x, gate, rim, bcs, rim_bc, cum, dt, band_tail, band_decay, total, mid = project(
        tok, in_gain, w_xbc[0], w_gate[0], w_dt[0].T, dt_bias, decay_rate, taps, conv_bias
    )
    x, bcs, pieces = edges(
        top, bottom, in_gain, w_xbc[0], rim, rim_bc, taps, conv_bias, band_tail, total, mid, x, bcs
    )
    swap = functools.partial(
        lax.all_to_all, axis_name="band", split_axis=0, concat_axis=0, tiled=True
    )
    onward = functools.partial(
        lax.ppermute, axis_name="segment", perm=[(i, (i + 1) % segments) for i in range(segments)]
    )
    arrived = swap(pieces.reshape(BANDS, 16, GROUP + 128))
    local_a = scan(0, x, bcs, cum, dt, gate, skip)
    arrived, local_a = lax.optimization_barrier((arrived, local_a))
    states = relay(arrived)
    states, x_b = lax.optimization_barrier((states, x))
    entering = swap(states)
    local_b = scan(1, x_b, bcs, cum, dt, gate, skip)

    grid = lambda a: a.reshape(ROWS, LINE, a.shape[-1])
    hidden, first = finish(
        grid(local_a), grid(local_b), grid(gate), grid(bcs), band_decay, entering, out_gain, cells, w_out[0]
    )
    first = swap(first.reshape(BANDS, LENGTH // BANDS, HALF))
    second = onward(rest(hidden, cells, w_out[0]).reshape(BANDS, LENGTH // BANDS, HALF))
    second = swap(second)
    first = onward(first)
    both = jnp.concatenate([first, second], axis=-1)
    handed = both.reshape(BANDS, LINE // BANDS, ROWS, D).swapaxes(0, 1)
    return handed.reshape(1, LINE // BANDS, BANDS * ROWS, D)


def solution(mesh):
    in_specs = (
        P("segment", "band", None, None),
        P("segment", None),
        P("segment", None, None),
        P("segment", None, None),
        P("segment", None, None),
        P("segment", None),
        P("segment", None),
        P("segment", None, None),
        P("segment", None),
        P("segment", None),
        P("segment", None),
        P("segment", None, None),
    )
    out_specs = P("segment", "band", None, None)
    return jax.shard_map(shards, mesh=mesh, in_specs=in_specs, out_specs=out_specs, check_vma=False)
```

time: 174 us -> 160 us (0.920)
  blocking collectives: 0 us -> 57.6 us
  waiting for transfers between devices: 51 us -> 0.02 us
  local copies, waits for them, and re-layouts: 29.7 us -> 3.46 us
  Pallas kernels: 54.4 us -> 71.9 us
  starting transfers between devices: 34.1 us -> 23.6 us
    all_to_all x0 -> x2, blocking collectives: none -> 57.6 us  [the longest x1 30.5 us: shards(): first = swap(first.reshape(BANDS, LENGTH // BANDS, HALF))]
    all_to_all x3 -> x1, waiting for transfers between devices: 28.7 us -> 0.01 us  [shards(): entering = swap(states)]
    unnamed x56 -> x10, local copies, waits for them, and re-layouts: 27 us -> 2.29 us
    ppermute x2, waiting for transfers between devices: 13.9 us -> 0.01 us  [the longest x1 0.01 us: shards(): onward(rest(hidden, cells, w_out[0]).reshape(BANDS, LENGTH // BANDS, HALF))]
    pallas_call x4 -> x5, Pallas kernels: 49.2 us -> 62.9 us  [the longest x1 24.1 us: project(): pl.pallas_call(project_kernel, grid=(6,), in_specs=[pl.BlockSpec(memory_s...]
    all_to_all x3 -> x1, starting transfers between devices: 18.2 us -> 7.2 us  [shards(): entering = swap(states)]
    all_to_all x1, waiting for transfers between devices: 8.42 us -> 0.01 us  [shards(): arrived = swap(pieces.reshape(BANDS, 16, GROUP + 128))]
    pallas_call x1, Pallas kernels: 4.25 us -> 7.21 us  [rest(): pl.pallas_call(rest_kernel, grid=(LINE // 32,), in_specs=[pl.BlockSpec((R...]
  transfers between devices with their start and end apart: 8 -> 6, of which waited for: 5 -> 0; matrix products, arithmetic and copies ran while one was open for 1% -> 0% of each run, Pallas kernels for 15% -> 27%
where the time goes in v3:
time: 160 us; the launch traced here: 159 us
  Pallas kernels  71.9 us (45%)
  blocking collectives  57.6 us (36%)
  starting transfers between devices  23.6 us (15%)
  local copies, waits for them, and re-layouts  3.46 us (2%)
  other arithmetic  1.95 us (1%)
    all_to_all x1, blocking collectives, shards(): first = swap(first.reshape(BANDS, LENGTH // BANDS, HALF))  30.5 us
    all_to_all x1, blocking collectives, shards(): second = swap(second)  27 us
    pallas_call x1, Pallas kernels, project(): pl.pallas_call(project_kernel, grid=(6,), in_specs=[pl.BlockSpec(memory_s...  24.1 us
    pallas_call x2, Pallas kernels, scan(): pl.pallas_call(functools.partial(scan_kernel, half), grid=(ROWS // 2,), i...  18.8 us
    pallas_call x1, Pallas kernels, finish(): pl.pallas_call(finish_kernel, grid=(LINE // 32,), in_specs=[cells(HALF),...  11.6 us
    all_to_all x1, starting transfers between devices, shards(): arrived = swap(pieces.reshape(BANDS, 16, GROUP + 128))  10.1 us
    pallas_call x1, Pallas kernels, edges(): pl.pallas_call(edge_kernel, grid=(4,), in_specs=[whole(LINE, D), whole(LI...  8.41 us
    pallas_call x1, Pallas kernels, rest(): pl.pallas_call(rest_kernel, grid=(LINE // 32,), in_specs=[pl.BlockSpec((R...  7.21 us
  transfers between devices with their start and end apart: 6, of which 0 were waited for; matrix products, arithmetic and copies ran while one was open for 0% of the time, Pallas kernels for 27%

profile of v3, /device:TPU:0, one launch (start us, length us, event | category | flops | bytes accessed | tf_op | source)
XLA Modules:
  0.0 158.6 jit_solution(13599496499167210651)
XLA Ops:
  0.0 1.2 slice_bitcast_fusion
  1.2 1.3 collective-permute-start.1
  2.5 4.6 %collective-permute-start = (bf16[128,1536]{1,0:T(8,128)(2,1)S(1)}, bf16[128,1536]{1,0:T(8,128)(2,1)S(1)}, u32[]{:S(2)}, u32[]{:S(2)}) collective-permute-start(bf16[128,1536]{1,0:T(8,128)(2,1)S(1)} %get-tuple-element.46), channel_id=1, source_target_pairs={{0,1},{1,2},{2,3},{3,4},{4,5},{5,6},{6,7},{7,8},{8,9},{9,10},{10,1... | collective-permute-start | bytes 1179656 | tf_op jit(solution)/shard_map/ppermute | solution.py:710
  7.0 24.1 %project.1 = (bf16[1024,1536]{1,0:T(8,128)(2,1)}, bf16[1024,1536]{1,0:T(8,128)(2,1)}, bf16[512,1536]{1,0:T(8,128)(2,1)}, bf16[1024,128]{1,0:T(8,128)(2,1)}, bf16...) custom-call(bf16[1024,1536]{1,0:T(8,128)(2,1)} %bitcast.34, ...), custom_call_target="tpu_custom_call" | custom-call | flops 10141827072 | bytes 20971520 | tf_op jit(solution)/shard_map/project/pallas_call | solution.py:250
  31.1 0.0 collective-permute-done.1.bottom
  31.1 0.0 copy-start.3
  31.1 0.0 collective-permute-done.top
  31.2 0.0 copy-start.4
  31.2 0.7 copy-done.3
  31.9 0.2 copy-done.4
  32.1 8.4 %edges.1 = (bf16[1024,1536]{1,0:T(8,128)(2,1)}, bf16[1024,128]{1,0:T(8,128)(2,1)}, bf16[4,4,16,512]{3,2,1,0:T(8,128)(2,1)}) custom-call(bf16[128,1536]{1,0:T(8,128)(2,1)} %copy-done.4, bf16[128,1536]{1,0:T(8,128)(2,1)} %copy-done.3, f32[1,1536]{1,0:T(1,128)} %gain.4, bf16[1536,1664]{1,0:T(8,128)(2,1)} %bitcast.30, ...), custom_call_target="tpu_custom_call", output_to_operand_aliasing={{0}: (14, {}), {1}: (15, {})} | custom-call | flops 1325662208 | bytes 10485760 | tf_op jit(solution)/shard_map/edges/pallas_call | solution.py:402
  40.5 10.1 %all-to-all-start = ((bf16[16,16,512]{2,1,0:T(8,128)(2,1)}), bf16[16,16,512]{2,1,0:T(8,128)(2,1)S(1)}, u32[]{:S(2)}, u32[]{:S(2)}) async-start(bf16[16,16,512]{2,1,0:T(8,128)(2,1)} %bitcast.42), calls=%async_computation | async-start | bytes 524288 | tf_op jit(solution)/shard_map/all_to_all | solution.py:726
  50.5 9.4 %scan.2 = bf16[1024,768]{1,0:T(8,128)(2,1)} custom-call(bf16[1024,1536]{1,0:T(8,128)(2,1)} %get-tuple-element.40.x_even.x_odd, bf16[1024,1536]{1,0:T(8,128)(2,1)} %get-tuple-element.40.x_even.x_odd, bf16[1024,128]{1,0:T(8,128)(2,1)} %get-tuple-element.34.bcs, f32[24,1024]{1,0:T(8,128)} %get-tuple-element.35.cum, f32[24,1024]{1,0:T(8,128)} %get-tuple-element.36.dt, ...), custom_call_target="tpu_custom_call" | custom-call | flops 2147483648 | bytes 5242880 | tf_op jit(solution)/shard_map/scan/pallas_call | solution.py:533
  59.9 0.0 all-to-all-done.arrived
  59.9 0.0 copy-start.1
  59.9 0.7 copy-done.1
  60.6 1.8 %relay.1 = bf16[16,16,384]{2,1,0:T(8,128)(2,1)} custom-call(bf16[16,16,512]{2,1,0:T(8,128)(2,1)} %copy-done.1), custom_call_target="tpu_custom_call" | custom-call | tf_op jit(solution)/shard_map/relay/pallas_call | solution.py:586
  62.5 7.2 %all-to-all-start.1 = ((bf16[16,16,384]{2,1,0:T(8,128)(2,1)}), bf16[16,16,384]{2,1,0:T(8,128)(2,1)S(1)}, u32[]{:S(2)}, u32[]{:S(2)}) async-start(bf16[16,16,384]{2,1,0:T(8,128)(2,1)} %relay.1), calls=%async_computation.1 | async-start | bytes 393216 | tf_op jit(solution)/shard_map/all_to_all | solution.py:731
  69.7 9.4 %scan.3 = bf16[1024,768]{1,0:T(8,128)(2,1)} custom-call(bf16[1024,1536]{1,0:T(8,128)(2,1)} %get-tuple-element.40.x_even.x_odd, bf16[1024,1536]{1,0:T(8,128)(2,1)} %get-tuple-element.40.x_even.x_odd, bf16[1024,128]{1,0:T(8,128)(2,1)} %get-tuple-element.34.bcs, f32[24,1024]{1,0:T(8,128)} %get-tuple-element.35.cum, f32[24,1024]{1,0:T(8,128)} %get-tuple-element.36.dt, ...), custom_call_target="tpu_custom_call" | custom-call | flops 2147483648 | bytes 5242880 | tf_op jit(solution)/shard_map/scan/pallas_call | solution.py:533
  79.1 0.0 all-to-all-done.1.entering
  79.1 0.0 copy-start.2
  79.1 0.7 copy-done.2
  79.8 11.6 %finish.1 = (bf16[8,128,1536]{2,1,0:T(8,128)(2,1)}, bf16[1024,768]{1,0:T(8,128)(2,1)}) custom-call(bf16[8,128,768]{2,1,0:T(8,128)(2,1)} %bitcast.37, bf16[8,128,768]{2,1,0:T(8,128)(2,1)} %bitcast.38, bf16[8,128,1536]{2,1,0:T(8,128)(2,1)} %bitcast.27, bf16[8,128,128]{2,1,0:T(8,128)(2,1)} %bitcast.39, f32[24,1024]{1,0:T(8,128)} %get-tuple-element.41.band_decay, ...), custom_call_target="tpu_custom_call" | custom-call | flops 2415919104 | bytes 16777216 | tf_op jit(solution)/shard_map/finish/pallas_call | solution.py:632
  91.4 0.0 copy-start
  91.4 7.2 %rest.1 = bf16[1024,768]{1,0:T(8,128)(2,1)} custom-call(bf16[8,128,1536]{2,1,0:T(8,128)(2,1)} %get-tuple-element.44.hidden, bf16[8,128,1536]{2,1,0:T(8,128)(2,1)} %bitcast.36, bf16[1536,1536]{1,0:T(8,128)(2,1)} %bitcast.33), custom_call_target="tpu_custom_call" | custom-call | flops 1048576 | bytes 1048576 | tf_op jit(solution)/shard_map/rest/pallas_call | solution.py:675
  98.6 0.0 collective-permute-start.3
  98.6 0.0 copy-done
  98.6 30.5 %all_to_all.20 = bf16[16,64,768]{2,1,0:T(8,128)(2,1)S(1)} all-to-all(bf16[16,64,768]{2,1,0:T(8,128)(2,1)S(1)} %bitcast.41), channel_id=1, replica_groups=mesh['segment'=8,'band'=16] {'band'}, dimensions={0} | all-to-all | bytes 3145728 | tf_op jit(solution)/shard_map/all_to_all | solution.py:738
  129.1 0.5 collective-permute-start.2
  129.6 0.0 collective-permute-done.3
  129.6 27.0 %all_to_all.21 = bf16[16,64,768]{2,1,0:T(8,128)(2,1)S(1)} all-to-all(bf16[16,64,768]{2,1,0:T(8,128)(2,1)S(1)} %collective-permute-done.3), channel_id=1, replica_groups=mesh['segment'=8,'band'=16] {'band'}, dimensions={0} | all-to-all | bytes 3145728 | tf_op jit(solution)/shard_map/all_to_all | solution.py:740
  156.6 0.0 collective-permute-done.2
  156.6 1.9 %copy_bitcast_fusion = bf16[1,8,128,1536]{3,2,1,0:T(8,128)(2,1)} fusion(bf16[16,64,768]{2,1,0:T(8,128)(2,1)S(1)} %all_to_all.21, bf16[16,64,768]{2,1,0:T(8,128)(2,1)S(1)} %collective-permute-done.2), kind=kLoop, calls=%fused_computation.1 | loop fusion | flops 6291456 | bytes 6291456 | tf_op jit(solution)/shard_map/reshape | solution.py:744
Async XLA Ops:
  1.2 30.0 %collective-permute-start.1 = (bf16[128,1536]{1,0:T(8,128)(2,1)S(1)}, bf16[128,1536]{1,0:T(8,128)(2,1)S(1)}, u32[]{:S(2)}, u32[]{:S(2)}) collective-permute-start(bf16[128,1536]{1,0:T(8,128)(2,1)S(1)} %get-tuple-element.45), channel_id=1, source_target_pairs={{1,0},{2,1},{3,2},{4,3},{5,4},{6,5},{7,6},{8,7},{9,8},{10,9},{11,1... | collective-permute-start | bytes 1179656 | tf_op jit(solution)/shard_map/ppermute | solution.py:711
  2.5 28.7 %collective-permute-start = (bf16[128,1536]{1,0:T(8,128)(2,1)S(1)}, bf16[128,1536]{1,0:T(8,128)(2,1)S(1)}, u32[]{:S(2)}, u32[]{:S(2)}) collective-permute-start(bf16[128,1536]{1,0:T(8,128)(2,1)S(1)} %get-tuple-element.46), channel_id=1, source_target_pairs={{0,1},{1,2},{2,3},{3,4},{4,5},{5,6},{6,7},{7,8},{8,9},{9,10},{10,1... | collective-permute-start | bytes 1179656 | tf_op jit(solution)/shard_map/ppermute | solution.py:710
  31.1 0.8 copy-start.3
  31.2 0.9 copy-start.4
  40.5 19.5 %all-to-all-start = ((bf16[16,16,512]{2,1,0:T(8,128)(2,1)}), bf16[16,16,512]{2,1,0:T(8,128)(2,1)S(1)}, u32[]{:S(2)}, u32[]{:S(2)}) async-start(bf16[16,16,512]{2,1,0:T(8,128)(2,1)} %bitcast.42), calls=%async_computation | async-start | bytes 524288 | tf_op jit(solution)/shard_map/all_to_all | solution.py:726
  59.9 0.7 copy-start.1
  62.5 16.6 %all-to-all-start.1 = ((bf16[16,16,384]{2,1,0:T(8,128)(2,1)}), bf16[16,16,384]{2,1,0:T(8,128)(2,1)S(1)}, u32[]{:S(2)}, u32[]{:S(2)}) async-start(bf16[16,16,384]{2,1,0:T(8,128)(2,1)} %relay.1), calls=%async_computation.1 | async-start | bytes 393216 | tf_op jit(solution)/shard_map/all_to_all | solution.py:731
  79.1 0.7 copy-start.2
  91.4 7.2 %copy-start = (bf16[1024,768]{1,0:T(8,128)(2,1)S(1)}, bf16[1024,768]{1,0:T(8,128)(2,1)}, u32[]{:S(2)}) copy-start(bf16[1024,768]{1,0:T(8,128)(2,1)} %get-tuple-element.43) | copy-start | bytes 4718596
  98.6 31.0 %collective-permute-start.3 = (bf16[16,64,768]{2,1,0:T(8,128)(2,1)}, bf16[16,64,768]{2,1,0:T(8,128)(2,1)S(1)}, u32[]{:S(2)}, u32[]{:S(2)}) collective-permute-start(bf16[16,64,768]{2,1,0:T(8,128)(2,1)} %bitcast.40), channel_id=1, source_target_pairs={{0,16},{16,32},{32,48},{48,64},{64,80},{80,96},{96,112},{112,0},{1... | collective-permute-start | bytes 4718600 | tf_op jit(solution)/shard_map/ppermute | solution.py:739
  129.1 27.5 %collective-permute-start.2 = (bf16[16,64,768]{2,1,0:T(8,128)(2,1)S(1)}, bf16[16,64,768]{2,1,0:T(8,128)(2,1)S(1)}, u32[]{:S(2)}, u32[]{:S(2)}) collective-permute-start(bf16[16,64,768]{2,1,0:T(8,128)(2,1)S(1)} %all_to_all.20), channel_id=1, source_target_pairs={{0,16},{16,32},{32,48},{48,64},{64,80},{80,96},{96,112},{112,0},{1... | collective-permute-start | bytes 4718600 | tf_op jit(solution)/shard_map/ppermute | solution.py:741

commit v4 on v3

v4 whole, which is shorter than its diff:
```python
import functools

import jax
import jax.numpy as jnp
from jax import lax
from jax.experimental import pallas as pl
from jax.experimental.pallas import tpu as pltpu
from jax.sharding import PartitionSpec as P

EPSILON = 1e-05
ROWS = 8
LINE = 128
LENGTH = ROWS * LINE
HEADS = 24
WIDTH = 64
STATE = 64
INNER = HEADS * WIDTH
D = 1536
HALF = INNER // 2
FIRST = 896
GROUP = 384
GROUP_HEADS = GROUP // WIDTH
BANDS = 16
F32 = jnp.float32
BF16 = jnp.bfloat16
MIB = 1 << 20
LOG2E = 1.4426950408889634


def params(mib=24):
    return pltpu.CompilerParams(vmem_limit_bytes=mib * MIB)


kept = pl.BlockSpec(memory_space=pltpu.VMEM)
far = pl.BlockSpec(memory_space=pl.ANY)


def small(*shape):
    return pl.BlockSpec(shape, lambda *i: (0,) * len(shape))


def near(a):
    return pltpu.with_memory_space_constraint(a, pltpu.VMEM)


def hbm(a):
    return pltpu.with_memory_space_constraint(a, pltpu.HBM)


def upright(row):
    return jnp.broadcast_to(row, (LINE, HEADS)).T[:, :1]


def whole(*shape):
    return pl.BlockSpec(shape, lambda i: (0,) * len(shape), pipeline_mode=pl.Buffered(1))


def dot(a, b):
    return jnp.dot(a, b, preferred_element_type=F32)


def rms(values, gain):
    return values * lax.rsqrt(jnp.mean(values * values, -1, keepdims=True) + EPSILON) * gain


def silu(v):
    half = 0.5 * v
    return half + half * jnp.tanh(half)


def head_spread(channels, first):
    head = lax.broadcasted_iota(jnp.int32, (2 * HEADS, channels), 0)
    head = jnp.where(head < HEADS, head, head - HEADS)
    channel = lax.broadcasted_iota(jnp.int32, (2 * HEADS, channels), 1)
    return jnp.where(head - first == channel // WIDTH, 1.0, 0.0).astype(BF16)


def two_terms(values_t):
    high = values_t.astype(BF16).astype(F32)
    return jnp.concatenate([high, values_t - high], axis=0).T.astype(BF16)


def place(r):
    return (r + 1) % ROWS * LINE


def fill(padded, tile, slot, line):
    padded[tile, slot, pl.ds(8, LINE), :] = line.astype(F32)


def convolved(padded, tile, slot, taps, bias):
    total = bias
    for i in range(3):
        for j in range(3):
            total = total + padded[tile, slot - 1 + i, pl.ds(7 + j, LINE), :] * taps[3 * i + j]
    return silu(total).astype(BF16)


def lanes(refs, start):
    return [ref[:, start : start + 128] for ref in refs]


def project_kernel(
    tok,
    gain,
    w_xbc,
    w_g,
    w_dt,
    dt_bias,
    rate,
    taps_ref,
    bias,
    skip,
    out_gain,
    x,
    gate,
    rim,
    bcs,
    rim_bc,
    cum,
    dt,
    band_tail,
    band_decay,
    total,
    mid,
    w_near,
    tok_near,
    gain_near,
    taps_near,
    bias_near,
    skip_near,
    out_gain_near,
    normed,
    lines_a,
    lines_b,
    lines_bc,
    b_t,
    tails,
    w_g_near,
    tok_sem,
    w_sem,
    w_g_sem,
):
    def tokens_in(m):
        part = pl.ds(m * 256, 256)
        return pltpu.make_async_copy(tok.at[part, :], tok_near.at[part, :], tok_sem.at[m])

    def w_in(n):
        part = pl.ds(n * 512, 512 if n < 3 else 128)
        return pltpu.make_async_copy(w_xbc.at[:, part], w_near.at[:, part], w_sem.at[n])

    def gate_in(n):
        part = pl.ds(n * 512, 512)
        return pltpu.make_async_copy(w_g.at[:, part], w_g_near.at[:, part], w_g_sem.at[n])

    taps = [taps_ref[n] for n in range(9)]

    def store(m, values, padded, out, start, tiles, tile=0):
        for n in range(m * 2, m * 2 + 2):
            line = values[(n - m * 2) * LINE : (n - m * 2 + 1) * LINE]
            for k in range(tiles):
                fill(padded, tile + k, n, line[:, k * 128 : (k + 1) * 128])
            if n in (0, 1, 6, 7):
                place_n = (n if n < 2 else n - 4) * LINE
                out[pl.ds(place_n, LINE), pl.ds(start, tiles * 128)] = line

    def multiply_x(m, here, padded, chunk, side):
        start = chunk * 512 + side * 256
        values = dot(here, w_near[:, pl.ds(start, 256)]).astype(BF16)
        store(m, values, padded, rim, start, 2, side * 2)

    def multiply_gate(m, n, side):
        rows, part = pl.ds(m * 256, 256), pl.ds(n * 512 + side * 256, 256)
        gate[rows, part] = silu(dot(normed[rows, :], w_g_near[:, part])).astype(BF16)

    def inside(k, padded, chunk, rows):
        start = chunk * 512 + k * 128
        for r in rows:
            x[pl.ds(place(r), LINE), pl.ds(start, 128)] = convolved(
                padded, k, r, lanes(taps, start), bias[:, start : start + 128]
            )

    def add_state(piece):
        part = pl.ds(piece * 256, 256)
        spread = head_spread(256, piece * 4)
        own = x[pl.ds(2 * LINE, (ROWS - 2) * LINE), part].astype(F32)
        mid[:, part] = dot(b_t[pl.ds(0, STATE), :], (own * dot(tails[...], spread)).astype(BF16))

    tokens_in(0).start()
    w_in(3).start()
    w_in(0).start()
    for m in range(1, 4):
        tokens_in(m).start()
    w_in(1).start()
    w_in(2).start()
    for n in range(3):
        gate_in(n).start()
    gain_near[...] = gain[...]
    taps_near[...] = taps_ref[...]
    bias_near[...] = bias[...]
    skip_near[...] = skip[...]
    out_gain_near[...] = out_gain[...]
    for padded in (lines_a, lines_b, lines_bc):
        for n in range(ROWS):
            for k in range(padded.shape[0]):
                padded[k, n, pl.ds(0, 8), :] = jnp.zeros((8, 128), F32)
                padded[k, n, pl.ds(LINE + 8, 8), :] = jnp.zeros((8, 128), F32)
    for m in range(4):
        tokens_in(m).wait()
        if m == 0:
            w_in(3).wait()
            w_in(0).wait()
        part = pl.ds(m * 256, 256)
        here = rms(tok_near[part, :].astype(F32), gain[...]).astype(BF16)
        normed[part, :] = here
        store(m, dot(here, w_near[:, pl.ds(INNER, 128)]).astype(BF16), lines_bc, rim_bc, 0, 1)
        for side in range(2):
            multiply_x(m, here, lines_a, 0, side)

    w_in(1).wait()
    for r in range(1, ROWS - 1):
        values = convolved(
            lines_bc, 0, r, lanes(taps, INNER), bias[:, INNER : INNER + 128]
        )
        bcs[pl.ds(place(r), LINE), :] = values
        b_t[:, pl.ds((r - 1) * LINE, LINE)] = values.astype(F32).T.astype(BF16)
    raw = lax.dot_general(
        w_dt[...], normed[...], (((1,), (1,)), ((), ())), preferred_element_type=F32
    ) + upright(dt_bias[...])
    steps = jnp.maximum(raw, 0.0) + jnp.log1p(jnp.exp(-jnp.abs(raw)))
    dt[...] = steps
    for m in range(4):
        for side in range(2):
            multiply_x(m, normed[pl.ds(m * 256, 256), :], lines_b, 1, side)
            inside(m, lines_a, 0, range(1 + 3 * side, 4 + 3 * side))

    w_in(2).wait()
    log_decay = -upright(rate[...]) * steps
    i = lax.broadcasted_iota(jnp.int32, (LINE, LINE), 0)
    j = lax.broadcasted_iota(jnp.int32, (LINE, LINE), 1)
    sums = jnp.dot(
        jnp.concatenate([log_decay[:, r * LINE : (r + 1) * LINE] for r in range(ROWS)], axis=0),
        jnp.where(i <= j, 1.0, 0.0).astype(F32),
        precision=lax.Precision.HIGHEST,
        preferred_element_type=F32,
    )
    lines = [sums[r * HEADS : (r + 1) * HEADS] for r in range(ROWS)]
    ends = [line[:, LINE - 1 :] for line in lines]
    before = [jnp.zeros_like(ends[0])]
    after = [jnp.zeros_like(ends[0])]
    for r in range(ROWS - 1):
        before.append(before[-1] + ends[r])
        after.append(after[-1] + ends[ROWS - 1 - r])
    for r in range(ROWS):
        part = slice(r * LINE, (r + 1) * LINE)
        cum[:, part] = lines[r]
        band_decay[:, part] = jnp.exp(lines[r] + before[r])
        tail = steps[:, part] * jnp.exp((ends[r] - lines[r]) + after[ROWS - 1 - r])
        band_tail[:, part] = tail
        if 0 < r < ROWS - 1:
            tails[pl.ds((r - 1) * LINE, LINE), :] = two_terms(tail)
    total[...] = jnp.broadcast_to(before[-1] + ends[-1], (HEADS, LINE)).T[:1]
    for m in range(4):
        for side in range(2):
            multiply_x(m, normed[pl.ds(m * 256, 256), :], lines_a, 2, side)
            inside(m, lines_b, 1, range(1 + 3 * side, 4 + 3 * side))

    gate_in(0).wait()
    for m in range(4):
        for side in range(2):
            multiply_gate(m, 0, side)
            inside(m, lines_a, 2, range(1 + 3 * side, 4 + 3 * side))
    for n in (1, 2):
        gate_in(n).wait()
        for m in range(4):
            for side in range(2):
                multiply_gate(m, n, side)
            if m < 3:
                add_state((n - 1) * 3 + m)


def project(tok, gain, w_xbc, w_gate, w_dt_t, dt_bias, rate, taps, conv_bias, skip, out_gain):
    per_head = pltpu.VMEM((HEADS, LENGTH), F32)
    return pl.pallas_call(
        project_kernel,
        in_specs=[
            far,
            small(1, D),
            far,
            far,
            small(HEADS, D),
            small(1, HEADS),
            small(1, HEADS),
            small(9, 1, INNER + 128),
            small(1, INNER + 128),
            small(1, HEADS),
            small(1, INNER),
        ],
        out_specs=[kept] * 18,
        out_shape=[
            pltpu.VMEM((LENGTH, INNER), BF16),
            pltpu.VMEM((LENGTH, INNER), BF16),
            pltpu.VMEM((4 * LINE, INNER), BF16),
            pltpu.VMEM((LENGTH, 128), BF16),
            pltpu.VMEM((4 * LINE, 128), BF16),
            per_head,
            per_head,
            per_head,
            per_head,
            pltpu.VMEM((1, HEADS), F32),
            pltpu.VMEM((STATE, INNER), F32),
            pltpu.VMEM((D, INNER + 128), BF16),
            pltpu.VMEM((LENGTH, D), BF16),
            pltpu.VMEM((1, D), F32),
            pltpu.VMEM((9, 1, INNER + 128), F32),
            pltpu.VMEM((1, INNER + 128), F32),
            pltpu.VMEM((1, HEADS), F32),
            pltpu.VMEM((1, INNER), F32),
        ],
        scratch_shapes=[
            pltpu.VMEM((LENGTH, D), BF16),
            pltpu.VMEM((4, ROWS, LINE + 16, 128), F32),
            pltpu.VMEM((4, ROWS, LINE + 16, 128), F32),
            pltpu.VMEM((1, ROWS, LINE + 16, 128), F32),
            pltpu.VMEM((128, (ROWS - 2) * LINE), BF16),
            pltpu.VMEM(((ROWS - 2) * LINE, 2 * HEADS), BF16),
            pltpu.VMEM((D, INNER), BF16),
            pltpu.SemaphoreType.DMA((4,)),
            pltpu.SemaphoreType.DMA((4,)),
            pltpu.SemaphoreType.DMA((3,)),
        ],
        compiler_params=params(),
        cost_estimate=pl.CostEstimate(
            flops=2 * LENGTH * D * 3224, bytes_accessed=20 << 20, transcendentals=LENGTH * INNER
        ),
        name="project",
    )(hbm(tok), hbm(gain), hbm(w_xbc), hbm(w_gate), *map(hbm, (w_dt_t, dt_bias, rate, taps, conv_bias, skip, out_gain)))


def edge_kernel(
    top,
    bottom,
    gain,
    w_near,
    rim,
    rim_bc,
    taps_ref,
    bias,
    band_tail,
    total,
    mid,
    x_in,
    bcs_in,
    x,
    bcs,
    pieces,
    edge,
    lines,
    b_t,
    tails,
):
    del x_in, bcs_in
    taps = [taps_ref[n] for n in range(9)]

    def both(side, own, own_start, start, out, out_start, tiles):
        for k in range(tiles):
            part = slice(k * 128, (k + 1) * 128)
            own_part = pl.ds(own_start + k * 128, 128)
            tile = start // 128 + k
            for slot, line in enumerate(
                [side[:LINE, part], own[pl.ds(0, LINE), own_part], own[pl.ds(LINE, LINE), own_part]]
                + [own[pl.ds(2 * LINE, LINE), own_part], own[pl.ds(3 * LINE, LINE), own_part]]
                + [side[LINE:, part]]
            ):
                fill(lines, tile % 4, slot, line)
            for slot, r in ((1, 0), (4, ROWS - 1)):
                out[pl.ds(place(r), LINE), pl.ds(out_start + k * 128, 128)] = convolved(
                    lines, tile % 4, slot, lanes(taps, tile * 128), bias[:, tile * 128 : tile * 128 + 128]
                )

    for slot in range(6):
        for k in range(4):
            lines[k, slot, pl.ds(0, 8), :] = jnp.zeros((8, 128), F32)
            lines[k, slot, pl.ds(LINE + 8, 8), :] = jnp.zeros((8, 128), F32)
    tails[pl.ds(place(0), LINE), :] = two_terms(band_tail[:, :LINE])
    tails[pl.ds(place(ROWS - 1), LINE), :] = two_terms(band_tail[:, LENGTH - LINE :])
    head = lax.broadcasted_iota(jnp.int32, (HEADS, 128), 0)
    lane = lax.broadcasted_iota(jnp.int32, (HEADS, 128), 1)
    first = total[...].astype(BF16)
    rest = total[...] - first.astype(F32)
    second = rest.astype(BF16)
    third = (rest - second.astype(F32)).astype(BF16)
    for g in range(4):
        pick = jnp.where(head == lane + g * GROUP_HEADS, 1.0, 0.0).astype(BF16)
        terms = jnp.concatenate(
            [dot(jnp.broadcast_to(t, (8, HEADS)), pick)[:1] for t in (first, second, third)]
            + [jnp.zeros((13, 128), F32)],
            axis=0,
        ).astype(BF16)
        for a in range(4):
            pieces[a, g, :, pl.ds(GROUP, 128)] = terms
    for n, side in enumerate((top, bottom)):
        edge[pl.ds(n * LINE, LINE), :] = rms(side[...].astype(F32), gain[...]).astype(BF16)
    both(dot(edge[...], w_near[:, pl.ds(INNER, 128)]).astype(BF16), rim_bc, 0, INNER, bcs, 0, 1)
    b_t[...] = bcs[pl.ds(0, 2 * LINE), :].astype(F32).T.astype(BF16)
    for n in range(3):
        start = n * 512
        part = pl.ds(start, 512)
        both(dot(edge[...], w_near[:, part]).astype(BF16), rim, start, start, x, start, 4)
        weighted = x[pl.ds(0, 2 * LINE), part].astype(F32) * dot(tails[...], head_spread(512, n * 8))
        state = mid[:, part] + dot(b_t[pl.ds(0, STATE), :], weighted.astype(BF16))
        for k in range(4):
            g, within = divmod(n * 4 + k, 3)
            for a in range(4):
                pieces[a, g, :, pl.ds(within * 128, 128)] = state[
                    16 * a : 16 * a + 16, k * 128 : (k + 1) * 128
                ].astype(BF16)


def edges(top, bottom, gain, w_near, rim, rim_bc, taps, conv_bias, band_tail, total, mid, x, bcs):
    return pl.pallas_call(
        edge_kernel,
        in_specs=[kept] * 13,
        out_specs=[kept, kept, pl.BlockSpec(memory_space=pltpu.VMEM)],
        out_shape=[
            pltpu.VMEM((LENGTH, INNER), BF16),
            pltpu.VMEM((LENGTH, 128), BF16),
            jax.ShapeDtypeStruct((4, 4, 16, GROUP + 128), BF16),
        ],
        input_output_aliases={11: 0, 12: 1},
        scratch_shapes=[
            pltpu.VMEM((2 * LINE, D), BF16),
            pltpu.VMEM((4, 6, LINE + 16, 128), F32),
            pltpu.VMEM((128, 2 * LINE), BF16),
            pltpu.VMEM((2 * LINE, 2 * HEADS), BF16),
        ],
        compiler_params=params(),
        cost_estimate=pl.CostEstimate(
            flops=2 * 256 * D * 1664 + 10 * LENGTH * 1664,
            bytes_accessed=10 << 20,
            transcendentals=256 * 1664,
        ),
        name="edges",
    )(
        near(top),
        near(bottom),
        near(gain),
        near(w_near),
        near(rim),
        near(rim_bc),
        near(taps),
        near(conv_bias),
        near(band_tail),
        near(total),
        near(mid),
        near(x),
        near(bcs),
    )


def scan_kernel(half, x, bcs, cum, dt, gate, skip, *refs):
    if half:
        w, out, w_near, direct, state, sums, steps, weights, b_t, c, w_sem = refs
        fetch = pltpu.make_async_copy(w, w_near, w_sem)
        fetch.start()
    else:
        out, direct, state, sums, steps, weights, b_t, c = refs
    lane = lax.broadcasted_iota(jnp.int32, (LINE, LINE), 1)
    row = lax.broadcasted_iota(jnp.int32, (LINE, LINE), 0)
    left = lane < WIDTH
    direct[...] = dot(
        two_terms(jnp.broadcast_to(upright(skip[...]), (HEADS, 8))),
        head_spread(HALF, half * HEADS // 2),
    )
    state[...] = jnp.zeros_like(state)
    for r in range(ROWS):
        part = slice(r * LINE, (r + 1) * LINE)
        sums[r] = (cum[:, part] * LOG2E).T
        steps[r] = dt[:, part].T
        both = bcs[pl.ds(place(r), LINE), :].astype(F32)
        b_t[r] = both.T.astype(BF16)[:STATE]
        c[r] = pltpu.roll(both, STATE, 1).astype(BF16)[:, :STATE]
    for r in range(ROWS):
        weights[r] = jnp.where(row >= lane, dot(c[r], b_t[r]), 0.0)

    def line(r, placed):
        rows = pl.ds(pl.multiple_of(r * LINE, LINE), LINE)
        placed_rows = pl.ds(pl.multiple_of(placed * LINE, LINE), LINE)
        sums_here, steps_here, weights_here = sums[r], steps[r], weights[r]
        sums_t = cum[:, rows] * LOG2E
        steps_t = dt[:, rows]

        def mixing(h):
            along = jnp.broadcast_to(sums_here[:, h : h + 1], (LINE, LINE))
            decay = jnp.exp2(jnp.minimum(along - sums_t[h : h + 1], 0.0))
            return along, (decay * (weights_here * steps_t[h : h + 1])).astype(BF16)

        for q in range(HEADS // 8):
            quad = pl.ds(q * 256, 256)
            carried = dot(c[r], state[:, quad].astype(BF16))
            tails, decays = [], []
            for p in (2 * q, 2 * q + 1):
                part = pl.ds(p * 128, 128)
                whole_part = pl.ds(half * HALF + p * 128, 128)
                h = half * HEADS // 2 + 2 * p
                values = x[placed_rows, whole_part].astype(F32)
                (along_a, mixing_a), (along_b, mixing_b) = mixing(h), mixing(h + 1)
                columns = jnp.concatenate(
                    [jnp.where(left, values, 0.0), jnp.where(left, 0.0, values)], axis=0
                ).astype(BF16)
                inner = dot(jnp.concatenate([mixing_a, mixing_b], axis=1), columns)
                here = jnp.where(left, along_a, along_b)
                carry = jnp.exp2(here)
                stepped = jnp.where(left, steps_here[:, h : h + 1], steps_here[:, h + 1 : h + 2])
                tails.append((values * stepped * jnp.exp2(here[LINE - 1 :] - here)).astype(BF16))
                decays.append(carry[LINE - 1 :])
                side = slice((p % 2) * 128, (p % 2) * 128 + 128)
                y = inner + carry * carried[:, side] + direct[0:1, part] * values
                out[rows, part] = (y * gate[rows, whole_part].astype(F32)).astype(BF16)
            state[:, quad] = jnp.concatenate(decays, axis=1) * state[:, quad] + dot(
                b_t[r], jnp.concatenate(tails, axis=1)
            )

    @pl.loop(0, ROWS // 2)
    def _(pair):
        line(2 * pair, 2 * pair + 1)
        line(2 * pair + 1, lax.rem(2 * pair + 2, ROWS))

    if half:
        fetch.wait()


def scan(half, x, bcs, cum, dt, gate, skip, *w):
    weights = [pltpu.VMEM((INNER, D), BF16)] * half
    return pl.pallas_call(
        functools.partial(scan_kernel, half),
        in_specs=[kept] * 6 + [far] * half,
        out_specs=[kept] * (1 + half),
        out_shape=[pltpu.VMEM((LENGTH, HALF), BF16)] + weights,
        scratch_shapes=[
            pltpu.VMEM((8, HALF), F32),
            pltpu.VMEM((STATE, HALF), F32),
            pltpu.VMEM((ROWS, LINE, HEADS), F32),
            pltpu.VMEM((ROWS, LINE, HEADS), F32),
            pltpu.VMEM((ROWS, LINE, LINE), F32),
            pltpu.VMEM((ROWS, STATE, LINE), BF16),
            pltpu.VMEM((ROWS, LINE, STATE), BF16),
        ]
        + [pltpu.SemaphoreType.DMA(())] * half,
        compiler_params=params(),
        cost_estimate=pl.CostEstimate(
            flops=2 << 30, bytes_accessed=5 << 20, transcendentals=LENGTH * LINE * HEADS // 2
        ),
        name="scan",
    )(near(x), near(bcs), near(cum), near(dt), near(gate), near(skip), *map(hbm, w))


def relay_kernel(arrived, out):
    logs = jnp.concatenate(
        [
            jnp.sum(arrived[j, :, pl.ds(GROUP, 128)].astype(F32), axis=0, keepdims=True)
            for j in range(BANDS)
        ],
        axis=0,
    )
    decay = jnp.exp(logs)
    high = decay.astype(BF16)
    low = (decay - high.astype(F32)).astype(BF16)
    lane = lax.broadcasted_iota(jnp.int32, (128, GROUP), 0)
    channel = lax.broadcasted_iota(jnp.int32, (128, GROUP), 1)
    spread = jnp.where(lane == channel // WIDTH, 1.0, 0.0).astype(BF16)
    wide = dot(high, spread) + dot(low, spread)
    state = jnp.zeros((16, GROUP), F32)
    for j in range(BANDS):
        out[j] = state.astype(BF16)
        state = wide[j : j + 1] * state + arrived[j, :, pl.ds(0, GROUP)].astype(F32)


def relay(arrived):
    return pl.pallas_call(
        relay_kernel,
        out_shape=jax.ShapeDtypeStruct((BANDS, 16, GROUP), BF16),
        compiler_params=params(16),
        name="relay",
    )(arrived)


def columns_out(values, tokens, turned, out, step):
    values = values + tokens.astype(F32)
    rows = pl.ds(pl.multiple_of(step * 256, 256), 256)
    for k in range(values.shape[1] // 128):
        part = slice(k * 128, (k + 1) * 128)
        for r in range(ROWS):
            turned[k, pl.ds(r, 32, stride=ROWS), :] = values[r * 32 : (r + 1) * 32, part]
        out[rows, part] = turned[k].astype(BF16)


def finish_kernel(
    local_a, local_b, gate, bcs, band_decay, entering, gain, tok, w, out, hidden, spread, state, decays, turned
):
    step = pl.program_id(0)

    @pl.when(step == 0)
    def _():
        spread[...] = head_spread(INNER, 0)
        state[pl.ds(0, STATE), :] = jnp.zeros((STATE, INNER), BF16)
        for a in range(4):
            for g in range(4):
                state[pl.ds(STATE + 16 * a, 16), pl.ds(g * GROUP, GROUP)] = entering[4 * a + g]
        for r in range(ROWS):
            decays[r] = two_terms(band_decay[:, r * LINE : (r + 1) * LINE])

    here = pl.ds(pl.multiple_of(step * 32, 32), 32)
    cells = lambda ref: ref[:, here, :].reshape(256, ref.shape[2])
    both = jnp.concatenate([bcs[1:, here, :], bcs[:1, here, :]], axis=0).reshape(256, 128)
    decay = dot(cells(decays), spread[...])
    local = jnp.concatenate([cells(local_a), cells(local_b)], axis=1)
    gated = local.astype(F32) + dot(both, state[...]) * decay * cells(gate).astype(F32)
    normed = rms(gated, gain[...]).astype(BF16)
    hidden[:, here, :] = normed.reshape(ROWS, 32, INNER)
    columns_out(
        dot(normed, w[:, pl.ds(0, FIRST)]),
        tok[:, here, pl.ds(0, FIRST)].reshape(256, FIRST),
        turned,
        out,
        step,
    )


def finish(local_a, local_b, gate, bcs, band_decay, entering, gain, tok, w_near):
    return pl.pallas_call(
        finish_kernel,
        grid=(LINE // 32,),
        in_specs=[kept] * 5 + [whole(BANDS, 16, GROUP), kept, kept, kept],
        out_specs=[kept, kept],
        out_shape=[
            pltpu.VMEM((LENGTH, FIRST), BF16),
            pltpu.VMEM((ROWS, LINE, INNER), BF16),
        ],
        scratch_shapes=[
            pltpu.VMEM((2 * HEADS, INNER), BF16),
            pltpu.VMEM((2 * STATE, INNER), BF16),
            pltpu.VMEM((ROWS, LINE, 2 * HEADS), BF16),
            pltpu.VMEM((FIRST // 128, 256, 128), F32),
        ],
        compiler_params=params(),
        cost_estimate=pl.CostEstimate(
            flops=2 * LENGTH * D * FIRST, bytes_accessed=16 << 20, transcendentals=LENGTH
        ),
        name="finish",
    )(
        near(local_a),
        near(local_b),
        near(gate),
        near(bcs),
        near(band_decay),
        entering,
        near(gain),
        near(tok),
        near(w_near),
    )


def rest_kernel(hidden, tok, w, out, turned):
    step = pl.program_id(0)
    here = pl.ds(pl.multiple_of(step * 32, 32), 32)
    part = pl.ds(FIRST, D - FIRST)
    columns_out(
        dot(hidden[:, here, :].reshape(256, INNER), w[:, part]),
        tok[:, here, part].reshape(256, D - FIRST),
        turned,
        out,
        step,
    )


def rest(hidden, tok, w_near):
    return pl.pallas_call(
        rest_kernel,
        grid=(LINE // 32,),
        in_specs=[kept] * 3,
        out_specs=kept,
        out_shape=pltpu.VMEM((LENGTH, D - FIRST), BF16),
        scratch_shapes=[pltpu.VMEM(((D - FIRST) // 128, 256, 128), F32)],
        compiler_params=params(),
        cost_estimate=pl.CostEstimate(
            flops=2 * LENGTH * D * (D - FIRST), bytes_accessed=8 << 20, transcendentals=0
        ),
        name="rest",
    )(near(hidden), near(tok), near(w_near))


def shards(
    tokens,
    in_gain,
    w_xbc,
    w_gate,
    w_dt,
    dt_bias,
    decay_rate,
    conv_w,
    conv_bias,
    skip,
    out_gain,
    w_out,
):
    bands = lax.axis_size("band")
    segments = lax.axis_size("segment")
    cells = tokens[0]
    tok = cells.reshape(LENGTH, D)
    top = lax.ppermute(cells[ROWS - 1], "band", [(i, i + 1) for i in range(bands - 1)])
    bottom = lax.ppermute(cells[0], "band", [(i + 1, i) for i in range(bands - 1)])

    (
        x,
        gate,
        rim,
        bcs,
        rim_bc,
        cum,
        dt,
        band_tail,
        band_decay,
        total,
        mid,
        w_xbc_near,
        tok_near,
        in_gain_near,
        taps_near,
        bias_near,
        skip_near,
        out_gain_near,
    ) = project(
        tok,
        in_gain,
        w_xbc[0],
        w_gate[0],
        w_dt[0].T,
        dt_bias,
        decay_rate,
        conv_w.swapaxes(0, 1),
        conv_bias,
        skip,
        out_gain,
    )
    x, bcs, pieces = edges(
        top,
        bottom,
        in_gain_near,
        w_xbc_near,
        rim,
        rim_bc,
        taps_near,
        bias_near,
        band_tail,
        total,
        mid,
        x,
        bcs,
    )
    swap = functools.partial(
        lax.all_to_all, axis_name="band", split_axis=0, concat_axis=0, tiled=True
    )
    onward = functools.partial(
        lax.ppermute, axis_name="segment", perm=[(i, (i + 1) % segments) for i in range(segments)]
    )
    arrived = swap(pieces.reshape(BANDS, 16, GROUP + 128))
    (local_a,) = scan(0, x, bcs, cum, dt, gate, skip_near)
    arrived, local_a = lax.optimization_barrier((arrived, local_a))
    states = relay(arrived)
    states, skip_b = lax.optimization_barrier((states, skip_near))
    entering = swap(states)
    local_b, w_out_near = scan(1, x, bcs, cum, dt, gate, skip_b, w_out[0])

    grid = lambda a: a.reshape(ROWS, LINE, a.shape[-1])
    parted = lambda a: a.reshape(BANDS, LENGTH // BANDS, a.shape[-1])
    first, hidden = finish(
        grid(local_a),
        grid(local_b),
        grid(gate),
        grid(bcs),
        band_decay,
        entering,
        out_gain_near,
        grid(tok_near),
        w_out_near,
    )
    first = swap(parted(first))
    second = onward(parted(rest(hidden, grid(tok_near), w_out_near)))
    second = swap(second)
    first = onward(first)
    both = jnp.concatenate([first, second], axis=-1)
    handed = both.reshape(BANDS, LINE // BANDS, ROWS, D).swapaxes(0, 1)
    return handed.reshape(1, LINE // BANDS, BANDS * ROWS, D)


def solution(mesh):
    in_specs = (
        P("segment", "band", None, None),
        P("segment", None),
        P("segment", None, None),
        P("segment", None, None),
        P("segment", None, None),
        P("segment", None),
        P("segment", None),
        P("segment", None, None),
        P("segment", None),
        P("segment", None),
        P("segment", None),
        P("segment", None, None),
    )
    out_specs = P("segment", "band", None, None)
    return jax.shard_map(shards, mesh=mesh, in_specs=in_specs, out_specs=out_specs, check_vma=False)
```

time: 160 us -> 163 us (1.019)
  blocking collectives: 57.6 us -> 25 us
  local copies, waits for them, and re-layouts: 3.46 us -> 30.9 us
  waiting for transfers between devices: 0.02 us -> 18.6 us
  Pallas kernels: 71.9 us -> 54.3 us
  starting transfers between devices: 23.6 us -> 30.7 us
    all_to_all x1 -> x0, blocking collectives: 30.5 us -> none  [shards(): first = swap(first.reshape(BANDS, LENGTH // BANDS, HALF))]
    unnamed x10 -> x46, local copies, waits for them, and re-layouts: 2.29 us -> 29.8 us
    pallas_call x6, Pallas kernels: 70.1 us -> 53.2 us  [the longest x1 22.4 us: project(): pl.pallas_call(project_kernel, in_specs=[far, small(1, D), far, far, smal...]
    all_to_all x0 -> x1, waiting for transfers between devices: none -> 16.2 us  [shards(): first = swap(parted(first))]
    all_to_all x0 -> x1, starting transfers between devices: none -> 7.47 us  [shards(): first = swap(parted(first))]
    ppermute x1, waiting for transfers between devices: 0.01 us -> 2.39 us  [shards(): second = onward(parted(rest(hidden, grid(tok_near), w_out_near)))]
    all_to_all x1, blocking collectives: 27 us -> 25 us  [shards(): second = swap(second)]
  transfers between devices with their start and end apart: 6 -> 7, of which waited for: 0 -> 2; matrix products, arithmetic and copies ran while one was open for 0% -> 0% of each run, Pallas kernels for 27% -> 25%
where the time goes in v4:
time: 163 us; the launch traced here: 162 us
  Pallas kernels  54.3 us (33%)
  local copies, waits for them, and re-layouts  30.9 us (19%)
  starting transfers between devices  30.7 us (19%)
  blocking collectives  25 us (15%)
  waiting for transfers between devices  18.6 us (11%)
  other arithmetic  1.96 us (1%)
    unnamed x46, local copies, waits for them, and re-layouts  29.8 us
    all_to_all x1, blocking collectives, shards(): second = swap(second)  25 us
    pallas_call x1, Pallas kernels, project(): pl.pallas_call(project_kernel, in_specs=[far, small(1, D), far, far, smal...  22.4 us
    all_to_all x1, waiting for transfers between devices, shards(): first = swap(parted(first))  16.2 us
    pallas_call x2, Pallas kernels, scan(): pl.pallas_call(functools.partial(scan_kernel, half), in_specs=[kept] * 6...  13.3 us
    all_to_all x1, starting transfers between devices, shards(): arrived = swap(pieces.reshape(BANDS, 16, GROUP + 128))  10.1 us
    pallas_call x1, Pallas kernels, finish(): pl.pallas_call(finish_kernel, grid=(LINE // 32,), in_specs=[kept] * 5 + [...  8.61 us
    all_to_all x1, starting transfers between devices, shards(): first = swap(parted(first))  7.47 us
  transfers between devices with their start and end apart: 7, of which 2 were waited for; matrix products, arithmetic and copies ran while one was open for 0% of the time, Pallas kernels for 25%

profile of v4, /device:TPU:0, one launch (start us, length us, event | category | flops | bytes accessed | tf_op | source)
XLA Modules:
  0.0 161.7 jit_solution(1310543951127625083)
XLA Ops:
  0.0 1.2 slice_bitcast_fusion
  1.2 1.3 collective-permute-start.1
  2.5 4.6 %collective-permute-start = (bf16[128,1536]{1,0:T(8,128)(2,1)S(1)}, bf16[128,1536]{1,0:T(8,128)(2,1)S(1)}, u32[]{:S(2)}, u32[]{:S(2)}) collective-permute-start(bf16[128,1536]{1,0:T(8,128)(2,1)S(1)} %get-tuple-element.64), channel_id=1, source_target_pairs={{0,1},{1,2},{2,3},{3,4},{4,5},{5,6},{6,7},{7,8},{8,9},{9,10},{10,1... | collective-permute-start | bytes 1179656 | tf_op jit(solution)/shard_map/ppermute | solution.py:711
  7.0 22.4 %project.1 = (bf16[1024,1536]{1,0:T(8,128)(2,1)S(1)}, bf16[1024,1536]{1,0:T(8,128)(2,1)S(1)}, bf16[512,1536]{1,0:T(8,128)(2,1)S(1)}, bf16[1024,128]{1,0:T(8,128)...) custom-call(bf16[1024,1536]{1,0:T(8,128)(2,1)} %bitcast.36, ...), custom_call_target="tpu_custom_call" | custom-call | flops 10141827072 | bytes 20971520 | tf_op jit(solution)/shard_map/project/pallas_call | solution.py:284
  29.5 0.0 copy-start.6
  29.5 1.7 %copy-done.6 = bf16[1024,1536]{1,0:T(8,128)(2,1)} copy-done((bf16[1024,1536]{1,0:T(8,128)(2,1)}, bf16[1024,1536]{1,0:T(8,128)(2,1)S(1)}, u32[]{:S(2)}) %copy-start.6) | copy-done | bytes 3145752
  31.1 0.0 copy-start.21
  31.1 0.0 collective-permute-done.1.bottom
  31.1 0.0 collective-permute-done.top
  31.1 4.2 %edges.1 = (bf16[1024,1536]{1,0:T(8,128)(2,1)S(1)}, bf16[1024,128]{1,0:T(8,128)(2,1)S(1)}, bf16[4,4,16,512]{3,2,1,0:T(8,128)(2,1)S(1)}) custom-call(bf16[128,1536]{1,0:T(8,128)(2,1)S(1)} %collective-permute-done.top, bf16[128,1536]{1,0:T(8,128)(2,1)S(1)} %collective-permute-done.1.bottom, ...), custom_call_target="tpu_custom_call", output_to_operand_aliasing={{0}: (11, {}), {1}: (12, {})} | custom-call | flops 1325662208 | bytes 10485760 | tf_op jit(solution)/shard_map/edges/pallas_call | solution.py:421
  35.4 0.0 copy-done.17
  35.4 0.0 copy-done.21
  35.4 0.0 copy-start
  35.4 1.7 %copy-done = bf16[1024,1536]{1,0:T(8,128)(2,1)} copy-done((bf16[1024,1536]{1,0:T(8,128)(2,1)}, bf16[1024,1536]{1,0:T(8,128)(2,1)S(1)}, u32[]{:S(2)}) %copy-start) | copy-done | bytes 3145752
  37.1 0.0 copy-start.20
  37.1 0.7 copy-done.20
  37.8 10.1 %all-to-all-start = ((bf16[16,16,512]{2,1,0:T(8,128)(2,1)}), bf16[16,16,512]{2,1,0:T(8,128)(2,1)}, u32[]{:S(2)}, u32[]{:S(2)}) async-start(bf16[16,16,512]{2,1,0:T(8,128)(2,1)} %bitcast.34), calls=%async_computation | async-start | bytes 524288 | tf_op jit(solution)/shard_map/all_to_all | solution.py:767
  47.9 0.0 copy-start.1
  47.9 1.9 %copy-done.1 = bf16[1024,1536]{1,0:T(8,128)(2,1)S(1)} copy-done((bf16[1024,1536]{1,0:T(8,128)(2,1)S(1)}, bf16[1024,1536]{1,0:T(8,128)(2,1)}, u32[]{:S(2)}) %copy-start.1) | copy-done | bytes 3145752
  49.8 0.0 copy-start.18
  49.8 0.9 copy-done.18
  50.7 6.6 %scan.2 = bf16[1024,768]{1,0:T(8,128)(2,1)S(1)} custom-call(bf16[1024,1536]{1,0:T(8,128)(2,1)S(1)} %copy-done.1, bf16[1024,128]{1,0:T(8,128)(2,1)S(1)} %get-tuple-element.47.bcs, f32[24,1024]{1,0:T(8,128)S(1)} %get-tuple-element.48.cum, f32[24,1024]{1,0:T(8,128)S(1)} %copy-done.18, bf16[1024,1536]{1,0:T(8,128)(2,1)S(1)} %get-tuple-element.50.gate, ...), custom_call_target="tpu_custom_call" | custom-call | flops 2147483648 | bytes 5242880 | tf_op jit(solution)/shard_map/scan/pallas_call | solution.py:535
  57.3 0.0 copy-start.9
  57.4 1.2 copy-done.9
  58.6 0.0 all-to-all-done.arrived
  58.6 1.2 relay.1
  59.7 0.0 copy-start.16
  59.8 0.7 copy-done.16
  60.4 7.2 %all-to-all-start.1 = ((bf16[16,16,384]{2,1,0:T(8,128)(2,1)}), bf16[16,16,384]{2,1,0:T(8,128)(2,1)}, u32[]{:S(2)}, u32[]{:S(2)}) async-start(bf16[16,16,384]{2,1,0:T(8,128)(2,1)} %copy-done.16), calls=%async_computation.1 | async-start | bytes 393216 | tf_op jit(solution)/shard_map/all_to_all | solution.py:772
  67.7 0.0 copy-start.2
  67.7 1.9 %copy-done.2 = bf16[1024,1536]{1,0:T(8,128)(2,1)S(1)} copy-done((bf16[1024,1536]{1,0:T(8,128)(2,1)S(1)}, bf16[1024,1536]{1,0:T(8,128)(2,1)}, u32[]{:S(2)}) %copy-start.2) | copy-done | bytes 3145752
  69.5 0.0 copy-start.19
  69.5 0.9 copy-done.19
  70.4 6.6 %scan.3 = (bf16[1024,768]{1,0:T(8,128)(2,1)S(1)}, bf16[1536,1536]{1,0:T(8,128)(2,1)S(1)}) custom-call(bf16[1024,1536]{1,0:T(8,128)(2,1)S(1)} %copy-done.2, bf16[1024,128]{1,0:T(8,128)(2,1)S(1)} %get-tuple-element.47.bcs, f32[24,1024]{1,0:T(8,128)S(1)} %get-tuple-element.48.cum, f32[24,1024]{1,0:T(8,128)S(1)} %copy-done.19, ...), custom_call_target="tpu_custom_call" | custom-call | flops 2147483648 | bytes 5242880 | tf_op jit(solution)/shard_map/scan/pallas_call | solution.py:535
  77.1 0.0 copy-start.3
  77.1 2.1 %copy-done.3 = bf16[1536,1536]{1,0:T(8,128)(2,1)} copy-done((bf16[1536,1536]{1,0:T(8,128)(2,1)}, bf16[1536,1536]{1,0:T(8,128)(2,1)S(1)}, u32[]{:S(2)}) %copy-start.3) | copy-done | bytes 4718616
  79.2 0.0 copy-start.14
  79.2 1.1 copy-done.14
  80.4 0.0 all-to-all-done.1.entering
  80.4 0.0 copy-start.4
  80.4 2.3 %copy-done.4 = bf16[1536,1536]{1,0:T(8,128)(2,1)S(1)} copy-done((bf16[1536,1536]{1,0:T(8,128)(2,1)S(1)}, bf16[1536,1536]{1,0:T(8,128)(2,1)}, u32[]{:S(2)}) %copy-start.4) | copy-done | bytes 4718616
  82.7 0.0 copy-start.7
  82.7 1.9 %copy-done.7 = bf16[1024,1536]{1,0:T(8,128)(2,1)S(1)} copy-done((bf16[1024,1536]{1,0:T(8,128)(2,1)S(1)}, bf16[1024,1536]{1,0:T(8,128)(2,1)}, u32[]{:S(2)}) %copy-start.7) | copy-done | bytes 3145752
  84.6 0.0 copy-start.10
  84.6 1.4 copy-done.10
  86.0 1.4 copy-done.15
  87.4 0.9 copy-done.22
  88.3 8.6 %finish.1 = (bf16[1024,896]{1,0:T(8,128)(2,1)S(1)}, bf16[8,128,1536]{2,1,0:T(8,128)(2,1)S(1)}) custom-call(bf16[8,128,768]{2,1,0:T(8,128)(2,1)S(1)} %bitcast.30, bf16[8,128,768]{2,1,0:T(8,128)(2,1)S(1)} %bitcast.33, bf16[8,128,1536]{2,1,0:T(8,128)(2,1)S(1)} %bitcast.27, bf16[8,128,128]{2,1,0:T(8,128)(2,1)S(1)} %bitcast.31, f32[24,1024]{1,0:T(8,128)S(1)} %copy-done.22, ...), custom_call_target="tpu_custom_call" | custom-call | flops 2818572288 | bytes 16777216 | tf_op jit(solution)/shard_map/finish/pallas_call | solution.py:631
  96.9 0.0 copy-start.11
  96.9 1.7 %copy-done.11 = bf16[8,128,1536]{2,1,0:T(8,128)(2,1)} copy-done((bf16[8,128,1536]{2,1,0:T(8,128)(2,1)}, bf16[8,128,1536]{2,1,0:T(8,128)(2,1)S(1)}, u32[]{:S(2)}) %copy-start.11) | copy-done | bytes 3145752
  98.6 1.2 copy-done.13
  99.8 7.5 %all-to-all-start.2 = ((bf16[16,64,896]{2,1,0:T(8,128)(2,1)}), bf16[16,64,896]{2,1,0:T(8,128)(2,1)}, u32[]{:S(2)}, u32[]{:S(2)}) async-start(bf16[16,64,896]{2,1,0:T(8,128)(2,1)} %bitcast.32), calls=%async_computation.2 | async-start | bytes 3670016 | tf_op jit(solution)/shard_map/all_to_all | solution.py:788
  107.3 0.0 copy-done.8
  107.3 0.0 copy-start.5
  107.3 2.3 %copy-done.5 = bf16[1536,1536]{1,0:T(8,128)(2,1)S(1)} copy-done((bf16[1536,1536]{1,0:T(8,128)(2,1)S(1)}, bf16[1536,1536]{1,0:T(8,128)(2,1)}, u32[]{:S(2)}) %copy-start.5) | copy-done | bytes 4718616
  109.6 1.9 %copy-done.12 = bf16[8,128,1536]{2,1,0:T(8,128)(2,1)S(1)} copy-done((bf16[8,128,1536]{2,1,0:T(8,128)(2,1)S(1)}, bf16[8,128,1536]{2,1,0:T(8,128)(2,1)}, u32[]{:S(2)}) %copy-start.12) | copy-done | bytes 3145752
  111.5 4.6 %rest.1 = bf16[1024,640]{1,0:T(8,128)(2,1)} custom-call(bf16[8,128,1536]{2,1,0:T(8,128)(2,1)S(1)} %copy-done.12, bf16[8,128,1536]{2,1,0:T(8,128)(2,1)S(1)} %bitcast.29, bf16[1536,1536]{1,0:T(8,128)(2,1)S(1)} %copy-done.5), custom_call_target="tpu_custom_call" | custom-call | flops 2013265920 | bytes 8388608 | tf_op jit(solution)/shard_map/rest/pallas_call | solution.py:678
  116.2 0.0 collective-permute-start.3
  116.2 16.2 %all-to-all-done.2 = bf16[16,64,896]{2,1,0:T(8,128)(2,1)} async-done(((bf16[16,64,896]{2,1,0:T(8,128)(2,1)}), bf16[16,64,896]{2,1,0:T(8,128)(2,1)}, u32[]{:S(2)}, u32[]{:S(2)}) %all-to-all-start.2) | async-done | bytes 1835040 | tf_op jit(solution)/shard_map/all_to_all | solution.py:788
  132.3 0.0 collective-permute-start.2
  132.3 2.4 %collective-permute-done.3 = bf16[16,64,640]{2,1,0:T(8,128)(2,1)} collective-permute-done((bf16[16,64,640]{2,1,0:T(8,128)(2,1)}, bf16[16,64,640]{2,1,0:T(8,128)(2,1)}, u32[]{:S(2)}, u32[]{:S(2)}) %collective-permute-start.3) | collective-permute-done | bytes 1310752 | tf_op jit(solution)/shard_map/ppermute | solution.py:789
  134.7 25.0 %all_to_all.20 = bf16[16,64,640]{2,1,0:T(8,128)(2,1)S(1)} all-to-all(bf16[16,64,640]{2,1,0:T(8,128)(2,1)} %collective-permute-done.3), channel_id=1, replica_groups=mesh['segment'=8,'band'=16] {'band'}, dimensions={0} | all-to-all | bytes 2621440 | tf_op jit(solution)/shard_map/all_to_all | solution.py:790
  159.8 0.0 collective-permute-done.2
  159.8 2.0 %copy_bitcast_fusion = bf16[1,8,128,1536]{3,2,1,0:T(8,128)(2,1)} fusion(bf16[16,64,640]{2,1,0:T(8,128)(2,1)S(1)} %all_to_all.20, bf16[16,64,896]{2,1,0:T(8,128)(2,1)S(1)} %collective-permute-done.2), kind=kLoop, calls=%fused_computation.1 | loop fusion | flops 6291456 | bytes 6291456 | tf_op jit(solution)/shard_map/reshape | solution.py:794
  (6 shorter events, 0.0 us)
Async XLA Ops:
  1.2 30.0 %collective-permute-start.1 = (bf16[128,1536]{1,0:T(8,128)(2,1)S(1)}, bf16[128,1536]{1,0:T(8,128)(2,1)S(1)}, u32[]{:S(2)}, u32[]{:S(2)}) collective-permute-start(bf16[128,1536]{1,0:T(8,128)(2,1)S(1)} %get-tuple-element.63), channel_id=1, source_target_pairs={{1,0},{2,1},{3,2},{4,3},{5,4},{6,5},{7,6},{8,7},{9,8},{10,9},{11,1... | collective-permute-start | bytes 1179656 | tf_op jit(solution)/shard_map/ppermute | solution.py:712
  2.5 28.7 %collective-permute-start = (bf16[128,1536]{1,0:T(8,128)(2,1)S(1)}, bf16[128,1536]{1,0:T(8,128)(2,1)S(1)}, u32[]{:S(2)}, u32[]{:S(2)}) collective-permute-start(bf16[128,1536]{1,0:T(8,128)(2,1)S(1)} %get-tuple-element.64), channel_id=1, source_target_pairs={{0,1},{1,2},{2,3},{3,4},{4,5},{5,6},{6,7},{7,8},{8,9},{9,10},{10,1... | collective-permute-start | bytes 1179656 | tf_op jit(solution)/shard_map/ppermute | solution.py:711
  29.5 1.7 %copy-start.6 = (bf16[1024,1536]{1,0:T(8,128)(2,1)}, bf16[1024,1536]{1,0:T(8,128)(2,1)S(1)}, u32[]{:S(2)}) copy-start(bf16[1024,1536]{1,0:T(8,128)(2,1)S(1)} %get-tuple-element.59) | copy-start | bytes 9437188
  31.1 4.3 %copy-start.17 = (f32[24,1024]{1,0:T(8,128)}, f32[24,1024]{1,0:T(8,128)S(1)}, u32[]{:S(2)}) copy-start(f32[24,1024]{1,0:T(8,128)S(1)} %get-tuple-element.49.dt) | copy-start | bytes 294916
  31.1 4.3 %copy-start.21 = (f32[24,1024]{1,0:T(8,128)}, f32[24,1024]{1,0:T(8,128)S(1)}, u32[]{:S(2)}) copy-start(f32[24,1024]{1,0:T(8,128)S(1)} %get-tuple-element.56.band_decay) | copy-start | bytes 294916
  35.4 1.7 %copy-start = (bf16[1024,1536]{1,0:T(8,128)(2,1)}, bf16[1024,1536]{1,0:T(8,128)(2,1)S(1)}, u32[]{:S(2)}) copy-start(bf16[1024,1536]{1,0:T(8,128)(2,1)S(1)} %get-tuple-element.46.x) | copy-start | bytes 9437188
  37.1 0.7 copy-start.20
  37.8 20.8 %all-to-all-start = ((bf16[16,16,512]{2,1,0:T(8,128)(2,1)}), bf16[16,16,512]{2,1,0:T(8,128)(2,1)}, u32[]{:S(2)}, u32[]{:S(2)}) async-start(bf16[16,16,512]{2,1,0:T(8,128)(2,1)} %bitcast.34), calls=%async_computation | async-start | bytes 524288 | tf_op jit(solution)/shard_map/all_to_all | solution.py:767
  47.9 1.9 %copy-start.1 = (bf16[1024,1536]{1,0:T(8,128)(2,1)S(1)}, bf16[1024,1536]{1,0:T(8,128)(2,1)}, u32[]{:S(2)}) copy-start(bf16[1024,1536]{1,0:T(8,128)(2,1)} %copy-done) | copy-start | bytes 9437188
  49.8 0.9 copy-start.18
  57.3 1.2 copy-start.9
  59.7 0.7 copy-start.16
  60.4 19.9 %all-to-all-start.1 = ((bf16[16,16,384]{2,1,0:T(8,128)(2,1)}), bf16[16,16,384]{2,1,0:T(8,128)(2,1)}, u32[]{:S(2)}, u32[]{:S(2)}) async-start(bf16[16,16,384]{2,1,0:T(8,128)(2,1)} %copy-done.16), calls=%async_computation.1 | async-start | bytes 393216 | tf_op jit(solution)/shard_map/all_to_all | solution.py:772
  67.7 1.9 %copy-start.2 = (bf16[1024,1536]{1,0:T(8,128)(2,1)S(1)}, bf16[1024,1536]{1,0:T(8,128)(2,1)}, u32[]{:S(2)}) copy-start(bf16[1024,1536]{1,0:T(8,128)(2,1)} %copy-done) | copy-start | bytes 9437188
  69.5 0.9 copy-start.19
  77.1 2.1 %copy-start.3 = (bf16[1536,1536]{1,0:T(8,128)(2,1)}, bf16[1536,1536]{1,0:T(8,128)(2,1)S(1)}, u32[]{:S(2)}) copy-start(bf16[1536,1536]{1,0:T(8,128)(2,1)S(1)} %get-tuple-element.60.w) | copy-start | bytes 14155780
  79.2 1.1 copy-start.14
  80.4 2.3 %copy-start.4 = (bf16[1536,1536]{1,0:T(8,128)(2,1)S(1)}, bf16[1536,1536]{1,0:T(8,128)(2,1)}, u32[]{:S(2)}) copy-start(bf16[1536,1536]{1,0:T(8,128)(2,1)} %copy-done.3) | copy-start | bytes 14155780
  82.7 1.9 %copy-start.7 = (bf16[1024,1536]{1,0:T(8,128)(2,1)S(1)}, bf16[1024,1536]{1,0:T(8,128)(2,1)}, u32[]{:S(2)}) copy-start(bf16[1024,1536]{1,0:T(8,128)(2,1)} %copy-done.6) | copy-start | bytes 9437188
  84.6 1.4 copy-start.10
  86.0 1.4 copy-start.15
  87.4 0.9 copy-start.22
  96.9 1.7 %copy-start.11 = (bf16[8,128,1536]{2,1,0:T(8,128)(2,1)}, bf16[8,128,1536]{2,1,0:T(8,128)(2,1)S(1)}, u32[]{:S(2)}) copy-start(bf16[8,128,1536]{2,1,0:T(8,128)(2,1)S(1)} %get-tuple-element.62.hidden) | copy-start | bytes 9437188
  98.6 1.2 copy-start.13
  99.8 7.5 %copy-start.8 = (bf16[1024,1536]{1,0:T(8,128)(2,1)S(1)}, bf16[1024,1536]{1,0:T(8,128)(2,1)}, u32[]{:S(2)}) copy-start(bf16[1024,1536]{1,0:T(8,128)(2,1)} %copy-done.6) | copy-start | bytes 9437188
  99.8 32.5 %all-to-all-start.2 = ((bf16[16,64,896]{2,1,0:T(8,128)(2,1)}), bf16[16,64,896]{2,1,0:T(8,128)(2,1)}, u32[]{:S(2)}, u32[]{:S(2)}) async-start(bf16[16,64,896]{2,1,0:T(8,128)(2,1)} %bitcast.32), calls=%async_computation.2 | async-start | bytes 3670016 | tf_op jit(solution)/shard_map/all_to_all | solution.py:788
  107.3 2.3 %copy-start.5 = (bf16[1536,1536]{1,0:T(8,128)(2,1)S(1)}, bf16[1536,1536]{1,0:T(8,128)(2,1)}, u32[]{:S(2)}) copy-start(bf16[1536,1536]{1,0:T(8,128)(2,1)} %copy-done.3) | copy-start | bytes 14155780
  109.6 1.9 %copy-start.12 = (bf16[8,128,1536]{2,1,0:T(8,128)(2,1)S(1)}, bf16[8,128,1536]{2,1,0:T(8,128)(2,1)}, u32[]{:S(2)}) copy-start(bf16[8,128,1536]{2,1,0:T(8,128)(2,1)} %copy-done.11) | copy-start | bytes 9437188
  116.2 18.6 %collective-permute-start.3 = (bf16[16,64,640]{2,1,0:T(8,128)(2,1)}, bf16[16,64,640]{2,1,0:T(8,128)(2,1)}, u32[]{:S(2)}, u32[]{:S(2)}) collective-permute-start(bf16[16,64,640]{2,1,0:T(8,128)(2,1)} %bitcast.16), channel_id=1, source_target_pairs={{0,16},{16,32},{32,48},{48,64},{64,80},{80,96},{96,112},{112,0},{1... | collective-permute-start | bytes 3932168 | tf_op jit(solution)/shard_map/ppermute | solution.py:789
  132.3 27.4 %collective-permute-start.2 = (bf16[16,64,896]{2,1,0:T(8,128)(2,1)}, bf16[16,64,896]{2,1,0:T(8,128)(2,1)S(1)}, u32[]{:S(2)}, u32[]{:S(2)}) collective-permute-start(bf16[16,64,896]{2,1,0:T(8,128)(2,1)} %all-to-all-done.2), channel_id=1, source_target_pairs={{0,16},{16,32},{32,48},{48,64},{64,80},{80,96},{96,112},{112,0},{1... | collective-permute-start | bytes 5505032 | tf_op jit(solution)/shard_map/ppermute | solution.py:791

commit v5 on v4

--- a/solution.py
+++ b/solution.py
@@ -110,10 +110,8 @@
     rate,
     taps_ref,
     bias,
-    skip,
-    out_gain,
     x,
-    gate,
+    gate_out,
     rim,
     bcs,
     rim_bc,
@@ -124,12 +122,11 @@
     total,
     mid,
     w_near,
-    tok_near,
     gain_near,
     taps_near,
     bias_near,
-    skip_near,
-    out_gain_near,
+    tok_near,
+    gate,
     normed,
     lines_a,
     lines_b,
@@ -140,6 +137,7 @@
     tok_sem,
     w_sem,
     w_g_sem,
+    gate_sem,
 ):
     def tokens_in(m):
         part = pl.ds(m * 256, 256)
@@ -152,6 +150,10 @@
     def gate_in(n):
         part = pl.ds(n * 512, 512)
         return pltpu.make_async_copy(w_g.at[:, part], w_g_near.at[:, part], w_g_sem.at[n])
+
+    def send_gate(n):
+        part = pl.ds(n * 512, 512)
+        return pltpu.make_async_copy(gate.at[:, part], gate_out.at[:, part], gate_sem.at[n])
 
     taps = [taps_ref[n] for n in range(9)]
 
@@ -198,8 +200,6 @@
     gain_near[...] = gain[...]
     taps_near[...] = taps_ref[...]
     bias_near[...] = bias[...]
-    skip_near[...] = skip[...]
-    out_gain_near[...] = out_gain[...]
     for padded in (lines_a, lines_b, lines_bc):
         for n in range(ROWS):
             for k in range(padded.shape[0]):
@@ -270,6 +270,7 @@
         for side in range(2):
             multiply_gate(m, 0, side)
             inside(m, lines_a, 2, range(1 + 3 * side, 4 + 3 * side))
+    send_gate(0).start()
     for n in (1, 2):
         gate_in(n).wait()
         for m in range(4):
@@ -277,10 +278,13 @@
                 multiply_gate(m, n, side)
             if m < 3:
                 add_state((n - 1) * 3 + m)
-
-
-def project(tok, gain, w_xbc, w_gate, w_dt_t, dt_bias, rate, taps, conv_bias, skip, out_gain):
-    per_head = pltpu.VMEM((HEADS, LENGTH), F32)
+        send_gate(n).start()
+    for n in range(3):
+        send_gate(n).wait()
+
+
+def project(tok, gain, w_xbc, w_gate, w_dt_t, dt_bias, rate, taps, conv_bias):
+    per_head = pltpu.HBM((HEADS, LENGTH), F32)
     return pl.pallas_call(
         project_kernel,
         in_specs=[
@@ -293,31 +297,32 @@
             small(1, HEADS),
             small(9, 1, INNER + 128),
             small(1, INNER + 128),
-            small(1, HEADS),
-            small(1, INNER),
-        ],
-        out_specs=[kept] * 18,
+        ],
+        out_specs=[kept, far, kept, kept, kept]
+        + [small(HEADS, LENGTH)] * 2
+        + [kept]
+        + [small(HEADS, LENGTH)]
+        + [kept] * 6,
         out_shape=[
             pltpu.VMEM((LENGTH, INNER), BF16),
-            pltpu.VMEM((LENGTH, INNER), BF16),
+            pltpu.HBM((LENGTH, INNER), BF16),
             pltpu.VMEM((4 * LINE, INNER), BF16),
             pltpu.VMEM((LENGTH, 128), BF16),
             pltpu.VMEM((4 * LINE, 128), BF16),
             per_head,
             per_head,
-            per_head,
+            pltpu.VMEM((HEADS, LENGTH), F32),
             per_head,
             pltpu.VMEM((1, HEADS), F32),
             pltpu.VMEM((STATE, INNER), F32),
             pltpu.VMEM((D, INNER + 128), BF16),
-            pltpu.VMEM((LENGTH, D), BF16),
             pltpu.VMEM((1, D), F32),
             pltpu.VMEM((9, 1, INNER + 128), F32),
             pltpu.VMEM((1, INNER + 128), F32),
-            pltpu.VMEM((1, HEADS), F32),
-            pltpu.VMEM((1, INNER), F32),
         ],
         scratch_shapes=[
+            pltpu.VMEM((LENGTH, D), BF16),
+            pltpu.VMEM((LENGTH, INNER), BF16),
             pltpu.VMEM((LENGTH, D), BF16),
             pltpu.VMEM((4, ROWS, LINE + 16, 128), F32),
             pltpu.VMEM((4, ROWS, LINE + 16, 128), F32),
@@ -328,13 +333,14 @@
             pltpu.SemaphoreType.DMA((4,)),
             pltpu.SemaphoreType.DMA((4,)),
             pltpu.SemaphoreType.DMA((3,)),
+            pltpu.SemaphoreType.DMA((3,)),
         ],
         compiler_params=params(),
         cost_estimate=pl.CostEstimate(
             flops=2 * LENGTH * D * 3224, bytes_accessed=20 << 20, transcendentals=LENGTH * INNER
         ),
         name="project",
-    )(hbm(tok), hbm(gain), hbm(w_xbc), hbm(w_gate), *map(hbm, (w_dt_t, dt_bias, rate, taps, conv_bias, skip, out_gain)))
+    )(hbm(tok), hbm(gain), hbm(w_xbc), hbm(w_gate), *map(hbm, (w_dt_t, dt_bias, rate, taps, conv_bias)))
 
 
 def edge_kernel(
@@ -349,17 +355,28 @@
     band_tail,
     total,
     mid,
-    x_in,
-    bcs_in,
-    x,
+    x_near,
+    bcs_near,
+    x_out,
     bcs,
     pieces,
+    x,
     edge,
     lines,
     b_t,
     tails,
+    mid_sem,
+    edge_sem,
 ):
-    del x_in, bcs_in
+    inner_part = pl.ds(2 * LINE, (ROWS - 2) * LINE)
+    send_mid = pltpu.make_async_copy(x_near.at[inner_part, :], x_out.at[inner_part, :], mid_sem)
+    send_mid.start()
+
+    def send_edge(n):
+        rows, part = pl.ds(0, 2 * LINE), pl.ds(n * 512, 512)
+        return pltpu.make_async_copy(x.at[:, part], x_out.at[rows, part], edge_sem.at[n])
+
+    bcs[inner_part, :] = bcs_near[inner_part, :]
     taps = [taps_ref[n] for n in range(9)]
 
     def both(side, own, own_start, start, out, out_start, tiles):
@@ -407,7 +424,8 @@
         start = n * 512
         part = pl.ds(start, 512)
         both(dot(edge[...], w_near[:, part]).astype(BF16), rim, start, start, x, start, 4)
-        weighted = x[pl.ds(0, 2 * LINE), part].astype(F32) * dot(tails[...], head_spread(512, n * 8))
+        send_edge(n).start()
+        weighted = x[:, part].astype(F32) * dot(tails[...], head_spread(512, n * 8))
         state = mid[:, part] + dot(b_t[pl.ds(0, STATE), :], weighted.astype(BF16))
         for k in range(4):
             g, within = divmod(n * 4 + k, 3)
@@ -415,24 +433,29 @@
                 pieces[a, g, :, pl.ds(within * 128, 128)] = state[
                     16 * a : 16 * a + 16, k * 128 : (k + 1) * 128
                 ].astype(BF16)
+    send_mid.wait()
+    for n in range(3):
+        send_edge(n).wait()
 
 
 def edges(top, bottom, gain, w_near, rim, rim_bc, taps, conv_bias, band_tail, total, mid, x, bcs):
     return pl.pallas_call(
         edge_kernel,
         in_specs=[kept] * 13,
-        out_specs=[kept, kept, pl.BlockSpec(memory_space=pltpu.VMEM)],
+        out_specs=[far, small(LENGTH, 128), small(4, 4, 16, GROUP + 128)],
         out_shape=[
-            pltpu.VMEM((LENGTH, INNER), BF16),
-            pltpu.VMEM((LENGTH, 128), BF16),
-            jax.ShapeDtypeStruct((4, 4, 16, GROUP + 128), BF16),
-        ],
-        input_output_aliases={11: 0, 12: 1},
+            pltpu.HBM((LENGTH, INNER), BF16),
+            pltpu.HBM((LENGTH, 128), BF16),
+            pltpu.HBM((4, 4, 16, GROUP + 128), BF16),
+        ],
         scratch_shapes=[
+            pltpu.VMEM((2 * LINE, INNER), BF16),
             pltpu.VMEM((2 * LINE, D), BF16),
             pltpu.VMEM((4, 6, LINE + 16, 128), F32),
             pltpu.VMEM((128, 2 * LINE), BF16),
             pltpu.VMEM((2 * LINE, 2 * HEADS), BF16),
+            pltpu.SemaphoreType.DMA(()),
+            pltpu.SemaphoreType.DMA((3,)),
         ],
         compiler_params=params(),
         cost_estimate=pl.CostEstimate(
@@ -458,19 +481,64 @@
     )
 
 
-def scan_kernel(half, x, bcs, cum, dt, gate, skip, *refs):
-    if half:
-        w, out, w_near, direct, state, sums, steps, weights, b_t, c, w_sem = refs
-        fetch = pltpu.make_async_copy(w, w_near, w_sem)
-        fetch.start()
-    else:
-        out, direct, state, sums, steps, weights, b_t, c = refs
+def scan_kernel(
+    x_far,
+    bcs,
+    cum,
+    dt,
+    gate_far,
+    skip,
+    band_decay,
+    out_gain,
+    w_far,
+    tok_far,
+    out,
+    gate,
+    w_near,
+    tok_near,
+    bcs_near,
+    decay_near,
+    gain_near,
+    x,
+    direct,
+    state,
+    sums,
+    steps,
+    weights,
+    b_t,
+    c,
+    sem,
+    late_sem,
+):
+    def rows_of(place):
+        return pl.ds(pl.multiple_of(place * LINE, LINE), LINE)
+
+    def x_in(r):
+        rows = rows_of(lax.rem(r + 1, ROWS))
+        return pltpu.make_async_copy(x_far.at[rows, :], x.at[rows, :], sem.at[0, r])
+
+    def gate_in(r):
+        rows = rows_of(r)
+        return pltpu.make_async_copy(gate_far.at[rows, :], gate.at[rows, :], sem.at[1, r])
+
+    late = [
+        pltpu.make_async_copy(w_far, w_near, late_sem.at[0]),
+        pltpu.make_async_copy(tok_far, tok_near, late_sem.at[1]),
+    ]
+    for r in range(ROWS):
+        x_in(r).start()
+        gate_in(r).start()
+    for copy in late:
+        copy.start()
+    bcs_near[...] = bcs[...]
+    decay_near[...] = band_decay[...]
+    gain_near[...] = out_gain[...]
     lane = lax.broadcasted_iota(jnp.int32, (LINE, LINE), 1)
     row = lax.broadcasted_iota(jnp.int32, (LINE, LINE), 0)
     left = lane < WIDTH
     direct[...] = dot(
         two_terms(jnp.broadcast_to(upright(skip[...]), (HEADS, 8))),
-        head_spread(HALF, half * HEADS // 2),
+        head_spread(INNER, 0),
     )
     state[...] = jnp.zeros_like(state)
     for r in range(ROWS):
@@ -483,9 +551,8 @@
     for r in range(ROWS):
         weights[r] = jnp.where(row >= lane, dot(c[r], b_t[r]), 0.0)
 
-    def line(r, placed):
-        rows = pl.ds(pl.multiple_of(r * LINE, LINE), LINE)
-        placed_rows = pl.ds(pl.multiple_of(placed * LINE, LINE), LINE)
+    def line(r):
+        rows, placed_rows = rows_of(r), rows_of(lax.rem(r + 1, ROWS))
         sums_here, steps_here, weights_here = sums[r], steps[r], weights[r]
         sums_t = cum[:, rows] * LOG2E
         steps_t = dt[:, rows]
@@ -495,15 +562,14 @@
             decay = jnp.exp2(jnp.minimum(along - sums_t[h : h + 1], 0.0))
             return along, (decay * (weights_here * steps_t[h : h + 1])).astype(BF16)
 
-        for q in range(HEADS // 8):
+        for q in range(HEADS // 4):
             quad = pl.ds(q * 256, 256)
             carried = dot(c[r], state[:, quad].astype(BF16))
             tails, decays = [], []
             for p in (2 * q, 2 * q + 1):
                 part = pl.ds(p * 128, 128)
-                whole_part = pl.ds(half * HALF + p * 128, 128)
-                h = half * HEADS // 2 + 2 * p
-                values = x[placed_rows, whole_part].astype(F32)
+                h = 2 * p
+                values = x[placed_rows, part].astype(F32)
                 (along_a, mixing_a), (along_b, mixing_b) = mixing(h), mixing(h + 1)
                 columns = jnp.concatenate(
                     [jnp.where(left, values, 0.0), jnp.where(left, 0.0, values)], axis=0
@@ -516,43 +582,77 @@
                 decays.append(carry[LINE - 1 :])
                 side = slice((p % 2) * 128, (p % 2) * 128 + 128)
                 y = inner + carry * carried[:, side] + direct[0:1, part] * values
-                out[rows, part] = (y * gate[rows, whole_part].astype(F32)).astype(BF16)
+                out[rows, part] = (y * gate[rows, part].astype(F32)).astype(BF16)
             state[:, quad] = jnp.concatenate(decays, axis=1) * state[:, quad] + dot(
                 b_t[r], jnp.concatenate(tails, axis=1)
             )
 
     @pl.loop(0, ROWS // 2)
     def _(pair):
-        line(2 * pair, 2 * pair + 1)
-        line(2 * pair + 1, lax.rem(2 * pair + 2, ROWS))
-
-    if half:
-        fetch.wait()
-
-
-def scan(half, x, bcs, cum, dt, gate, skip, *w):
-    weights = [pltpu.VMEM((INNER, D), BF16)] * half
+        for r in (2 * pair, 2 * pair + 1):
+            x_in(r).wait()
+            gate_in(r).wait()
+        line(2 * pair)
+        line(2 * pair + 1)
+
+    for copy in late:
+        copy.wait()
+
+
+def scan(x, bcs, cum, dt, gate, skip, band_decay, out_gain, w_out, tok):
     return pl.pallas_call(
-        functools.partial(scan_kernel, half),
-        in_specs=[kept] * 6 + [far] * half,
-        out_specs=[kept] * (1 + half),
-        out_shape=[pltpu.VMEM((LENGTH, HALF), BF16)] + weights,
+        scan_kernel,
+        in_specs=[
+            far,
+            small(LENGTH, 128),
+            small(HEADS, LENGTH),
+            small(HEADS, LENGTH),
+            far,
+            small(1, HEADS),
+            small(HEADS, LENGTH),
+            small(1, INNER),
+            far,
+            far,
+        ],
+        out_specs=[kept] * 7,
+        out_shape=[
+            pltpu.VMEM((LENGTH, INNER), BF16),
+            pltpu.VMEM((LENGTH, INNER), BF16),
+            pltpu.VMEM((INNER, D), BF16),
+            pltpu.VMEM((ROWS, LINE, D), BF16),
+            pltpu.VMEM((LENGTH, 128), BF16),
+            pltpu.VMEM((HEADS, LENGTH), F32),
+            pltpu.VMEM((1, INNER), F32),
+        ],
         scratch_shapes=[
-            pltpu.VMEM((8, HALF), F32),
-            pltpu.VMEM((STATE, HALF), F32),
+            pltpu.VMEM((LENGTH, INNER), BF16),
+            pltpu.VMEM((8, INNER), F32),
+            pltpu.VMEM((STATE, INNER), F32),
             pltpu.VMEM((ROWS, LINE, HEADS), F32),
             pltpu.VMEM((ROWS, LINE, HEADS), F32),
             pltpu.VMEM((ROWS, LINE, LINE), F32),
             pltpu.VMEM((ROWS, STATE, LINE), BF16),
             pltpu.VMEM((ROWS, LINE, STATE), BF16),
-        ]
-        + [pltpu.SemaphoreType.DMA(())] * half,
+            pltpu.SemaphoreType.DMA((2, ROWS)),
+            pltpu.SemaphoreType.DMA((2,)),
+        ],
         compiler_params=params(),
         cost_estimate=pl.CostEstimate(
-            flops=2 << 30, bytes_accessed=5 << 20, transcendentals=LENGTH * LINE * HEADS // 2
+            flops=4 << 30, bytes_accessed=20 << 20, transcendentals=LENGTH * LINE * HEADS
         ),
         name="scan",
-    )(near(x), near(bcs), near(cum), near(dt), near(gate), near(skip), *map(hbm, w))
+    )(
+        hbm(x),
+        hbm(bcs),
+        hbm(cum),
+        hbm(dt),
+        hbm(gate),
+        hbm(skip),
+        hbm(band_decay),
+        hbm(out_gain),
+        hbm(w_out),
+        hbm(tok),
+    )
 
 
 def relay_kernel(arrived, out):
@@ -579,24 +679,24 @@
 def relay(arrived):
     return pl.pallas_call(
         relay_kernel,
-        out_shape=jax.ShapeDtypeStruct((BANDS, 16, GROUP), BF16),
+        out_specs=kept,
+        out_shape=pltpu.VMEM((BANDS, 16, GROUP), BF16),
         compiler_params=params(16),
         name="relay",
     )(arrived)
 
 
-def columns_out(values, tokens, turned, out, step):
+def columns_out(values, tokens, turned, out):
     values = values + tokens.astype(F32)
-    rows = pl.ds(pl.multiple_of(step * 256, 256), 256)
     for k in range(values.shape[1] // 128):
         part = slice(k * 128, (k + 1) * 128)
         for r in range(ROWS):
             turned[k, pl.ds(r, 32, stride=ROWS), :] = values[r * 32 : (r + 1) * 32, part]
-        out[rows, part] = turned[k].astype(BF16)
+        out[:, part] = turned[k].astype(BF16)
 
 
 def finish_kernel(
-    local_a, local_b, gate, bcs, band_decay, entering, gain, tok, w, out, hidden, spread, state, decays, turned
+    local, gate, bcs, band_decay, entering, gain, tok, w, out, hidden, spread, state, decays, turned
 ):
     step = pl.program_id(0)
 
@@ -614,28 +714,29 @@
     cells = lambda ref: ref[:, here, :].reshape(256, ref.shape[2])
     both = jnp.concatenate([bcs[1:, here, :], bcs[:1, here, :]], axis=0).reshape(256, 128)
     decay = dot(cells(decays), spread[...])
-    local = jnp.concatenate([cells(local_a), cells(local_b)], axis=1)
-    gated = local.astype(F32) + dot(both, state[...]) * decay * cells(gate).astype(F32)
+    gated = cells(local).astype(F32) + dot(both, state[...]) * decay * cells(gate).astype(F32)
     normed = rms(gated, gain[...]).astype(BF16)
-    hidden[:, here, :] = normed.reshape(ROWS, 32, INNER)
+    hidden[...] = normed.reshape(ROWS, 32, INNER)
     columns_out(
         dot(normed, w[:, pl.ds(0, FIRST)]),
         tok[:, here, pl.ds(0, FIRST)].reshape(256, FIRST),
         turned,
         out,
-        step,
-    )
-
-
-def finish(local_a, local_b, gate, bcs, band_decay, entering, gain, tok, w_near):
+    )
+
+
+def finish(local, gate, bcs, band_decay, entering, gain, tok, w_out):
     return pl.pallas_call(
         finish_kernel,
         grid=(LINE // 32,),
-        in_specs=[kept] * 5 + [whole(BANDS, 16, GROUP), kept, kept, kept],
-        out_specs=[kept, kept],
+        in_specs=[kept] * 8,
+        out_specs=[
+            pl.BlockSpec((256, FIRST), lambda i: (i, 0)),
+            pl.BlockSpec((ROWS, 32, INNER), lambda i: (0, i, 0)),
+        ],
         out_shape=[
-            pltpu.VMEM((LENGTH, FIRST), BF16),
-            pltpu.VMEM((ROWS, LINE, INNER), BF16),
+            pltpu.HBM((LENGTH, FIRST), BF16),
+            pltpu.HBM((ROWS, LINE, INNER), BF16),
         ],
         scratch_shapes=[
             pltpu.VMEM((2 * HEADS, INNER), BF16),
@@ -648,46 +749,52 @@
             flops=2 * LENGTH * D * FIRST, bytes_accessed=16 << 20, transcendentals=LENGTH
         ),
         name="finish",
-    )(
-        near(local_a),
-        near(local_b),
-        near(gate),
-        near(bcs),
-        near(band_decay),
-        entering,
-        near(gain),
-        near(tok),
-        near(w_near),
-    )
-
-
-def rest_kernel(hidden, tok, w, out, turned):
+    )(*map(near, (local, gate, bcs, band_decay, entering, gain, tok, w_out)))
+
+
+def rest_kernel(hidden, w_far, tok_far, out, turned, w, tok_all, sem):
     step = pl.program_id(0)
+    part = pl.ds(FIRST, D - FIRST)
+    fetch = [
+        pltpu.make_async_copy(w_far.at[:, part], w, sem.at[0]),
+        pltpu.make_async_copy(tok_far.at[:, :, part], tok_all, sem.at[1]),
+    ]
+
+    @pl.when(step == 0)
+    def _():
+        for copy in fetch:
+            copy.start()
+        for copy in fetch:
+            copy.wait()
+
     here = pl.ds(pl.multiple_of(step * 32, 32), 32)
-    part = pl.ds(FIRST, D - FIRST)
     columns_out(
-        dot(hidden[:, here, :].reshape(256, INNER), w[:, part]),
-        tok[:, here, part].reshape(256, D - FIRST),
+        dot(hidden[...].reshape(256, INNER), w[...]),
+        tok_all[:, here, :].reshape(256, D - FIRST),
         turned,
         out,
-        step,
-    )
-
-
-def rest(hidden, tok, w_near):
+    )
+
+
+def rest(hidden, tok, w_out):
     return pl.pallas_call(
         rest_kernel,
         grid=(LINE // 32,),
-        in_specs=[kept] * 3,
-        out_specs=kept,
-        out_shape=pltpu.VMEM((LENGTH, D - FIRST), BF16),
-        scratch_shapes=[pltpu.VMEM(((D - FIRST) // 128, 256, 128), F32)],
-        compiler_params=params(),
+        in_specs=[pl.BlockSpec((ROWS, 32, INNER), lambda i: (0, i, 0)), far, far],
+        out_specs=pl.BlockSpec((256, D - FIRST), lambda i: (i, 0)),
+        out_shape=pltpu.HBM((LENGTH, D - FIRST), BF16),
+        scratch_shapes=[
+            pltpu.VMEM(((D - FIRST) // 128, 256, 128), F32),
+            pltpu.VMEM((INNER, D - FIRST), BF16),
+            pltpu.VMEM((ROWS, LINE, D - FIRST), BF16),
+            pltpu.SemaphoreType.DMA((2,)),
+        ],
+        compiler_params=params(60),
         cost_estimate=pl.CostEstimate(
             flops=2 * LENGTH * D * (D - FIRST), bytes_accessed=8 << 20, transcendentals=0
         ),
         name="rest",
-    )(near(hidden), near(tok), near(w_near))
+    )(hidden, hbm(w_out), hbm(tok))
 
 
 def shards(
@@ -724,12 +831,9 @@
         total,
         mid,
         w_xbc_near,
-        tok_near,
         in_gain_near,
         taps_near,
         bias_near,
-        skip_near,
-        out_gain_near,
     ) = project(
         tok,
         in_gain,
@@ -740,8 +844,6 @@
         decay_rate,
         conv_w.swapaxes(0, 1),
         conv_bias,
-        skip,
-        out_gain,
     )
     x, bcs, pieces = edges(
         top,
@@ -765,28 +867,19 @@
         lax.ppermute, axis_name="segment", perm=[(i, (i + 1) % segments) for i in range(segments)]
     )
     arrived = swap(pieces.reshape(BANDS, 16, GROUP + 128))
-    (local_a,) = scan(0, x, bcs, cum, dt, gate, skip_near)
-    arrived, local_a = lax.optimization_barrier((arrived, local_a))
-    states = relay(arrived)
-    states, skip_b = lax.optimization_barrier((states, skip_near))
-    entering = swap(states)
-    local_b, w_out_near = scan(1, x, bcs, cum, dt, gate, skip_b, w_out[0])
+    local, gate, w_out_near, tok_near, bcs, band_decay, gain_near = scan(
+        x, bcs, cum, dt, gate, skip, band_decay, out_gain, w_out[0], cells
+    )
+    arrived, local = lax.optimization_barrier((arrived, local))
+    entering = swap(relay(arrived))
 
     grid = lambda a: a.reshape(ROWS, LINE, a.shape[-1])
     parted = lambda a: a.reshape(BANDS, LENGTH // BANDS, a.shape[-1])
     first, hidden = finish(
-        grid(local_a),
-        grid(local_b),
-        grid(gate),
-        grid(bcs),
-        band_decay,
-        entering,
-        out_gain_near,
-        grid(tok_near),
-        w_out_near,
+        grid(local), grid(gate), grid(bcs), band_decay, entering, gain_near, tok_near, w_out_near
     )
     first = swap(parted(first))
-    second = onward(parted(rest(hidden, grid(tok_near), w_out_near)))
+    second = onward(parted(rest(hidden, cells, w_out[0])))
     second = swap(second)
     first = onward(first)
     both = jnp.concatenate([first, second], axis=-1)

time: 163 us -> 155 us (0.951)
  local copies, waits for them, and re-layouts: 30.9 us -> 14.3 us
  blocking collectives: 25 us -> 40.1 us
  starting transfers between devices: 30.7 us -> 19.7 us
  Pallas kernels: 54.3 us -> 60.1 us
    unnamed x46 -> x16, local copies, waits for them, and re-layouts: 29.8 us -> 13.2 us
    all_to_all x0 -> x1, blocking collectives: none -> 15.1 us  [shards(): entering = swap(relay(arrived))]
    all_to_all x1 -> x0, starting transfers between devices: 7.22 us -> none  [shards(): entering = swap(states)]
    pallas_call x6 -> x5, Pallas kernels: 31.9 us -> 35.9 us  [the longest x1 13.3 us: scan(): pl.pallas_call(scan_kernel, in_specs=[far, small(LENGTH, 128), small(HEAD...]
    all_to_all x1, starting transfers between devices: 7.47 us -> 3.72 us  [shards(): first = swap(parted(first))]
    pallas_call x1, Pallas kernels: 22.4 us -> 24.1 us  [project(): pl.pallas_call(project_kernel, in_specs=[far, small(1, D), far, far, smal...]
  transfers between devices with their start and end apart: 7 -> 6, of which waited for: 2 -> 2; matrix products, arithmetic and copies ran while one was open for 0% -> 0% of each run, Pallas kernels for 25% -> 29%
where the time goes in v5:
time: 155 us
  Pallas kernels  60.1 us (39%)
  blocking collectives  40.1 us (26%)
  starting transfers between devices  19.7 us (13%)
  waiting for transfers between devices  18.4 us (12%)
  local copies, waits for them, and re-layouts  14.3 us (9%)
  other arithmetic  1.96 us (1%)
    all_to_all x1, blocking collectives, shards(): second = swap(second)  25 us
    pallas_call x1, Pallas kernels, project(): pl.pallas_call(project_kernel, in_specs=[far, small(1, D), far, far, smal...  24.1 us
    all_to_all x1, waiting for transfers between devices, shards(): first = swap(parted(first))  16.4 us
    all_to_all x1, blocking collectives, shards(): entering = swap(relay(arrived))  15.1 us
    pallas_call x1, Pallas kernels, scan(): pl.pallas_call(scan_kernel, in_specs=[far, small(LENGTH, 128), small(HEAD...  13.3 us
    unnamed x16, local copies, waits for them, and re-layouts  13.2 us
    all_to_all x1, starting transfers between devices, shards(): arrived = swap(pieces.reshape(BANDS, 16, GROUP + 128))  10.1 us
    pallas_call x1, Pallas kernels, finish(): pl.pallas_call(finish_kernel, grid=(LINE // 32,), in_specs=[kept] * 8, ou...  8.78 us
  transfers between devices with their start and end apart: 6, of which 2 were waited for; matrix products, arithmetic and copies ran while one was open for 0% of the time, Pallas kernels for 29%

profile of v5, /device:TPU:0, one launch (start us, length us, event | category | flops | bytes accessed | tf_op | source)
XLA Modules:
  0.0 154.7 jit_solution(14023099735784664813)
XLA Ops:
  0.0 1.2 slice_bitcast_fusion
  1.2 1.3 collective-permute-start.1
  2.5 4.6 %collective-permute-start = (bf16[128,1536]{1,0:T(8,128)(2,1)S(1)}, bf16[128,1536]{1,0:T(8,128)(2,1)S(1)}, u32[]{:S(2)}, u32[]{:S(2)}) collective-permute-start(bf16[128,1536]{1,0:T(8,128)(2,1)S(1)} %get-tuple-element.64), channel_id=1, source_target_pairs={{0,1},{1,2},{2,3},{3,4},{4,5},{5,6},{6,7},{7,8},{8,9},{9,10},{10,1... | collective-permute-start | bytes 1179656 | tf_op jit(solution)/shard_map/ppermute | solution.py:818
  7.0 24.1 %project.1 = (bf16[1024,1536]{1,0:T(8,128)(2,1)S(1)}, bf16[1024,1536]{1,0:T(8,128)(2,1)}, bf16[512,1536]{1,0:T(8,128)(2,1)S(1)}, bf16[1024,128]{1,0:T(8,128)(2,1...) custom-call(bf16[1024,1536]{1,0:T(8,128)(2,1)} %bitcast.29, ...), custom_call_target="tpu_custom_call" | custom-call | flops 10141827072 | bytes 20971520 | tf_op jit(solution)/shard_map/project/pallas_call | solution.py:288
  31.2 0.0 collective-permute-done.1.bottom
  31.2 0.0 collective-permute-done.top
  31.2 5.8 %edges.1 = (bf16[1024,1536]{1,0:T(8,128)(2,1)}, bf16[1024,128]{1,0:T(8,128)(2,1)}, bf16[4,4,16,512]{3,2,1,0:T(8,128)(2,1)}) custom-call(bf16[128,1536]{1,0:T(8,128)(2,1)S(1)} %collective-permute-done.top, bf16[128,1536]{1,0:T(8,128)(2,1)S(1)} %collective-permute-done.1.bottom, f32[1,1536]{1,0:T(1,128)S(1)} %get-tuple-element.34.gain, ...), custom_call_target="tpu_custom_call" | custom-call | flops 1325662208 | bytes 10485760 | tf_op jit(solution)/shard_map/edges/pallas_call | solution.py:442
  37.0 10.1 %all-to-all-start = ((bf16[16,16,512]{2,1,0:T(8,128)(2,1)}), bf16[16,16,512]{2,1,0:T(8,128)(2,1)S(1)}, u32[]{:S(2)}, u32[]{:S(2)}) async-start(bf16[16,16,512]{2,1,0:T(8,128)(2,1)} %bitcast.36), calls=%async_computation | async-start | bytes 524288 | tf_op jit(solution)/shard_map/all_to_all | solution.py:869
  47.1 13.3 %scan.1 = (bf16[1024,1536]{1,0:T(8,128)(2,1)S(1)}, bf16[1024,1536]{1,0:T(8,128)(2,1)S(1)}, bf16[1536,1536]{1,0:T(8,128)(2,1)S(1)}, bf16[8,128,1536]{2,1,0:T(8,12...) custom-call(bf16[1024,1536]{1,0:T(8,128)(2,1)} %get-tuple-element.46.x_far, ...), custom_call_target="tpu_custom_call" | custom-call | flops 4294967296 | bytes 20971520 | tf_op jit(solution)/shard_map/scan/pallas_call | solution.py:603
  60.4 0.0 copy-start
  60.4 2.1 %copy-done = bf16[1536,1536]{1,0:T(8,128)(2,1)} copy-done((bf16[1536,1536]{1,0:T(8,128)(2,1)}, bf16[1536,1536]{1,0:T(8,128)(2,1)S(1)}, u32[]{:S(2)}) %copy-start) | copy-done | bytes 4718616
  62.5 0.0 copy-start.2
  62.5 1.7 %copy-done.2 = bf16[1024,1536]{1,0:T(8,128)(2,1)} copy-done((bf16[1024,1536]{1,0:T(8,128)(2,1)}, bf16[1024,1536]{1,0:T(8,128)(2,1)S(1)}, u32[]{:S(2)}) %copy-start.2) | copy-done | bytes 3145752
  64.1 0.0 copy-start.4
  64.1 1.6 %copy-done.4 = bf16[8,128,1536]{2,1,0:T(8,128)(2,1)} copy-done((bf16[8,128,1536]{2,1,0:T(8,128)(2,1)}, bf16[8,128,1536]{2,1,0:T(8,128)(2,1)S(1)}, u32[]{:S(2)}) %copy-start.4) | copy-done | bytes 3145752
  65.8 0.0 copy-start.6
  65.8 0.7 copy-done.6
  66.5 0.0 all-to-all-done.arrived
  66.5 0.2 relay.1
  66.7 15.1 %all_to_all.20.entering = bf16[16,16,384]{2,1,0:T(8,128)(2,1)S(1)} all-to-all(bf16[16,16,384]{2,1,0:T(8,128)(2,1)S(1)} %relay.1), channel_id=1, replica_groups=mesh['segment'=8,'band'=16] {'band'}, dimensions={0} | all-to-all | bytes 393216 | tf_op jit(solution)/shard_map/all_to_all | solution.py:874
  81.8 0.0 copy-start.1
  81.8 2.3 %copy-done.1 = bf16[1536,1536]{1,0:T(8,128)(2,1)S(1)} copy-done((bf16[1536,1536]{1,0:T(8,128)(2,1)S(1)}, bf16[1536,1536]{1,0:T(8,128)(2,1)}, u32[]{:S(2)}) %copy-start.1) | copy-done | bytes 4718616
  84.1 0.0 copy-start.3
  84.1 1.9 %copy-done.3 = bf16[1024,1536]{1,0:T(8,128)(2,1)S(1)} copy-done((bf16[1024,1536]{1,0:T(8,128)(2,1)S(1)}, bf16[1024,1536]{1,0:T(8,128)(2,1)}, u32[]{:S(2)}) %copy-start.3) | copy-done | bytes 3145752
  86.0 0.0 copy-start.5
  86.0 1.9 %copy-done.5 = bf16[8,128,1536]{2,1,0:T(8,128)(2,1)S(1)} copy-done((bf16[8,128,1536]{2,1,0:T(8,128)(2,1)S(1)}, bf16[8,128,1536]{2,1,0:T(8,128)(2,1)}, u32[]{:S(2)}) %copy-start.5) | copy-done | bytes 3145752
  87.9 0.0 copy-start.7
  87.9 0.9 copy-done.7
  88.9 8.8 %finish.1 = (bf16[1024,896]{1,0:T(8,128)(2,1)}, bf16[8,128,1536]{2,1,0:T(8,128)(2,1)}) custom-call(bf16[8,128,1536]{2,1,0:T(8,128)(2,1)S(1)} %bitcast.26, bf16[8,128,1536]{2,1,0:T(8,128)(2,1)S(1)} %bitcast.27, bf16[8,128,128]{2,1,0:T(8,128)(2,1)S(1)} %bitcast.28, f32[24,1024]{1,0:T(8,128)S(1)} %get-tuple-element.56.band_decay, ...), custom_call_target="tpu_custom_call" | custom-call | flops 2818572288 | bytes 16777216 | tf_op jit(solution)/shard_map/finish/pallas_call | solution.py:729
  97.6 3.7 %all-to-all-start.2 = ((bf16[16,64,896]{2,1,0:T(8,128)(2,1)}), bf16[16,64,896]{2,1,0:T(8,128)(2,1)S(1)}, u32[]{:S(2)}, u32[]{:S(2)}) async-start(bf16[16,64,896]{2,1,0:T(8,128)(2,1)} %bitcast.34), calls=%async_computation.2 | async-start | bytes 3670016 | tf_op jit(solution)/shard_map/all_to_all | solution.py:881
  101.4 7.9 %rest.1 = bf16[1024,640]{1,0:T(8,128)(2,1)} custom-call(bf16[8,128,1536]{2,1,0:T(8,128)(2,1)} %get-tuple-element.62.hidden, bf16[1536,1536]{1,0:T(8,128)(2,1)} %bitcast.33, bf16[8,128,1536]{2,1,0:T(8,128)(2,1)} %bitcast.31), custom_call_target="tpu_custom_call" | custom-call | flops 2013265920 | bytes 8388608 | tf_op jit(solution)/shard_map/rest/pallas_call | solution.py:780
  109.3 0.0 collective-permute-start.3
  109.3 16.4 %all-to-all-done.2 = bf16[16,64,896]{2,1,0:T(8,128)(2,1)S(1)} async-done(((bf16[16,64,896]{2,1,0:T(8,128)(2,1)}), bf16[16,64,896]{2,1,0:T(8,128)(2,1)S(1)}, u32[]{:S(2)}, u32[]{:S(2)}) %all-to-all-start.2) | async-done | bytes 1835040 | tf_op jit(solution)/shard_map/all_to_all | solution.py:881
  125.7 0.0 collective-permute-start.2
  125.7 2.0 %collective-permute-done.3 = bf16[16,64,640]{2,1,0:T(8,128)(2,1)S(1)} collective-permute-done((bf16[16,64,640]{2,1,0:T(8,128)(2,1)}, bf16[16,64,640]{2,1,0:T(8,128)(2,1)S(1)}, u32[]{:S(2)}, u32[]{:S(2)}) %collective-permute-start.3) | collective-permute-done | bytes 1310752 | tf_op jit(solution)/shard_map/ppermute | solution.py:882
  127.7 25.0 %all_to_all.21 = bf16[16,64,640]{2,1,0:T(8,128)(2,1)S(1)} all-to-all(bf16[16,64,640]{2,1,0:T(8,128)(2,1)S(1)} %collective-permute-done.3), channel_id=1, replica_groups=mesh['segment'=8,'band'=16] {'band'}, dimensions={0} | all-to-all | bytes 2621440 | tf_op jit(solution)/shard_map/all_to_all | solution.py:883
  152.7 0.0 collective-permute-done.2
  152.8 2.0 %copy_bitcast_fusion = bf16[1,8,128,1536]{3,2,1,0:T(8,128)(2,1)} fusion(bf16[16,64,640]{2,1,0:T(8,128)(2,1)S(1)} %all_to_all.21, bf16[16,64,896]{2,1,0:T(8,128)(2,1)S(1)} %collective-permute-done.2), kind=kLoop, calls=%fused_computation.1 | loop fusion | flops 6291456 | bytes 6291456 | tf_op jit(solution)/shard_map/reshape | solution.py:887
Async XLA Ops:
  1.2 30.0 %collective-permute-start.1 = (bf16[128,1536]{1,0:T(8,128)(2,1)S(1)}, bf16[128,1536]{1,0:T(8,128)(2,1)S(1)}, u32[]{:S(2)}, u32[]{:S(2)}) collective-permute-start(bf16[128,1536]{1,0:T(8,128)(2,1)S(1)} %get-tuple-element.63), channel_id=1, source_target_pairs={{1,0},{2,1},{3,2},{4,3},{5,4},{6,5},{7,6},{8,7},{9,8},{10,9},{11,1... | collective-permute-start | bytes 1179656 | tf_op jit(solution)/shard_map/ppermute | solution.py:819
  2.5 28.7 %collective-permute-start = (bf16[128,1536]{1,0:T(8,128)(2,1)S(1)}, bf16[128,1536]{1,0:T(8,128)(2,1)S(1)}, u32[]{:S(2)}, u32[]{:S(2)}) collective-permute-start(bf16[128,1536]{1,0:T(8,128)(2,1)S(1)} %get-tuple-element.64), channel_id=1, source_target_pairs={{0,1},{1,2},{2,3},{3,4},{4,5},{5,6},{6,7},{7,8},{8,9},{9,10},{10,1... | collective-permute-start | bytes 1179656 | tf_op jit(solution)/shard_map/ppermute | solution.py:818
  37.0 29.5 %all-to-all-start = ((bf16[16,16,512]{2,1,0:T(8,128)(2,1)}), bf16[16,16,512]{2,1,0:T(8,128)(2,1)S(1)}, u32[]{:S(2)}, u32[]{:S(2)}) async-start(bf16[16,16,512]{2,1,0:T(8,128)(2,1)} %bitcast.36), calls=%async_computation | async-start | bytes 524288 | tf_op jit(solution)/shard_map/all_to_all | solution.py:869
  60.4 2.1 %copy-start = (bf16[1536,1536]{1,0:T(8,128)(2,1)}, bf16[1536,1536]{1,0:T(8,128)(2,1)S(1)}, u32[]{:S(2)}) copy-start(bf16[1536,1536]{1,0:T(8,128)(2,1)S(1)} %get-tuple-element.60.w) | copy-start | bytes 14155780
  62.5 1.7 %copy-start.2 = (bf16[1024,1536]{1,0:T(8,128)(2,1)}, bf16[1024,1536]{1,0:T(8,128)(2,1)S(1)}, u32[]{:S(2)}) copy-start(bf16[1024,1536]{1,0:T(8,128)(2,1)S(1)} %get-tuple-element.54) | copy-start | bytes 9437188
  64.1 1.6 %copy-start.4 = (bf16[8,128,1536]{2,1,0:T(8,128)(2,1)}, bf16[8,128,1536]{2,1,0:T(8,128)(2,1)S(1)}, u32[]{:S(2)}) copy-start(bf16[8,128,1536]{2,1,0:T(8,128)(2,1)S(1)} %get-tuple-element.59.tok) | copy-start | bytes 9437188
  65.8 0.7 copy-start.6
  81.8 2.3 %copy-start.1 = (bf16[1536,1536]{1,0:T(8,128)(2,1)S(1)}, bf16[1536,1536]{1,0:T(8,128)(2,1)}, u32[]{:S(2)}) copy-start(bf16[1536,1536]{1,0:T(8,128)(2,1)} %copy-done) | copy-start | bytes 14155780
  84.1 1.9 %copy-start.3 = (bf16[1024,1536]{1,0:T(8,128)(2,1)S(1)}, bf16[1024,1536]{1,0:T(8,128)(2,1)}, u32[]{:S(2)}) copy-start(bf16[1024,1536]{1,0:T(8,128)(2,1)} %copy-done.2) | copy-start | bytes 9437188
  86.0 1.9 %copy-start.5 = (bf16[8,128,1536]{2,1,0:T(8,128)(2,1)S(1)}, bf16[8,128,1536]{2,1,0:T(8,128)(2,1)}, u32[]{:S(2)}) copy-start(bf16[8,128,1536]{2,1,0:T(8,128)(2,1)} %copy-done.4) | copy-start | bytes 9437188
  87.9 0.9 copy-start.7
  97.6 28.1 %all-to-all-start.2 = ((bf16[16,64,896]{2,1,0:T(8,128)(2,1)}), bf16[16,64,896]{2,1,0:T(8,128)(2,1)S(1)}, u32[]{:S(2)}, u32[]{:S(2)}) async-start(bf16[16,64,896]{2,1,0:T(8,128)(2,1)} %bitcast.34), calls=%async_computation.2 | async-start | bytes 3670016 | tf_op jit(solution)/shard_map/all_to_all | solution.py:881
  109.3 18.5 %collective-permute-start.3 = (bf16[16,64,640]{2,1,0:T(8,128)(2,1)}, bf16[16,64,640]{2,1,0:T(8,128)(2,1)S(1)}, u32[]{:S(2)}, u32[]{:S(2)}) collective-permute-start(bf16[16,64,640]{2,1,0:T(8,128)(2,1)} %bitcast.35), channel_id=1, source_target_pairs={{0,16},{16,32},{32,48},{48,64},{64,80},{80,96},{96,112},{112,0},{1... | collective-permute-start | bytes 3932168 | tf_op jit(solution)/shard_map/ppermute | solution.py:882
  125.7 27.0 %collective-permute-start.2 = (bf16[16,64,896]{2,1,0:T(8,128)(2,1)S(1)}, bf16[16,64,896]{2,1,0:T(8,128)(2,1)S(1)}, u32[]{:S(2)}, u32[]{:S(2)}) collective-permute-start(bf16[16,64,896]{2,1,0:T(8,128)(2,1)S(1)} %all-to-all-done.2), channel_id=1, source_target_pairs={{0,16},{16,32},{32,48},{48,64},{64,80},{80,96},{96,112},{112,0},{1... | collective-permute-start | bytes 5505032 | tf_op jit(solution)/shard_map/ppermute | solution.py:884

commit v6 on v5

--- a/solution.py
+++ b/solution.py
@@ -488,17 +488,9 @@
     dt,
     gate_far,
     skip,
-    band_decay,
-    out_gain,
-    w_far,
-    tok_far,
+    out_far,
     out,
     gate,
-    w_near,
-    tok_near,
-    bcs_near,
-    decay_near,
-    gain_near,
     x,
     direct,
     state,
@@ -508,7 +500,6 @@
     b_t,
     c,
     sem,
-    late_sem,
 ):
     def rows_of(place):
         return pl.ds(pl.multiple_of(place * LINE, LINE), LINE)
@@ -521,18 +512,13 @@
         rows = rows_of(r)
         return pltpu.make_async_copy(gate_far.at[rows, :], gate.at[rows, :], sem.at[1, r])
 
-    late = [
-        pltpu.make_async_copy(w_far, w_near, late_sem.at[0]),
-        pltpu.make_async_copy(tok_far, tok_near, late_sem.at[1]),
-    ]
+    def send(r):
+        rows = rows_of(r)
+        return pltpu.make_async_copy(out.at[rows, :], out_far.at[rows, :], sem.at[2, r])
+
     for r in range(ROWS):
         x_in(r).start()
         gate_in(r).start()
-    for copy in late:
-        copy.start()
-    bcs_near[...] = bcs[...]
-    decay_near[...] = band_decay[...]
-    gain_near[...] = out_gain[...]
     lane = lax.broadcasted_iota(jnp.int32, (LINE, LINE), 1)
     row = lax.broadcasted_iota(jnp.int32, (LINE, LINE), 0)
     left = lane < WIDTH
@@ -592,14 +578,15 @@
         for r in (2 * pair, 2 * pair + 1):
             x_in(r).wait()
             gate_in(r).wait()
-        line(2 * pair)
-        line(2 * pair + 1)
-
-    for copy in late:
-        copy.wait()
-
-
-def scan(x, bcs, cum, dt, gate, skip, band_decay, out_gain, w_out, tok):
+        for r in (2 * pair, 2 * pair + 1):
+            line(r)
+            send(r).start()
+
+    for r in range(ROWS):
+        send(r).wait()
+
+
+def scan(x, bcs, cum, dt, gate, skip):
     return pl.pallas_call(
         scan_kernel,
         in_specs=[
@@ -609,22 +596,12 @@
             small(HEADS, LENGTH),
             far,
             small(1, HEADS),
-            small(HEADS, LENGTH),
-            small(1, INNER),
-            far,
-            far,
-        ],
-        out_specs=[kept] * 7,
-        out_shape=[
+        ],
+        out_specs=far,
+        out_shape=pltpu.HBM((LENGTH, INNER), BF16),
+        scratch_shapes=[
             pltpu.VMEM((LENGTH, INNER), BF16),
             pltpu.VMEM((LENGTH, INNER), BF16),
-            pltpu.VMEM((INNER, D), BF16),
-            pltpu.VMEM((ROWS, LINE, D), BF16),
-            pltpu.VMEM((LENGTH, 128), BF16),
-            pltpu.VMEM((HEADS, LENGTH), F32),
-            pltpu.VMEM((1, INNER), F32),
-        ],
-        scratch_shapes=[
             pltpu.VMEM((LENGTH, INNER), BF16),
             pltpu.VMEM((8, INNER), F32),
             pltpu.VMEM((STATE, INNER), F32),
@@ -633,26 +610,14 @@
             pltpu.VMEM((ROWS, LINE, LINE), F32),
             pltpu.VMEM((ROWS, STATE, LINE), BF16),
             pltpu.VMEM((ROWS, LINE, STATE), BF16),
-            pltpu.SemaphoreType.DMA((2, ROWS)),
-            pltpu.SemaphoreType.DMA((2,)),
-        ],
-        compiler_params=params(),
+            pltpu.SemaphoreType.DMA((3, ROWS)),
+        ],
+        compiler_params=params(48),
         cost_estimate=pl.CostEstimate(
             flops=4 << 30, bytes_accessed=20 << 20, transcendentals=LENGTH * LINE * HEADS
         ),
         name="scan",
-    )(
-        hbm(x),
-        hbm(bcs),
-        hbm(cum),
-        hbm(dt),
-        hbm(gate),
-        hbm(skip),
-        hbm(band_decay),
-        hbm(out_gain),
-        hbm(w_out),
-        hbm(tok),
-    )
+    )(*map(hbm, (x, bcs, cum, dt, gate, skip)))
 
 
 def relay_kernel(arrived, out):
@@ -686,70 +651,155 @@
     )(arrived)
 
 
-def columns_out(values, tokens, turned, out):
+def columns_out(values, tokens, turned, out, rows=slice(None)):
     values = values + tokens.astype(F32)
     for k in range(values.shape[1] // 128):
         part = slice(k * 128, (k + 1) * 128)
         for r in range(ROWS):
             turned[k, pl.ds(r, 32, stride=ROWS), :] = values[r * 32 : (r + 1) * 32, part]
-        out[:, part] = turned[k].astype(BF16)
+        out[rows, part] = turned[k].astype(BF16)
 
 
 def finish_kernel(
-    local, gate, bcs, band_decay, entering, gain, tok, w, out, hidden, spread, state, decays, turned
+    local_far,
+    gate_far,
+    bcs,
+    band_decay,
+    entering,
+    gain,
+    tok_far,
+    w_far,
+    out_far,
+    hidden_far,
+    local,
+    gate,
+    tok,
+    w,
+    out,
+    hidden,
+    spread,
+    state,
+    decays,
+    turned,
+    sem,
+    w_sem,
 ):
-    step = pl.program_id(0)
-
-    @pl.when(step == 0)
-    def _():
-        spread[...] = head_spread(INNER, 0)
-        state[pl.ds(0, STATE), :] = jnp.zeros((STATE, INNER), BF16)
-        for a in range(4):
-            for g in range(4):
-                state[pl.ds(STATE + 16 * a, 16), pl.ds(g * GROUP, GROUP)] = entering[4 * a + g]
-        for r in range(ROWS):
-            decays[r] = two_terms(band_decay[:, r * LINE : (r + 1) * LINE])
-
-    here = pl.ds(pl.multiple_of(step * 32, 32), 32)
-    cells = lambda ref: ref[:, here, :].reshape(256, ref.shape[2])
-    both = jnp.concatenate([bcs[1:, here, :], bcs[:1, here, :]], axis=0).reshape(256, 128)
-    decay = dot(cells(decays), spread[...])
-    gated = cells(local).astype(F32) + dot(both, state[...]) * decay * cells(gate).astype(F32)
-    normed = rms(gated, gain[...]).astype(BF16)
-    hidden[...] = normed.reshape(ROWS, 32, INNER)
-    columns_out(
-        dot(normed, w[:, pl.ds(0, FIRST)]),
-        tok[:, here, pl.ds(0, FIRST)].reshape(256, FIRST),
-        turned,
-        out,
-    )
+    def columns_of(step):
+        return pl.ds(pl.multiple_of(step * 32, 32), 32)
+
+    def rows_of(step):
+        return pl.ds(pl.multiple_of(step * 256, 256), 256)
+
+    def local_in(step):
+        here = columns_of(step)
+        return pltpu.make_async_copy(local_far.at[:, here, :], local.at[:, here, :], sem.at[0, step])
+
+    def gate_in(step):
+        here = columns_of(step)
+        return pltpu.make_async_copy(gate_far.at[:, here, :], gate.at[:, here, :], sem.at[1, step])
+
+    def tok_in(step):
+        here = columns_of(step)
+        return pltpu.make_async_copy(
+            tok_far.at[:, here, pl.ds(0, FIRST)], tok.at[:, here, :], sem.at[2, step]
+        )
+
+    def send_hidden(step):
+        here = columns_of(step)
+        return pltpu.make_async_copy(hidden.at[:, here, :], hidden_far.at[:, here, :], sem.at[3, step])
+
+    def send_out(step):
+        rows = rows_of(step)
+        return pltpu.make_async_copy(out.at[rows, :], out_far.at[rows, :], sem.at[4, step])
+
+    fetch = pltpu.make_async_copy(w_far.at[:, pl.ds(0, FIRST)], w, w_sem)
+    for step in range(4):
+        local_in(step).start()
+        gate_in(step).start()
+        if step == 0:
+            fetch.start()
+        tok_in(step).start()
+    spread[...] = head_spread(INNER, 0)
+    state[pl.ds(0, STATE), :] = jnp.zeros((STATE, INNER), BF16)
+    for a in range(4):
+        for g in range(4):
+            state[pl.ds(STATE + 16 * a, 16), pl.ds(g * GROUP, GROUP)] = entering[4 * a + g]
+    for r in range(ROWS):
+        decays[r] = two_terms(band_decay[:, r * LINE : (r + 1) * LINE])
+
+    @pl.loop(0, 4)
+    def _(step):
+        here = columns_of(step)
+        cells = lambda ref: ref[:, here, :].reshape(256, ref.shape[2])
+        both = jnp.concatenate([bcs[1:, here, :], bcs[:1, here, :]], axis=0).reshape(256, 128)
+        entered = dot(both, state[...]) * dot(cells(decays), spread[...])
+        local_in(step).wait()
+        gate_in(step).wait()
+        gated = cells(local).astype(F32) + entered * cells(gate).astype(F32)
+        normed = rms(gated, gain[...]).astype(BF16)
+        hidden[:, here, :] = normed.reshape(ROWS, 32, INNER)
+        send_hidden(step).start()
+
+        @pl.when(step == 0)
+        def _():
+            fetch.wait()
+
+        tok_in(step).wait()
+        columns_out(dot(normed, w[...]), cells(tok), turned, out, rows_of(step))
+        send_out(step).start()
+
+    for step in range(4):
+        send_hidden(step).wait()
+        send_out(step).wait()
 
 
 def finish(local, gate, bcs, band_decay, entering, gain, tok, w_out):
     return pl.pallas_call(
         finish_kernel,
-        grid=(LINE // 32,),
-        in_specs=[kept] * 8,
-        out_specs=[
-            pl.BlockSpec((256, FIRST), lambda i: (i, 0)),
-            pl.BlockSpec((ROWS, 32, INNER), lambda i: (0, i, 0)),
-        ],
+        in_specs=[
+            far,
+            far,
+            small(ROWS, LINE, 128),
+            small(HEADS, LENGTH),
+            kept,
+            small(1, INNER),
+            far,
+            far,
+        ],
+        out_specs=[far, far],
         out_shape=[
             pltpu.HBM((LENGTH, FIRST), BF16),
             pltpu.HBM((ROWS, LINE, INNER), BF16),
         ],
         scratch_shapes=[
+            pltpu.VMEM((ROWS, LINE, INNER), BF16),
+            pltpu.VMEM((ROWS, LINE, INNER), BF16),
+            pltpu.VMEM((ROWS, LINE, FIRST), BF16),
+            pltpu.VMEM((INNER, FIRST), BF16),
+            pltpu.VMEM((LENGTH, FIRST), BF16),
+            pltpu.VMEM((ROWS, LINE, INNER), BF16),
             pltpu.VMEM((2 * HEADS, INNER), BF16),
             pltpu.VMEM((2 * STATE, INNER), BF16),
             pltpu.VMEM((ROWS, LINE, 2 * HEADS), BF16),
             pltpu.VMEM((FIRST // 128, 256, 128), F32),
-        ],
-        compiler_params=params(),
+            pltpu.SemaphoreType.DMA((5, 4)),
+            pltpu.SemaphoreType.DMA(()),
+        ],
+        compiler_params=params(48),
         cost_estimate=pl.CostEstimate(
             flops=2 * LENGTH * D * FIRST, bytes_accessed=16 << 20, transcendentals=LENGTH
         ),
         name="finish",
-    )(*map(near, (local, gate, bcs, band_decay, entering, gain, tok, w_out)))
+    )(
+        hbm(local),
+        hbm(gate),
+        hbm(bcs),
+        hbm(band_decay),
+        near(entering),
+        hbm(gain),
+        hbm(tok),
+        hbm(w_out),
+    )
 
 
 def rest_kernel(hidden, w_far, tok_far, out, turned, w, tok_all, sem):
@@ -867,16 +917,14 @@
         lax.ppermute, axis_name="segment", perm=[(i, (i + 1) % segments) for i in range(segments)]
     )
     arrived = swap(pieces.reshape(BANDS, 16, GROUP + 128))
-    local, gate, w_out_near, tok_near, bcs, band_decay, gain_near = scan(
-        x, bcs, cum, dt, gate, skip, band_decay, out_gain, w_out[0], cells
-    )
+    local = scan(x, bcs, cum, dt, gate, skip)
     arrived, local = lax.optimization_barrier((arrived, local))
     entering = swap(relay(arrived))
 
     grid = lambda a: a.reshape(ROWS, LINE, a.shape[-1])
     parted = lambda a: a.reshape(BANDS, LENGTH // BANDS, a.shape[-1])
     first, hidden = finish(
-        grid(local), grid(gate), grid(bcs), band_decay, entering, gain_near, tok_near, w_out_near
+        grid(local), grid(gate), grid(bcs), band_decay, entering, out_gain, cells, w_out[0]
     )
     first = swap(parted(first))
     second = onward(parted(rest(hidden, cells, w_out[0])))

time: 155 us -> 146 us (0.942)
  local copies, waits for them, and re-layouts: 14.3 us -> 1.17 us
  Pallas kernels: 60.1 us -> 63.9 us
    unnamed x16 -> x0, local copies, waits for them, and re-layouts: 13.2 us -> none
    pallas_call x1, Pallas kernels: 8.78 us -> 12.1 us  [finish(): pl.pallas_call(finish_kernel, in_specs=[far, far, small(ROWS, LINE, 128),...]
  transfers between devices with their start and end apart: 6 -> 6, of which waited for: 2 -> 2; matrix products, arithmetic and copies ran while one was open for 0% -> 0% of each run, Pallas kernels for 29% -> 32%
where the time goes in v6:
time: 146 us; the launch traced here: 145 us
  Pallas kernels  63.9 us (44%)
  blocking collectives  40.1 us (27%)
  starting transfers between devices  19.7 us (13%)
  waiting for transfers between devices  18.4 us (13%)
  other arithmetic  1.96 us (1%)
    all_to_all x1, blocking collectives, shards(): second = swap(second)  25 us
    pallas_call x1, Pallas kernels, project(): pl.pallas_call(project_kernel, in_specs=[far, small(1, D), far, far, smal...  24.1 us
    all_to_all x1, waiting for transfers between devices, shards(): first = swap(parted(first))  16.4 us
    all_to_all x1, blocking collectives, shards(): entering = swap(relay(arrived))  15.1 us
    pallas_call x1, Pallas kernels, scan(): pl.pallas_call(scan_kernel, in_specs=[far, small(LENGTH, 128), small(HEAD...  13.8 us
    pallas_call x1, Pallas kernels, finish(): pl.pallas_call(finish_kernel, in_specs=[far, far, small(ROWS, LINE, 128),...  12.1 us
    all_to_all x1, starting transfers between devices, shards(): arrived = swap(pieces.reshape(BANDS, 16, GROUP + 128))  10.1 us
    pallas_call x1, Pallas kernels, rest(): pl.pallas_call(rest_kernel, grid=(LINE // 32,), in_specs=[pl.BlockSpec((R...  7.9 us
  transfers between devices with their start and end apart: 6, of which 2 were waited for; matrix products, arithmetic and copies ran while one was open for 0% of the time, Pallas kernels for 32%

profile of v6, /device:TPU:0, one launch (start us, length us, event | category | flops | bytes accessed | tf_op | source)
XLA Modules:
  0.0 145.4 jit_solution(4067742720971756720)
XLA Ops:
  0.0 1.2 slice_bitcast_fusion
  1.2 1.3 collective-permute-start.1
  2.5 4.6 %collective-permute-start = (bf16[128,1536]{1,0:T(8,128)(2,1)S(1)}, bf16[128,1536]{1,0:T(8,128)(2,1)S(1)}, u32[]{:S(2)}, u32[]{:S(2)}) collective-permute-start(bf16[128,1536]{1,0:T(8,128)(2,1)S(1)} %get-tuple-element.50), channel_id=1, source_target_pairs={{0,1},{1,2},{2,3},{3,4},{4,5},{5,6},{6,7},{7,8},{8,9},{9,10},{10,1... | collective-permute-start | bytes 1179656 | tf_op jit(solution)/shard_map/ppermute | solution.py:868
  7.0 24.1 %project.1 = (bf16[1024,1536]{1,0:T(8,128)(2,1)S(1)}, bf16[1024,1536]{1,0:T(8,128)(2,1)}, bf16[512,1536]{1,0:T(8,128)(2,1)S(1)}, bf16[1024,128]{1,0:T(8,128)(2,1...) custom-call(bf16[1024,1536]{1,0:T(8,128)(2,1)} %bitcast.28, ...), custom_call_target="tpu_custom_call" | custom-call | flops 10141827072 | bytes 20971520 | tf_op jit(solution)/shard_map/project/pallas_call | solution.py:288
  31.2 0.0 collective-permute-done.1.bottom
  31.2 0.0 collective-permute-done.top
  31.2 5.7 %edges.1 = (bf16[1024,1536]{1,0:T(8,128)(2,1)}, bf16[1024,128]{1,0:T(8,128)(2,1)}, bf16[4,4,16,512]{3,2,1,0:T(8,128)(2,1)}) custom-call(bf16[128,1536]{1,0:T(8,128)(2,1)S(1)} %collective-permute-done.top, bf16[128,1536]{1,0:T(8,128)(2,1)S(1)} %collective-permute-done.1.bottom, f32[1,1536]{1,0:T(1,128)S(1)} %get-tuple-element.27.gain, ...), custom_call_target="tpu_custom_call" | custom-call | flops 1325662208 | bytes 10485760 | tf_op jit(solution)/shard_map/edges/pallas_call | solution.py:442
  36.9 10.1 %all-to-all-start = ((bf16[16,16,512]{2,1,0:T(8,128)(2,1)}), bf16[16,16,512]{2,1,0:T(8,128)(2,1)S(1)}, u32[]{:S(2)}, u32[]{:S(2)}) async-start(bf16[16,16,512]{2,1,0:T(8,128)(2,1)} %bitcast.36), calls=%async_computation | async-start | bytes 524288 | tf_op jit(solution)/shard_map/all_to_all | solution.py:919
  47.0 13.8 %scan.1 = bf16[1024,1536]{1,0:T(8,128)(2,1)} custom-call(bf16[1024,1536]{1,0:T(8,128)(2,1)} %get-tuple-element.39.x_far, bf16[1024,128]{1,0:T(8,128)(2,1)} %get-tuple-element.40.bcs, f32[24,1024]{1,0:T(8,128)} %get-tuple-element.41.cum, f32[24,1024]{1,0:T(8,128)} %get-tuple-element.42.dt, bf16[1024,1536]{1,0:T(8,128)(2,1)} %get-tuple-element.43.gate_far, ...), custom_call_target="tpu_custom_call" | custom-call | flops 4294967296 | bytes 20971520 | tf_op jit(solution)/shard_map/scan/pallas_call | solution.py:590
  60.9 0.0 all-to-all-done.arrived
  60.9 0.2 relay.1
  61.1 15.1 %all_to_all.20.entering = bf16[16,16,384]{2,1,0:T(8,128)(2,1)S(1)} all-to-all(bf16[16,16,384]{2,1,0:T(8,128)(2,1)S(1)} %relay.1), channel_id=1, replica_groups=mesh['segment'=8,'band'=16] {'band'}, dimensions={0} | all-to-all | bytes 393216 | tf_op jit(solution)/shard_map/all_to_all | solution.py:922
  76.2 12.1 %finish.1 = (bf16[1024,896]{1,0:T(8,128)(2,1)}, bf16[8,128,1536]{2,1,0:T(8,128)(2,1)}) custom-call(bf16[8,128,1536]{2,1,0:T(8,128)(2,1)} %bitcast.32, bf16[8,128,1536]{2,1,0:T(8,128)(2,1)} %bitcast.31, bf16[8,128,128]{2,1,0:T(8,128)(2,1)} %bitcast.35, f32[24,1024]{1,0:T(8,128)} %get-tuple-element.45.band_decay, ...), custom_call_target="tpu_custom_call" | custom-call | flops 2818572288 | bytes 16777216 | tf_op jit(solution)/shard_map/finish/pallas_call | solution.py:757
  88.3 3.7 %all-to-all-start.2 = ((bf16[16,64,896]{2,1,0:T(8,128)(2,1)}), bf16[16,64,896]{2,1,0:T(8,128)(2,1)S(1)}, u32[]{:S(2)}, u32[]{:S(2)}) async-start(bf16[16,64,896]{2,1,0:T(8,128)(2,1)} %bitcast.33), calls=%async_computation.2 | async-start | bytes 3670016 | tf_op jit(solution)/shard_map/all_to_all | solution.py:929
  92.1 7.9 %rest.1 = bf16[1024,640]{1,0:T(8,128)(2,1)} custom-call(bf16[8,128,1536]{2,1,0:T(8,128)(2,1)} %get-tuple-element.48.hidden, bf16[1536,1536]{1,0:T(8,128)(2,1)} %bitcast.27, bf16[8,128,1536]{2,1,0:T(8,128)(2,1)} %bitcast.30), custom_call_target="tpu_custom_call" | custom-call | flops 2013265920 | bytes 8388608 | tf_op jit(solution)/shard_map/rest/pallas_call | solution.py:830
  100.0 0.0 collective-permute-start.3
  100.0 16.4 %all-to-all-done.2 = bf16[16,64,896]{2,1,0:T(8,128)(2,1)S(1)} async-done(((bf16[16,64,896]{2,1,0:T(8,128)(2,1)}), bf16[16,64,896]{2,1,0:T(8,128)(2,1)S(1)}, u32[]{:S(2)}, u32[]{:S(2)}) %all-to-all-start.2) | async-done | bytes 1835040 | tf_op jit(solution)/shard_map/all_to_all | solution.py:929
  116.4 0.0 collective-permute-start.2
  116.4 2.0 %collective-permute-done.3 = bf16[16,64,640]{2,1,0:T(8,128)(2,1)S(1)} collective-permute-done((bf16[16,64,640]{2,1,0:T(8,128)(2,1)}, bf16[16,64,640]{2,1,0:T(8,128)(2,1)S(1)}, u32[]{:S(2)}, u32[]{:S(2)}) %collective-permute-start.3) | collective-permute-done | bytes 1310752 | tf_op jit(solution)/shard_map/ppermute | solution.py:930
  118.4 25.0 %all_to_all.21 = bf16[16,64,640]{2,1,0:T(8,128)(2,1)S(1)} all-to-all(bf16[16,64,640]{2,1,0:T(8,128)(2,1)S(1)} %collective-permute-done.3), channel_id=1, replica_groups=mesh['segment'=8,'band'=16] {'band'}, dimensions={0} | all-to-all | bytes 2621440 | tf_op jit(solution)/shard_map/all_to_all | solution.py:931
  143.4 0.0 collective-permute-done.2
  143.4 2.0 %copy_bitcast_fusion = bf16[1,8,128,1536]{3,2,1,0:T(8,128)(2,1)} fusion(bf16[16,64,640]{2,1,0:T(8,128)(2,1)S(1)} %all_to_all.21, bf16[16,64,896]{2,1,0:T(8,128)(2,1)S(1)} %collective-permute-done.2), kind=kLoop, calls=%fused_computation.1 | loop fusion | flops 6291456 | bytes 6291456 | tf_op jit(solution)/shard_map/reshape | solution.py:935
Async XLA Ops:
  1.2 30.0 %collective-permute-start.1 = (bf16[128,1536]{1,0:T(8,128)(2,1)S(1)}, bf16[128,1536]{1,0:T(8,128)(2,1)S(1)}, u32[]{:S(2)}, u32[]{:S(2)}) collective-permute-start(bf16[128,1536]{1,0:T(8,128)(2,1)S(1)} %get-tuple-element.49), channel_id=1, source_target_pairs={{1,0},{2,1},{3,2},{4,3},{5,4},{6,5},{7,6},{8,7},{9,8},{10,9},{11,1... | collective-permute-start | bytes 1179656 | tf_op jit(solution)/shard_map/ppermute | solution.py:869
  2.5 28.7 %collective-permute-start = (bf16[128,1536]{1,0:T(8,128)(2,1)S(1)}, bf16[128,1536]{1,0:T(8,128)(2,1)S(1)}, u32[]{:S(2)}, u32[]{:S(2)}) collective-permute-start(bf16[128,1536]{1,0:T(8,128)(2,1)S(1)} %get-tuple-element.50), channel_id=1, source_target_pairs={{0,1},{1,2},{2,3},{3,4},{4,5},{5,6},{6,7},{7,8},{8,9},{9,10},{10,1... | collective-permute-start | bytes 1179656 | tf_op jit(solution)/shard_map/ppermute | solution.py:868
  36.9 23.9 %all-to-all-start = ((bf16[16,16,512]{2,1,0:T(8,128)(2,1)}), bf16[16,16,512]{2,1,0:T(8,128)(2,1)S(1)}, u32[]{:S(2)}, u32[]{:S(2)}) async-start(bf16[16,16,512]{2,1,0:T(8,128)(2,1)} %bitcast.36), calls=%async_computation | async-start | bytes 524288 | tf_op jit(solution)/shard_map/all_to_all | solution.py:919
  88.3 28.1 %all-to-all-start.2 = ((bf16[16,64,896]{2,1,0:T(8,128)(2,1)}), bf16[16,64,896]{2,1,0:T(8,128)(2,1)S(1)}, u32[]{:S(2)}, u32[]{:S(2)}) async-start(bf16[16,64,896]{2,1,0:T(8,128)(2,1)} %bitcast.33), calls=%async_computation.2 | async-start | bytes 3670016 | tf_op jit(solution)/shard_map/all_to_all | solution.py:929
  100.0 18.5 %collective-permute-start.3 = (bf16[16,64,640]{2,1,0:T(8,128)(2,1)}, bf16[16,64,640]{2,1,0:T(8,128)(2,1)S(1)}, u32[]{:S(2)}, u32[]{:S(2)}) collective-permute-start(bf16[16,64,640]{2,1,0:T(8,128)(2,1)} %bitcast.34), channel_id=1, source_target_pairs={{0,16},{16,32},{32,48},{48,64},{64,80},{80,96},{96,112},{112,0},{1... | collective-permute-start | bytes 3932168 | tf_op jit(solution)/shard_map/ppermute | solution.py:930
  116.4 27.1 %collective-permute-start.2 = (bf16[16,64,896]{2,1,0:T(8,128)(2,1)S(1)}, bf16[16,64,896]{2,1,0:T(8,128)(2,1)S(1)}, u32[]{:S(2)}, u32[]{:S(2)}) collective-permute-start(bf16[16,64,896]{2,1,0:T(8,128)(2,1)S(1)} %all-to-all-done.2), channel_id=1, source_target_pairs={{0,16},{16,32},{32,48},{48,64},{64,80},{80,96},{96,112},{112,0},{1... | collective-permute-start | bytes 5505032 | tf_op jit(solution)/shard_map/ppermute | solution.py:932

commit v7 on v4

--- a/solution.py
+++ b/solution.py
@@ -458,19 +458,20 @@
     )
 
 
-def scan_kernel(half, x, bcs, cum, dt, gate, skip, *refs):
-    if half:
-        w, out, w_near, direct, state, sums, steps, weights, b_t, c, w_sem = refs
-        fetch = pltpu.make_async_copy(w, w_near, w_sem)
-        fetch.start()
-    else:
-        out, direct, state, sums, steps, weights, b_t, c = refs
+def scan_kernel(
+    x, bcs, cum, dt, gate, skip, w_far, out, w_near, direct, state, sums, steps, weights, b_t, c, w_sem
+):
+    def rows_of(place):
+        return pl.ds(pl.multiple_of(place * LINE, LINE), LINE)
+
+    fetch = pltpu.make_async_copy(w_far, w_near, w_sem)
+    fetch.start()
     lane = lax.broadcasted_iota(jnp.int32, (LINE, LINE), 1)
     row = lax.broadcasted_iota(jnp.int32, (LINE, LINE), 0)
     left = lane < WIDTH
     direct[...] = dot(
         two_terms(jnp.broadcast_to(upright(skip[...]), (HEADS, 8))),
-        head_spread(HALF, half * HEADS // 2),
+        head_spread(INNER, 0),
     )
     state[...] = jnp.zeros_like(state)
     for r in range(ROWS):
@@ -483,9 +484,8 @@
     for r in range(ROWS):
         weights[r] = jnp.where(row >= lane, dot(c[r], b_t[r]), 0.0)
 
-    def line(r, placed):
-        rows = pl.ds(pl.multiple_of(r * LINE, LINE), LINE)
-        placed_rows = pl.ds(pl.multiple_of(placed * LINE, LINE), LINE)
+    def line(r):
+        rows, placed_rows = rows_of(r), rows_of(lax.rem(r + 1, ROWS))
         sums_here, steps_here, weights_here = sums[r], steps[r], weights[r]
         sums_t = cum[:, rows] * LOG2E
         steps_t = dt[:, rows]
@@ -495,15 +495,14 @@
             decay = jnp.exp2(jnp.minimum(along - sums_t[h : h + 1], 0.0))
             return along, (decay * (weights_here * steps_t[h : h + 1])).astype(BF16)
 
-        for q in range(HEADS // 8):
+        for q in range(HEADS // 4):
             quad = pl.ds(q * 256, 256)
             carried = dot(c[r], state[:, quad].astype(BF16))
             tails, decays = [], []
             for p in (2 * q, 2 * q + 1):
                 part = pl.ds(p * 128, 128)
-                whole_part = pl.ds(half * HALF + p * 128, 128)
-                h = half * HEADS // 2 + 2 * p
-                values = x[placed_rows, whole_part].astype(F32)
+                h = 2 * p
+                values = x[placed_rows, part].astype(F32)
                 (along_a, mixing_a), (along_b, mixing_b) = mixing(h), mixing(h + 1)
                 columns = jnp.concatenate(
                     [jnp.where(left, values, 0.0), jnp.where(left, 0.0, values)], axis=0
@@ -516,43 +515,41 @@
                 decays.append(carry[LINE - 1 :])
                 side = slice((p % 2) * 128, (p % 2) * 128 + 128)
                 y = inner + carry * carried[:, side] + direct[0:1, part] * values
-                out[rows, part] = (y * gate[rows, whole_part].astype(F32)).astype(BF16)
+                out[rows, part] = (y * gate[rows, part].astype(F32)).astype(BF16)
             state[:, quad] = jnp.concatenate(decays, axis=1) * state[:, quad] + dot(
                 b_t[r], jnp.concatenate(tails, axis=1)
             )
 
     @pl.loop(0, ROWS // 2)
     def _(pair):
-        line(2 * pair, 2 * pair + 1)
-        line(2 * pair + 1, lax.rem(2 * pair + 2, ROWS))
-
-    if half:
-        fetch.wait()
-
-
-def scan(half, x, bcs, cum, dt, gate, skip, *w):
-    weights = [pltpu.VMEM((INNER, D), BF16)] * half
+        line(2 * pair)
+        line(2 * pair + 1)
+
+    fetch.wait()
+
+
+def scan(x, bcs, cum, dt, gate, skip, w_out):
     return pl.pallas_call(
-        functools.partial(scan_kernel, half),
-        in_specs=[kept] * 6 + [far] * half,
-        out_specs=[kept] * (1 + half),
-        out_shape=[pltpu.VMEM((LENGTH, HALF), BF16)] + weights,
+        scan_kernel,
+        in_specs=[kept] * 6 + [far],
+        out_specs=[kept] * 2,
+        out_shape=[pltpu.VMEM((LENGTH, INNER), BF16), pltpu.VMEM((INNER, D), BF16)],
         scratch_shapes=[
-            pltpu.VMEM((8, HALF), F32),
-            pltpu.VMEM((STATE, HALF), F32),
+            pltpu.VMEM((8, INNER), F32),
+            pltpu.VMEM((STATE, INNER), F32),
             pltpu.VMEM((ROWS, LINE, HEADS), F32),
             pltpu.VMEM((ROWS, LINE, HEADS), F32),
             pltpu.VMEM((ROWS, LINE, LINE), F32),
             pltpu.VMEM((ROWS, STATE, LINE), BF16),
             pltpu.VMEM((ROWS, LINE, STATE), BF16),
-        ]
-        + [pltpu.SemaphoreType.DMA(())] * half,
+            pltpu.SemaphoreType.DMA(()),
+        ],
         compiler_params=params(),
         cost_estimate=pl.CostEstimate(
-            flops=2 << 30, bytes_accessed=5 << 20, transcendentals=LENGTH * LINE * HEADS // 2
+            flops=4 << 30, bytes_accessed=20 << 20, transcendentals=LENGTH * LINE * HEADS
         ),
         name="scan",
-    )(near(x), near(bcs), near(cum), near(dt), near(gate), near(skip), *map(hbm, w))
+    )(*map(near, (x, bcs, cum, dt, gate, skip)), hbm(w_out))
 
 
 def relay_kernel(arrived, out):
@@ -579,15 +576,15 @@
 def relay(arrived):
     return pl.pallas_call(
         relay_kernel,
-        out_shape=jax.ShapeDtypeStruct((BANDS, 16, GROUP), BF16),
+        out_specs=kept,
+        out_shape=pltpu.VMEM((BANDS, 16, GROUP), BF16),
         compiler_params=params(16),
         name="relay",
     )(arrived)
 
 
-def columns_out(values, tokens, turned, out, step):
+def columns_out(values, tokens, turned, out, rows=slice(None)):
     values = values + tokens.astype(F32)
-    rows = pl.ds(pl.multiple_of(step * 256, 256), 256)
     for k in range(values.shape[1] // 128):
         part = slice(k * 128, (k + 1) * 128)
         for r in range(ROWS):
@@ -596,7 +593,7 @@
 
 
 def finish_kernel(
-    local_a, local_b, gate, bcs, band_decay, entering, gain, tok, w, out, hidden, spread, state, decays, turned
+    local, gate, bcs, band_decay, entering, gain, tok, w, out, hidden, spread, state, decays, turned
 ):
     step = pl.program_id(0)
 
@@ -614,28 +611,29 @@
     cells = lambda ref: ref[:, here, :].reshape(256, ref.shape[2])
     both = jnp.concatenate([bcs[1:, here, :], bcs[:1, here, :]], axis=0).reshape(256, 128)
     decay = dot(cells(decays), spread[...])
-    local = jnp.concatenate([cells(local_a), cells(local_b)], axis=1)
-    gated = local.astype(F32) + dot(both, state[...]) * decay * cells(gate).astype(F32)
+    gated = cells(local).astype(F32) + dot(both, state[...]) * decay * cells(gate).astype(F32)
     normed = rms(gated, gain[...]).astype(BF16)
-    hidden[:, here, :] = normed.reshape(ROWS, 32, INNER)
+    hidden[...] = normed.reshape(ROWS, 32, INNER)
     columns_out(
         dot(normed, w[:, pl.ds(0, FIRST)]),
         tok[:, here, pl.ds(0, FIRST)].reshape(256, FIRST),
         turned,
         out,
-        step,
-    )
-
-
-def finish(local_a, local_b, gate, bcs, band_decay, entering, gain, tok, w_near):
+    )
+
+
+def finish(local, gate, bcs, band_decay, entering, gain, tok, w_out):
     return pl.pallas_call(
         finish_kernel,
         grid=(LINE // 32,),
-        in_specs=[kept] * 5 + [whole(BANDS, 16, GROUP), kept, kept, kept],
-        out_specs=[kept, kept],
+        in_specs=[kept] * 8,
+        out_specs=[
+            pl.BlockSpec((256, FIRST), lambda i: (i, 0)),
+            pl.BlockSpec((ROWS, 32, INNER), lambda i: (0, i, 0)),
+        ],
         out_shape=[
-            pltpu.VMEM((LENGTH, FIRST), BF16),
-            pltpu.VMEM((ROWS, LINE, INNER), BF16),
+            pltpu.HBM((LENGTH, FIRST), BF16),
+            pltpu.HBM((ROWS, LINE, INNER), BF16),
         ],
         scratch_shapes=[
             pltpu.VMEM((2 * HEADS, INNER), BF16),
@@ -648,46 +646,52 @@
             flops=2 * LENGTH * D * FIRST, bytes_accessed=16 << 20, transcendentals=LENGTH
         ),
         name="finish",
-    )(
-        near(local_a),
-        near(local_b),
-        near(gate),
-        near(bcs),
-        near(band_decay),
-        entering,
-        near(gain),
-        near(tok),
-        near(w_near),
-    )
-
-
-def rest_kernel(hidden, tok, w, out, turned):
+    )(*map(near, (local, gate, bcs, band_decay, entering, gain, tok, w_out)))
+
+
+def rest_kernel(hidden, w_far, tok_far, out, turned, w, tok_all, sem):
     step = pl.program_id(0)
+    part = pl.ds(FIRST, D - FIRST)
+    fetch = [
+        pltpu.make_async_copy(w_far.at[:, part], w, sem.at[0]),
+        pltpu.make_async_copy(tok_far.at[:, :, part], tok_all, sem.at[1]),
+    ]
+
+    @pl.when(step == 0)
+    def _():
+        for copy in fetch:
+            copy.start()
+        for copy in fetch:
+            copy.wait()
+
     here = pl.ds(pl.multiple_of(step * 32, 32), 32)
-    part = pl.ds(FIRST, D - FIRST)
     columns_out(
-        dot(hidden[:, here, :].reshape(256, INNER), w[:, part]),
-        tok[:, here, part].reshape(256, D - FIRST),
+        dot(hidden[...].reshape(256, INNER), w[...]),
+        tok_all[:, here, :].reshape(256, D - FIRST),
         turned,
         out,
-        step,
-    )
-
-
-def rest(hidden, tok, w_near):
+    )
+
+
+def rest(hidden, tok, w_out):
     return pl.pallas_call(
         rest_kernel,
         grid=(LINE // 32,),
-        in_specs=[kept] * 3,
-        out_specs=kept,
-        out_shape=pltpu.VMEM((LENGTH, D - FIRST), BF16),
-        scratch_shapes=[pltpu.VMEM(((D - FIRST) // 128, 256, 128), F32)],
-        compiler_params=params(),
+        in_specs=[pl.BlockSpec((ROWS, 32, INNER), lambda i: (0, i, 0)), far, far],
+        out_specs=pl.BlockSpec((256, D - FIRST), lambda i: (i, 0)),
+        out_shape=pltpu.HBM((LENGTH, D - FIRST), BF16),
+        scratch_shapes=[
+            pltpu.VMEM(((D - FIRST) // 128, 256, 128), F32),
+            pltpu.VMEM((INNER, D - FIRST), BF16),
+            pltpu.VMEM((ROWS, LINE, D - FIRST), BF16),
+            pltpu.SemaphoreType.DMA((2,)),
+        ],
+        compiler_params=params(60),
         cost_estimate=pl.CostEstimate(
             flops=2 * LENGTH * D * (D - FIRST), bytes_accessed=8 << 20, transcendentals=0
         ),
         name="rest",
-    )(near(hidden), near(tok), near(w_near))
+    )(hidden, hbm(w_out), hbm(tok))
 
 
 def shards(
@@ -764,19 +768,15 @@
     onward = functools.partial(
         lax.ppermute, axis_name="segment", perm=[(i, (i + 1) % segments) for i in range(segments)]
     )
+    local, w_out_near = scan(x, bcs, cum, dt, gate, skip_near, w_out[0])
+    pieces, local = lax.optimization_barrier((pieces, local))
     arrived = swap(pieces.reshape(BANDS, 16, GROUP + 128))
-    (local_a,) = scan(0, x, bcs, cum, dt, gate, skip_near)
-    arrived, local_a = lax.optimization_barrier((arrived, local_a))
-    states = relay(arrived)
-    states, skip_b = lax.optimization_barrier((states, skip_near))
-    entering = swap(states)
-    local_b, w_out_near = scan(1, x, bcs, cum, dt, gate, skip_b, w_out[0])
+    entering = swap(relay(arrived))
 
     grid = lambda a: a.reshape(ROWS, LINE, a.shape[-1])
     parted = lambda a: a.reshape(BANDS, LENGTH // BANDS, a.shape[-1])
     first, hidden = finish(
-        grid(local_a),
-        grid(local_b),
+        grid(local),
         grid(gate),
         grid(bcs),
         band_decay,
@@ -786,7 +786,7 @@
         w_out_near,
     )
     first = swap(parted(first))
-    second = onward(parted(rest(hidden, grid(tok_near), w_out_near)))
+    second = onward(parted(rest(hidden, cells, w_out[0])))
     second = swap(second)
     first = onward(first)
     both = jnp.concatenate([first, second], axis=-1)

time: 163 us -> 142 us (0.87)
  blocking collectives: 25 us -> 54.9 us
  local copies, waits for them, and re-layouts: 30.9 us -> 1.17 us
  starting transfers between devices: 30.7 us -> 9.6 us
    all_to_all x0 -> x2, blocking collectives: none -> 29.9 us  [the longest x1 18.4 us: shards(): arrived = swap(pieces.reshape(BANDS, 16, GROUP + 128))]
    unnamed x46 -> x0, local copies, waits for them, and re-layouts: 29.8 us -> none
    all_to_all x2 -> x0, starting transfers between devices: 17.4 us -> none  [the longest x1 10.1 us: shards(): arrived = swap(pieces.reshape(BANDS, 16, GROUP + 128))]
    all_to_all x1, starting transfers between devices: 7.47 us -> 3.71 us  [shards(): first = swap(parted(first))]
    pallas_call x5 -> x4, Pallas kernels: 27.7 us -> 28.7 us  [the longest x1 11.6 us: scan(): pl.pallas_call(scan_kernel, in_specs=[kept] * 6 + [far], out_specs=[kept]...]
  transfers between devices with their start and end apart: 7 -> 5, of which waited for: 2 -> 2; matrix products, arithmetic and copies ran while one was open for 0% -> 0% of each run, Pallas kernels for 25% -> 22%
where the time goes in v7:
time: 142 us
  Pallas kernels  55.7 us (39%)
  blocking collectives  54.9 us (39%)
  waiting for transfers between devices  18.4 us (13%)
  starting transfers between devices  9.6 us (7%)
  other arithmetic  1.96 us (1%)
    all_to_all x1, blocking collectives, shards(): second = swap(second)  25 us
    pallas_call x1, Pallas kernels, project(): pl.pallas_call(project_kernel, in_specs=[far, small(1, D), far, far, smal...  22.6 us
    all_to_all x1, blocking collectives, shards(): arrived = swap(pieces.reshape(BANDS, 16, GROUP + 128))  18.4 us
    all_to_all x1, waiting for transfers between devices, shards(): first = swap(parted(first))  15.3 us
    pallas_call x1, Pallas kernels, scan(): pl.pallas_call(scan_kernel, in_specs=[kept] * 6 + [far], out_specs=[kept]...  11.6 us
    all_to_all x1, blocking collectives, shards(): entering = swap(relay(arrived))  11.5 us
    pallas_call x1, Pallas kernels, finish(): pl.pallas_call(finish_kernel, grid=(LINE // 32,), in_specs=[kept] * 8, ou...  9 us
    pallas_call x1, Pallas kernels, rest(): pl.pallas_call(rest_kernel, grid=(LINE // 32,), in_specs=[pl.BlockSpec((R...  7.9 us
  transfers between devices with their start and end apart: 5, of which 2 were waited for; matrix products, arithmetic and copies ran while one was open for 0% of the time, Pallas kernels for 22%

profile of v7, /device:TPU:0, one launch (start us, length us, event | category | flops | bytes accessed | tf_op | source)
XLA Modules:
  0.0 141.9 jit_solution(11030443738898948076)
XLA Ops:
  0.0 1.2 slice_bitcast_fusion
  1.2 1.3 collective-permute-start.1
  2.5 4.6 %collective-permute-start = (bf16[128,1536]{1,0:T(8,128)(2,1)S(1)}, bf16[128,1536]{1,0:T(8,128)(2,1)S(1)}, u32[]{:S(2)}, u32[]{:S(2)}) collective-permute-start(bf16[128,1536]{1,0:T(8,128)(2,1)S(1)} %get-tuple-element.60), channel_id=1, source_target_pairs={{0,1},{1,2},{2,3},{3,4},{4,5},{5,6},{6,7},{7,8},{8,9},{9,10},{10,1... | collective-permute-start | bytes 1179656 | tf_op jit(solution)/shard_map/ppermute | solution.py:715
  7.0 22.6 %project.1 = (bf16[1024,1536]{1,0:T(8,128)(2,1)S(1)}, bf16[1024,1536]{1,0:T(8,128)(2,1)S(1)}, bf16[512,1536]{1,0:T(8,128)(2,1)S(1)}, bf16[1024,128]{1,0:T(8,128)...) custom-call(bf16[1024,1536]{1,0:T(8,128)(2,1)} %bitcast.32, ...), custom_call_target="tpu_custom_call" | custom-call | flops 10141827072 | bytes 20971520 | tf_op jit(solution)/shard_map/project/pallas_call | solution.py:284
  29.7 0.0 collective-permute-done.1.bottom
  29.7 0.0 collective-permute-done.top
  29.7 4.5 %edges.1 = (bf16[1024,1536]{1,0:T(8,128)(2,1)S(1)}, bf16[1024,128]{1,0:T(8,128)(2,1)S(1)}, bf16[4,4,16,512]{3,2,1,0:T(8,128)(2,1)S(1)}) custom-call(bf16[128,1536]{1,0:T(8,128)(2,1)S(1)} %collective-permute-done.top, bf16[128,1536]{1,0:T(8,128)(2,1)S(1)} %collective-permute-done.1.bottom, ...), custom_call_target="tpu_custom_call", output_to_operand_aliasing={{0}: (11, {}), {1}: (12, {})} | custom-call | flops 1325662208 | bytes 10485760 | tf_op jit(solution)/shard_map/edges/pallas_call | solution.py:421
  34.1 11.6 %scan.1 = (bf16[1024,1536]{1,0:T(8,128)(2,1)S(1)}, bf16[1536,1536]{1,0:T(8,128)(2,1)S(1)}) custom-call(bf16[1024,1536]{1,0:T(8,128)(2,1)S(1)} %get-tuple-element.44.x, bf16[1024,128]{1,0:T(8,128)(2,1)S(1)} %get-tuple-element.45.bcs, f32[24,1024]{1,0:T(8,128)S(1)} %get-tuple-element.46.cum, f32[24,1024]{1,0:T(8,128)S(1)} %get-tuple-element.47.dt, ...), custom_call_target="tpu_custom_call" | custom-call | flops 4294967296 | bytes 20971520 | tf_op jit(solution)/shard_map/scan/pallas_call | solution.py:532
  45.7 18.4 %all_to_all.20.arrived = bf16[16,16,512]{2,1,0:T(8,128)(2,1)S(1)} all-to-all(bf16[16,16,512]{2,1,0:T(8,128)(2,1)S(1)} %bitcast.31), channel_id=1, replica_groups=mesh['segment'=8,'band'=16] {'band'}, dimensions={0} | all-to-all | bytes 524288 | tf_op jit(solution)/shard_map/all_to_all | solution.py:773
  64.1 0.2 relay.1
  64.3 11.5 %all_to_all.21.entering = bf16[16,16,384]{2,1,0:T(8,128)(2,1)S(1)} all-to-all(bf16[16,16,384]{2,1,0:T(8,128)(2,1)S(1)} %relay.1), channel_id=1, replica_groups=mesh['segment'=8,'band'=16] {'band'}, dimensions={0} | all-to-all | bytes 393216 | tf_op jit(solution)/shard_map/all_to_all | solution.py:774
  75.8 9.0 %finish.1 = (bf16[1024,896]{1,0:T(8,128)(2,1)}, bf16[8,128,1536]{2,1,0:T(8,128)(2,1)}) custom-call(bf16[8,128,1536]{2,1,0:T(8,128)(2,1)S(1)} %bitcast.29, bf16[8,128,1536]{2,1,0:T(8,128)(2,1)S(1)} %bitcast.27, bf16[8,128,128]{2,1,0:T(8,128)(2,1)S(1)} %bitcast.30, f32[24,1024]{1,0:T(8,128)S(1)} %get-tuple-element.52.band_decay, ...), custom_call_target="tpu_custom_call" | custom-call | flops 2818572288 | bytes 16777216 | tf_op jit(solution)/shard_map/finish/pallas_call | solution.py:626
  84.8 3.7 %all-to-all-start.2 = ((bf16[16,64,896]{2,1,0:T(8,128)(2,1)}), bf16[16,64,896]{2,1,0:T(8,128)(2,1)S(1)}, u32[]{:S(2)}, u32[]{:S(2)}) async-start(bf16[16,64,896]{2,1,0:T(8,128)(2,1)} %bitcast.36), calls=%async_computation.2 | async-start | bytes 3670016 | tf_op jit(solution)/shard_map/all_to_all | solution.py:788
  88.5 7.9 %rest.1 = bf16[1024,640]{1,0:T(8,128)(2,1)} custom-call(bf16[8,128,1536]{2,1,0:T(8,128)(2,1)} %get-tuple-element.58.hidden, bf16[1536,1536]{1,0:T(8,128)(2,1)} %bitcast.35, bf16[8,128,1536]{2,1,0:T(8,128)(2,1)} %bitcast.33), custom_call_target="tpu_custom_call" | custom-call | flops 2013265920 | bytes 8388608 | tf_op jit(solution)/shard_map/rest/pallas_call | solution.py:677
  96.4 0.0 collective-permute-start.3
  96.5 15.3 %all-to-all-done.2 = bf16[16,64,896]{2,1,0:T(8,128)(2,1)S(1)} async-done(((bf16[16,64,896]{2,1,0:T(8,128)(2,1)}), bf16[16,64,896]{2,1,0:T(8,128)(2,1)S(1)}, u32[]{:S(2)}, u32[]{:S(2)}) %all-to-all-start.2) | async-done | bytes 1835040 | tf_op jit(solution)/shard_map/all_to_all | solution.py:788
  111.8 0.0 collective-permute-start.2
  111.8 3.1 %collective-permute-done.3 = bf16[16,64,640]{2,1,0:T(8,128)(2,1)S(1)} collective-permute-done((bf16[16,64,640]{2,1,0:T(8,128)(2,1)}, bf16[16,64,640]{2,1,0:T(8,128)(2,1)S(1)}, u32[]{:S(2)}, u32[]{:S(2)}) %collective-permute-start.3) | collective-permute-done | bytes 1310752 | tf_op jit(solution)/shard_map/ppermute | solution.py:789
  114.9 25.0 %all_to_all.22 = bf16[16,64,640]{2,1,0:T(8,128)(2,1)S(1)} all-to-all(bf16[16,64,640]{2,1,0:T(8,128)(2,1)S(1)} %collective-permute-done.3), channel_id=1, replica_groups=mesh['segment'=8,'band'=16] {'band'}, dimensions={0} | all-to-all | bytes 2621440 | tf_op jit(solution)/shard_map/all_to_all | solution.py:790
  139.9 0.0 collective-permute-done.2
  139.9 2.0 %copy_bitcast_fusion = bf16[1,8,128,1536]{3,2,1,0:T(8,128)(2,1)} fusion(bf16[16,64,640]{2,1,0:T(8,128)(2,1)S(1)} %all_to_all.22, bf16[16,64,896]{2,1,0:T(8,128)(2,1)S(1)} %collective-permute-done.2), kind=kLoop, calls=%fused_computation.1 | loop fusion | flops 6291456 | bytes 6291456 | tf_op jit(solution)/shard_map/reshape | solution.py:794
Async XLA Ops:
  1.2 28.5 %collective-permute-start.1 = (bf16[128,1536]{1,0:T(8,128)(2,1)S(1)}, bf16[128,1536]{1,0:T(8,128)(2,1)S(1)}, u32[]{:S(2)}, u32[]{:S(2)}) collective-permute-start(bf16[128,1536]{1,0:T(8,128)(2,1)S(1)} %get-tuple-element.59), channel_id=1, source_target_pairs={{1,0},{2,1},{3,2},{4,3},{5,4},{6,5},{7,6},{8,7},{9,8},{10,9},{11,1... | collective-permute-start | bytes 1179656 | tf_op jit(solution)/shard_map/ppermute | solution.py:716
  2.5 27.2 %collective-permute-start = (bf16[128,1536]{1,0:T(8,128)(2,1)S(1)}, bf16[128,1536]{1,0:T(8,128)(2,1)S(1)}, u32[]{:S(2)}, u32[]{:S(2)}) collective-permute-start(bf16[128,1536]{1,0:T(8,128)(2,1)S(1)} %get-tuple-element.60), channel_id=1, source_target_pairs={{0,1},{1,2},{2,3},{3,4},{4,5},{5,6},{6,7},{7,8},{8,9},{9,10},{10,1... | collective-permute-start | bytes 1179656 | tf_op jit(solution)/shard_map/ppermute | solution.py:715
  84.8 27.0 %all-to-all-start.2 = ((bf16[16,64,896]{2,1,0:T(8,128)(2,1)}), bf16[16,64,896]{2,1,0:T(8,128)(2,1)S(1)}, u32[]{:S(2)}, u32[]{:S(2)}) async-start(bf16[16,64,896]{2,1,0:T(8,128)(2,1)} %bitcast.36), calls=%async_computation.2 | async-start | bytes 3670016 | tf_op jit(solution)/shard_map/all_to_all | solution.py:788
  96.4 18.5 %collective-permute-start.3 = (bf16[16,64,640]{2,1,0:T(8,128)(2,1)}, bf16[16,64,640]{2,1,0:T(8,128)(2,1)S(1)}, u32[]{:S(2)}, u32[]{:S(2)}) collective-permute-start(bf16[16,64,640]{2,1,0:T(8,128)(2,1)} %bitcast.37), channel_id=1, source_target_pairs={{0,16},{16,32},{32,48},{48,64},{64,80},{80,96},{96,112},{112,0},{1... | collective-permute-start | bytes 3932168 | tf_op jit(solution)/shard_map/ppermute | solution.py:789
  111.8 28.1 %collective-permute-start.2 = (bf16[16,64,896]{2,1,0:T(8,128)(2,1)S(1)}, bf16[16,64,896]{2,1,0:T(8,128)(2,1)S(1)}, u32[]{:S(2)}, u32[]{:S(2)}) collective-permute-start(bf16[16,64,896]{2,1,0:T(8,128)(2,1)S(1)} %all-to-all-done.2), channel_id=1, source_target_pairs={{0,16},{16,32},{32,48},{48,64},{64,80},{80,96},{96,112},{112,0},{1... | collective-permute-start | bytes 5505032 | tf_op jit(solution)/shard_map/ppermute | solution.py:791

commit v8 on v7

--- a/solution.py
+++ b/solution.py
@@ -17,7 +17,7 @@
 INNER = HEADS * WIDTH
 D = 1536
 HALF = INNER // 2
-FIRST = 896
+FIRST = 1024
 GROUP = 384
 GROUP_HEADS = GROUP // WIDTH
 BANDS = 16
@@ -520,10 +520,9 @@
                 b_t[r], jnp.concatenate(tails, axis=1)
             )
 
-    @pl.loop(0, ROWS // 2)
-    def _(pair):
-        line(2 * pair)
-        line(2 * pair + 1)
+    @pl.loop(0, ROWS)
+    def _(r):
+        line(r)
 
     fetch.wait()
 

time: 142 us -> 174 us (1.23)
  blocking collectives: 54.9 us -> 78.5 us
  waiting for transfers between devices: 18.4 us -> 29.4 us
  starting transfers between devices: 9.6 us -> 7.56 us
    all_to_all x0 -> x1, blocking collectives: none -> 29.8 us  [shards(): first = swap(parted(first))]
    ppermute x1, waiting for transfers between devices: 3.11 us -> 29.4 us  [shards(): second = onward(parted(rest(hidden, cells, w_out[0])))]
    all_to_all x1 -> x0, waiting for transfers between devices: 15.3 us -> none  [shards(): first = swap(parted(first))]
    all_to_all x1, blocking collectives: 25 us -> 18.8 us  [shards(): second = swap(second)]
    all_to_all x1 -> x0, starting transfers between devices: 3.71 us -> none  [shards(): first = swap(parted(first))]
  transfers between devices with their start and end apart: 5 -> 4, of which waited for: 2 -> 1; matrix products, arithmetic and copies ran while one was open for 0% -> 0% of each run, Pallas kernels for 22% -> 17%
where the time goes in v8:
time: 174 us; the launch traced here: 173 us
  blocking collectives  78.5 us (45%)
  Pallas kernels  54.5 us (31%)
  waiting for transfers between devices  29.4 us (17%)
  starting transfers between devices  7.56 us (4%)
  other arithmetic  1.91 us (1%)
    all_to_all x1, blocking collectives, shards(): first = swap(parted(first))  29.8 us
    ppermute x1, waiting for transfers between devices, shards(): second = onward(parted(rest(hidden, cells, w_out[0])))  29.4 us
    pallas_call x1, Pallas kernels, project(): pl.pallas_call(project_kernel, in_specs=[far, small(1, D), far, far, smal...  22.6 us
    all_to_all x1, blocking collectives, shards(): second = swap(second)  18.8 us
    all_to_all x1, blocking collectives, shards(): arrived = swap(pieces.reshape(BANDS, 16, GROUP + 128))  18.4 us
    all_to_all x1, blocking collectives, shards(): entering = swap(relay(arrived))  11.5 us
    pallas_call x1, Pallas kernels, scan(): pl.pallas_call(scan_kernel, in_specs=[kept] * 6 + [far], out_specs=[kept]...  11.1 us
    pallas_call x1, Pallas kernels, finish(): pl.pallas_call(finish_kernel, grid=(LINE // 32,), in_specs=[kept] * 8, ou...  9.15 us
  transfers between devices with their start and end apart: 4, of which 1 were waited for; matrix products, arithmetic and copies ran while one was open for 0% of the time, Pallas kernels for 17%

profile of v8, /device:TPU:0, one launch (start us, length us, event | category | flops | bytes accessed | tf_op | source)
XLA Modules:
  0.0 173.2 jit_solution(136954775518911981)
XLA Ops:
  0.0 1.2 slice_bitcast_fusion
  1.2 1.3 collective-permute-start.1
  2.5 4.6 %collective-permute-start = (bf16[128,1536]{1,0:T(8,128)(2,1)S(1)}, bf16[128,1536]{1,0:T(8,128)(2,1)S(1)}, u32[]{:S(2)}, u32[]{:S(2)}) collective-permute-start(bf16[128,1536]{1,0:T(8,128)(2,1)S(1)} %get-tuple-element.60), channel_id=1, source_target_pairs={{0,1},{1,2},{2,3},{3,4},{4,5},{5,6},{6,7},{7,8},{8,9},{9,10},{10,1... | collective-permute-start | bytes 1179656 | tf_op jit(solution)/shard_map/ppermute | solution.py:714
  7.0 22.6 %project.1 = (bf16[1024,1536]{1,0:T(8,128)(2,1)S(1)}, bf16[1024,1536]{1,0:T(8,128)(2,1)S(1)}, bf16[512,1536]{1,0:T(8,128)(2,1)S(1)}, bf16[1024,128]{1,0:T(8,128)...) custom-call(bf16[1024,1536]{1,0:T(8,128)(2,1)} %bitcast.32, ...), custom_call_target="tpu_custom_call" | custom-call | flops 10141827072 | bytes 20971520 | tf_op jit(solution)/shard_map/project/pallas_call | solution.py:284
  29.7 0.0 collective-permute-done.1.bottom
  29.7 0.0 collective-permute-done.top
  29.7 4.5 %edges.1 = (bf16[1024,1536]{1,0:T(8,128)(2,1)S(1)}, bf16[1024,128]{1,0:T(8,128)(2,1)S(1)}, bf16[4,4,16,512]{3,2,1,0:T(8,128)(2,1)S(1)}) custom-call(bf16[128,1536]{1,0:T(8,128)(2,1)S(1)} %collective-permute-done.top, bf16[128,1536]{1,0:T(8,128)(2,1)S(1)} %collective-permute-done.1.bottom, ...), custom_call_target="tpu_custom_call", output_to_operand_aliasing={{0}: (11, {}), {1}: (12, {})} | custom-call | flops 1325662208 | bytes 10485760 | tf_op jit(solution)/shard_map/edges/pallas_call | solution.py:421
  34.1 11.1 %scan.1 = (bf16[1024,1536]{1,0:T(8,128)(2,1)S(1)}, bf16[1536,1536]{1,0:T(8,128)(2,1)S(1)}) custom-call(bf16[1024,1536]{1,0:T(8,128)(2,1)S(1)} %get-tuple-element.44.x, bf16[1024,128]{1,0:T(8,128)(2,1)S(1)} %get-tuple-element.45.bcs, f32[24,1024]{1,0:T(8,128)S(1)} %get-tuple-element.46.cum, f32[24,1024]{1,0:T(8,128)S(1)} %get-tuple-element.47.dt, ...), custom_call_target="tpu_custom_call" | custom-call | flops 4294967296 | bytes 20971520 | tf_op jit(solution)/shard_map/scan/pallas_call | solution.py:531
  45.2 18.4 %all_to_all.20.arrived = bf16[16,16,512]{2,1,0:T(8,128)(2,1)S(1)} all-to-all(bf16[16,16,512]{2,1,0:T(8,128)(2,1)S(1)} %bitcast.31), channel_id=1, replica_groups=mesh['segment'=8,'band'=16] {'band'}, dimensions={0} | all-to-all | bytes 524288 | tf_op jit(solution)/shard_map/all_to_all | solution.py:772
  63.6 0.2 relay.1
  63.8 11.5 %all_to_all.21.entering = bf16[16,16,384]{2,1,0:T(8,128)(2,1)S(1)} all-to-all(bf16[16,16,384]{2,1,0:T(8,128)(2,1)S(1)} %relay.1), channel_id=1, replica_groups=mesh['segment'=8,'band'=16] {'band'}, dimensions={0} | all-to-all | bytes 393216 | tf_op jit(solution)/shard_map/all_to_all | solution.py:773
  75.3 9.1 %finish.1 = (bf16[1024,1024]{1,0:T(8,128)(2,1)}, bf16[8,128,1536]{2,1,0:T(8,128)(2,1)}) custom-call(bf16[8,128,1536]{2,1,0:T(8,128)(2,1)S(1)} %bitcast.29, bf16[8,128,1536]{2,1,0:T(8,128)(2,1)S(1)} %bitcast.27, bf16[8,128,128]{2,1,0:T(8,128)(2,1)S(1)} %bitcast.30, f32[24,1024]{1,0:T(8,128)S(1)} %get-tuple-element.52.band_decay, ...), custom_call_target="tpu_custom_call" | custom-call | flops 3221225472 | bytes 16777216 | tf_op jit(solution)/shard_map/finish/pallas_call | solution.py:625
  84.5 29.8 %all_to_all.22 = bf16[16,64,1024]{2,1,0:T(8,128)(2,1)} all-to-all(bf16[16,64,1024]{2,1,0:T(8,128)(2,1)} %bitcast.36), channel_id=1, replica_groups=mesh['segment'=8,'band'=16] {'band'}, dimensions={0} | all-to-all | bytes 4194304 | tf_op jit(solution)/shard_map/all_to_all | solution.py:787
  114.3 0.0 collective-permute-start.2
  114.3 7.0 %rest.1 = bf16[1024,512]{1,0:T(8,128)(2,1)} custom-call(bf16[8,128,1536]{2,1,0:T(8,128)(2,1)} %get-tuple-element.58.hidden, bf16[1536,1536]{1,0:T(8,128)(2,1)} %bitcast.35, bf16[8,128,1536]{2,1,0:T(8,128)(2,1)} %bitcast.33), custom_call_target="tpu_custom_call" | custom-call | flops 1610612736 | bytes 8388608 | tf_op jit(solution)/shard_map/rest/pallas_call | solution.py:676
  121.3 1.7 collective-permute-start.3
  123.0 29.4 %collective-permute-done.3 = bf16[16,64,512]{2,1,0:T(8,128)(2,1)S(1)} collective-permute-done((bf16[16,64,512]{2,1,0:T(8,128)(2,1)}, bf16[16,64,512]{2,1,0:T(8,128)(2,1)S(1)}, u32[]{:S(2)}, u32[]{:S(2)}) %collective-permute-start.3) | collective-permute-done | bytes 1048608 | tf_op jit(solution)/shard_map/ppermute | solution.py:788
  152.4 18.8 %all_to_all.23 = bf16[16,64,512]{2,1,0:T(8,128)(2,1)S(1)} all-to-all(bf16[16,64,512]{2,1,0:T(8,128)(2,1)S(1)} %collective-permute-done.3), channel_id=1, replica_groups=mesh['segment'=8,'band'=16] {'band'}, dimensions={0} | all-to-all | bytes 2097152 | tf_op jit(solution)/shard_map/all_to_all | solution.py:789
  171.3 0.0 collective-permute-done.2
  171.3 1.9 %copy_bitcast_fusion = bf16[1,8,128,1536]{3,2,1,0:T(8,128)(2,1)} fusion(bf16[16,64,512]{2,1,0:T(8,128)(2,1)S(1)} %all_to_all.23, bf16[16,64,1024]{2,1,0:T(8,128)(2,1)S(1)} %collective-permute-done.2), kind=kLoop, calls=%fused_computation.1 | loop fusion | flops 6291456 | bytes 6291456 | tf_op jit(solution)/shard_map/reshape | solution.py:793
Async XLA Ops:
  1.2 28.5 %collective-permute-start.1 = (bf16[128,1536]{1,0:T(8,128)(2,1)S(1)}, bf16[128,1536]{1,0:T(8,128)(2,1)S(1)}, u32[]{:S(2)}, u32[]{:S(2)}) collective-permute-start(bf16[128,1536]{1,0:T(8,128)(2,1)S(1)} %get-tuple-element.59), channel_id=1, source_target_pairs={{1,0},{2,1},{3,2},{4,3},{5,4},{6,5},{7,6},{8,7},{9,8},{10,9},{11,1... | collective-permute-start | bytes 1179656 | tf_op jit(solution)/shard_map/ppermute | solution.py:715
  2.5 27.2 %collective-permute-start = (bf16[128,1536]{1,0:T(8,128)(2,1)S(1)}, bf16[128,1536]{1,0:T(8,128)(2,1)S(1)}, u32[]{:S(2)}, u32[]{:S(2)}) collective-permute-start(bf16[128,1536]{1,0:T(8,128)(2,1)S(1)} %get-tuple-element.60), channel_id=1, source_target_pairs={{0,1},{1,2},{2,3},{3,4},{4,5},{5,6},{6,7},{7,8},{8,9},{9,10},{10,1... | collective-permute-start | bytes 1179656 | tf_op jit(solution)/shard_map/ppermute | solution.py:714
  114.3 57.0 %collective-permute-start.2 = (bf16[16,64,1024]{2,1,0:T(8,128)(2,1)}, bf16[16,64,1024]{2,1,0:T(8,128)(2,1)S(1)}, u32[]{:S(2)}, u32[]{:S(2)}) collective-permute-start(bf16[16,64,1024]{2,1,0:T(8,128)(2,1)} %all_to_all.22), channel_id=1, source_target_pairs={{0,16},{16,32},{32,48},{48,64},{64,80},{80,96},{96,112},{112,0},{1... | collective-permute-start | bytes 6291464 | tf_op jit(solution)/shard_map/ppermute | solution.py:790
  121.3 31.1 %collective-permute-start.3 = (bf16[16,64,512]{2,1,0:T(8,128)(2,1)}, bf16[16,64,512]{2,1,0:T(8,128)(2,1)S(1)}, u32[]{:S(2)}, u32[]{:S(2)}) collective-permute-start(bf16[16,64,512]{2,1,0:T(8,128)(2,1)} %bitcast.37), channel_id=1, source_target_pairs={{0,16},{16,32},{32,48},{48,64},{64,80},{80,96},{96,112},{112,0},{1... | collective-permute-start | bytes 3145736 | tf_op jit(solution)/shard_map/ppermute | solution.py:788
